TPU v7x, 128 devices: a whole 4x4x4 slice. The times are simulated.
128 devices in a mesh: lat: 8 (over z, y_hi), lon: 16 (over x, y_lo, core).
Axes of the slice: x: 4, y: 4 (y_hi: 2, y_lo: 2; y = y_hi * 2 + y_lo), z: 4, core: 2. Of those that a mesh axis runs over, the one named last changes fastest.
Arguments:
- obs_values: bfloat16 [1048576, 24], P(('lat', 'lon')), may hold values from -6 to 6
- tile_ids: int32 [1048576, 1], P(('lat', 'lon')), may hold values from 0 to 127; in each aligned block of 8192 rows (0 to 8191, 8192 to 16383, ...) at most 128 rows name the same one
- obs_rows: float32 [1048576], P(('lat', 'lon')), may hold values from 0 to 16
- obs_cols: float32 [1048576], P(('lat', 'lon')), may hold values from 0 to 128
- w_embed: bfloat16 [24, 128], replicated, may hold values from -0.25 to 0.25
- w_first: bfloat16 [3, 3, 128, 128], replicated, may hold values from -0.1875 to 0.1875
- w_second: bfloat16 [3, 3, 128, 128], replicated, may hold values from -0.1875 to 0.1875
- cotangent: bfloat16 [128, 2048, 128], P('lat', 'lon'), may hold values from -0.01171875 to 0.01171875
Outputs:
- field: bfloat16 [128, 2048, 128], P('lat', 'lon')
- grad_embed: float32 [24, 128], replicated
- grad_first: float32 [3, 3, 128, 128], replicated
- grad_second: float32 [3, 3, 128, 128], replicated
Inputs may be any that keep to these rules, and one draw needn't show every extreme that they name: `tile_ids`: within the rows of one device no tile is named by more than 128 rows, and in every draw some device names some tile exactly 128 times.
All inputs are finite; a program needn't handle non-finite values.
Results may differ from a plain program's by a relative error of at most 0.0083.
Values may be sent and summed in bfloat16 or wider, within the bound.
No kernel may reach another device: no remote copies, remote signals or barrier semaphores. Data moves between devices by JAX's collectives and lax.ppermute only.
A program may use at most 64 MiB of HBM per device.

v0:
```python
import jax
import jax.numpy as jnp
from jax import lax
from jax.sharding import PartitionSpec as P

spread_cells = 1.0


def with_halo(cells, sides, width, closed):
    for axis, dim in sides:
        count = lax.axis_size(axis)
        ends = count if closed else count - 1
        head = lax.slice_in_dim(cells, 0, width, axis=dim)
        tail = lax.slice_in_dim(cells, cells.shape[dim] - width, cells.shape[dim], axis=dim)
        cells = jnp.concatenate(
            [
                lax.ppermute(tail, axis, [(i, (i + 1) % count) for i in range(ends)]),
                cells,
                lax.ppermute(head, axis, [((i + 1) % count, i) for i in range(ends)]),
            ],
            axis=dim,
        )
    return cells


def from_partner(array, axis, stride):
    return lax.ppermute(array, axis, [(i, i ^ 1 << stride) for i in range(lax.axis_size(axis))])


def assign_slots(target, owners):
    owner_ids = jnp.arange(owners, dtype=jnp.int32)
    onehot = (target[:, None] == owner_ids[None, :]).astype(jnp.int32)
    running = jnp.cumsum(onehot, axis=0) - 1
    return jnp.sum(running * onehot, axis=1)


def gaussian_grid(got_values, got_where, tile_rows, tile_cols):
    value_count, slot_total = got_values.shape
    slab_size = min(slot_total, 4096)
    slab_count = slot_total // slab_size
    value_slabs = got_values.reshape(value_count, slab_count, slab_size).transpose(1, 0, 2)
    where_slabs = got_where.reshape(2, slab_count, slab_size).transpose(1, 0, 2)
    centre_row = jnp.arange(tile_rows, dtype=jnp.float32) + 0.5
    centre_col = jnp.arange(tile_cols, dtype=jnp.float32) + 0.5
    scale_two = 2.0 * spread_cells * spread_cells

    def accumulate(summed, packed):
        slab_values, slab_where = packed
        row_weight = jnp.exp(-jnp.square(slab_where[0][None, :] - centre_row[:, None]) / scale_two)
        col_weight = jnp.exp(
            -jnp.square(slab_where[1][None, :] - centre_col[:, None]) / scale_two
        ).astype(jnp.bfloat16)
        weighted = (row_weight[:, None, :] * slab_values[None, :, :]).astype(jnp.bfloat16)
        slab_sum = lax.dot_general(
            weighted.reshape(tile_rows * value_count, slab_size),
            col_weight,
            (((1,), (1,)), ((), ())),
            preferred_element_type=jnp.float32,
        )
        return (summed + slab_sum, None)

    start_sum = jnp.zeros((tile_rows * value_count, tile_cols), jnp.float32)
    summed, _ = lax.scan(accumulate, start_sum, (value_slabs, where_slabs))
    return summed.astype(jnp.bfloat16).reshape(tile_rows, value_count, tile_cols)


def extend(tile_field):
    lon_ext = with_halo(tile_field, (("lon", 1),), 1, True)
    lat_ext = with_halo(lon_ext, (("lat", 0),), 1, False)
    edge_rows = jnp.stack([lon_ext[0], lon_ext[-1]])
    partner = from_partner(edge_rows, "lon", lax.axis_size("lon").bit_length() - 2)
    band = lax.axis_index("lat")
    upper_row = jnp.where(band == 0, partner[0], lat_ext[0])
    lower_row = jnp.where(band == lax.axis_size("lat") - 1, partner[1], lat_ext[-1])
    return jnp.concatenate([upper_row[None], lat_ext[1:-1], lower_row[None]], axis=0)


def convolve(block_ext, weight):
    tile_rows = block_ext.shape[0] - 2
    tile_cols = block_ext.shape[1] - 2
    summed = jnp.zeros((tile_rows * tile_cols, weight.shape[3]), jnp.float32)
    for row_off in range(3):
        for col_off in range(3):
            window = block_ext[
                row_off : row_off + tile_rows, col_off : col_off + tile_cols
            ].reshape(tile_rows * tile_cols, -1)
            summed = summed + jnp.dot(
                window, weight[row_off, col_off], preferred_element_type=jnp.float32
            )
    return summed.reshape(tile_rows, tile_cols, weight.shape[3])


def weight_terms(block_ext, upstream):
    tile_rows, tile_cols, width_out = upstream.shape
    flat_up = upstream.reshape(tile_rows * tile_cols, width_out)
    kernel_rows = []
    for row_off in range(3):
        kernel_cols = []
        for col_off in range(3):
            window = block_ext[
                row_off : row_off + tile_rows, col_off : col_off + tile_cols
            ].reshape(tile_rows * tile_cols, -1)
            kernel_cols.append(
                lax.dot_general(
                    window, flat_up, (((0,), (0,)), ((), ())), preferred_element_type=jnp.float32
                )
            )
        kernel_rows.append(jnp.stack(kernel_cols))
    return jnp.stack(kernel_rows)


def spread_back(upstream, weight):
    tile_rows, tile_cols, width_out = upstream.shape
    width_in = weight.shape[2]
    flat_up = upstream.reshape(tile_rows * tile_cols, width_out)
    summed = jnp.zeros((tile_rows + 2, tile_cols + 2, width_in), jnp.float32)
    for row_off in range(3):
        for col_off in range(3):
            product = lax.dot_general(
                flat_up,
                weight[row_off, col_off],
                (((1,), (1,)), ((), ())),
                preferred_element_type=jnp.float32,
            )
            summed = summed.at[row_off : row_off + tile_rows, col_off : col_off + tile_cols].add(
                product.reshape(tile_rows, tile_cols, width_in)
            )
    return summed.astype(jnp.bfloat16)


def fold_rims(doubled):
    whole = doubled.astype(jnp.float32)
    interior = whole[2:-2, 2:-2]
    interior = interior.at[0].add(whole[0, 2:-2]).at[-1].add(whole[-1, 2:-2])
    interior = interior.at[:, 0].add(whole[2:-2, 0]).at[:, -1].add(whole[2:-2, -1])
    interior = interior.at[0, 0].add(whole[0, 0]).at[0, -1].add(whole[0, -1])
    interior = interior.at[-1, 0].add(whole[-1, 0]).at[-1, -1].add(whole[-1, -1])
    return interior


def per_device(obs_values, tile_ids, obs_rows, obs_cols, w_embed, w_first, w_second, cotangent):
    bands = lax.axis_size("lat")
    sectors = lax.axis_size("lon")
    owners = bands * sectors
    obs_count, value_count = obs_values.shape
    capacity = 2 * obs_count // owners
    slot_total = owners * capacity
    target = tile_ids[:, 0]
    slot_index = target * capacity + assign_slots(target, owners)
    value_buffer = (
        jnp.zeros((value_count, slot_total), jnp.bfloat16).at[:, slot_index].set(obs_values.T)
    )
    where_buffer = (
        jnp.zeros((2, slot_total), jnp.float32)
        .at[:, slot_index]
        .set(jnp.stack([obs_rows, obs_cols]))
    )
    got_values, got_where = (
        lax.all_to_all(
            value_buffer.reshape(value_count, owners, capacity).astype(jnp.float32),
            ("lat", "lon"),
            split_axis=1,
            concat_axis=1,
            tiled=True,
        ).astype(jnp.bfloat16),
        lax.all_to_all(
            where_buffer.reshape(2, owners, capacity),
            ("lat", "lon"),
            split_axis=1,
            concat_axis=1,
            tiled=True,
        ),
    )
    got_values = got_values.reshape(value_count, slot_total)
    got_where = got_where.reshape(2, slot_total)
    tile_rows, tile_cols, channels = cotangent.shape
    setconv = gaussian_grid(got_values, got_where, tile_rows, tile_cols)
    embedded = jnp.einsum(
        "ifj,fc->ijc", setconv, w_embed, preferred_element_type=jnp.float32
    ).astype(jnp.bfloat16)
    embed_ext = extend(embedded)
    pre_act = convolve(embed_ext, w_first)
    hidden = jax.nn.silu(pre_act).astype(jnp.bfloat16)
    hidden_ext = extend(hidden)
    field = convolve(hidden_ext, w_second).astype(jnp.bfloat16)
    grad_second = weight_terms(hidden_ext, cotangent)
    hidden_grad = fold_rims(extend(spread_back(cotangent, w_second)))
    sigmoid_pre = jax.nn.sigmoid(pre_act)
    pre_grad = (hidden_grad * sigmoid_pre * (1.0 + pre_act * (1.0 - sigmoid_pre))).astype(
        jnp.bfloat16
    )
    grad_first = weight_terms(embed_ext, pre_grad)
    embed_grad = fold_rims(extend(spread_back(pre_grad, w_first))).astype(jnp.bfloat16)
    grad_embed = jnp.einsum("ifj,ijc->fc", setconv, embed_grad, preferred_element_type=jnp.float32)
    grad_embed, grad_first, grad_second = lax.psum(
        (grad_embed, grad_first, grad_second), ("lat", "lon")
    )
    return (field, grad_embed, grad_first, grad_second)


def solution(mesh):
    in_specs = (
        P(("lat", "lon"), None),
        P(("lat", "lon"), None),
        P(("lat", "lon")),
        P(("lat", "lon")),
        P(),
        P(),
        P(),
        P("lat", "lon", None),
    )
    out_specs = (P("lat", "lon", None), P(), P(), P())
    return jax.shard_map(
        per_device, mesh=mesh, in_specs=in_specs, out_specs=out_specs, check_vma=False
    )
```

profile of v0, /device:TPU:1, one launch (start us, length us, event | category | flops | bytes accessed | tf_op | source)
XLA Modules:
  0.0 463.6 jit_solution(10336123159310977203)
XLA Ops:
  9.3 2.0 copy-done.1
  11.3 2.7 add_add_fusion
  14.0 2.4 copy.59
  16.5 2.8 fusion.8
  19.5 2.7 copy.60
  22.2 24.6 %scatter_custom_fusion = f32[2,16384]{0,1:T(8,128)} fusion(s32[8192]{0:T(1024)S(1)} %bitcast.357, f32[8192,2]{1,0:T(8,128)} %copy.60, f32[]{:T(128)} %constant.867.clone.1), kind=kCustom, calls=%fused_computation.24 | custom fusion | bytes 131584 | tf_op jit(solution)/shard_map/scatter | solution.py:156
  46.8 5.9 %copy.61 = f32[2,128,128]{2,0,1:T(2,128)} copy(f32[2,128,128]{0,2,1:T(8,128)} %bitcast.327) | data formatting | bytes 262144 | tf_op jit(solution)/shard_map/reshape | solution.py:167
  52.8 12.6 %all-to-all-start = ((f32[2,128,128]{2,0,1:T(2,128)}), f32[2,128,128]{2,0,1:T(2,128)}, u32[]{:S(2)}, u32[]{:S(2)}) async-start(f32[2,128,128]{2,0,1:T(2,128)} %copy.61), calls=%async_computation | async-start | bytes 262144 | tf_op jit(solution)/shard_map/all_to_all | solution.py:166
  67.1 1.6 convolution_add_fusion.26
  68.7 3.4 scatter-add.115
  72.9 2.2 add_select_fusion.1
  75.1 3.4 scatter-add.116
  79.2 2.1 scatter-add.120
  81.6 2.1 scatter-add.121
  84.3 2.1 scatter-add.125
  86.8 2.1 scatter-add.126
  92.2 1.5 collective-permute-done.10
  93.6 5.0 %collective-permute-start.13 = (bf16[1,132,128]{2,1,0:T(8,128)(2,1)S(1)}, bf16[1,132,128]{2,1,0:T(8,128)(2,1)}, u32[]{:S(2)}, u32[]{:S(2)}) collective-permute-start(bf16[1,132,128]{2,1,0:T(8,128)(2,1)S(1)} %get-tuple-element.488), channel_id=1, source_target_pairs={{0,16},{16,32},{32,48},{48,64},{64,80},{80,96},{96,112},{1,17},{17... | collective-permute-start | bytes 101384 | tf_op jit(solution)/shard_map/ppermute | solution.py:17
  99.3 1.3 collective-permute-start.14
  100.6 1.8 collective-permute-start.12
  102.9 2.0 copy.63
  104.9 23.8 %scatter_custom_fusion.1 = bf16[24,16384]{0,1:T(8,128)(2,1)} fusion(s32[8192]{0:T(1024)} %bitcast.358, bf16[8192,24]{1,0:T(8,128)(2,1)S(1)} %copy.63, bf16[]{:T(256)} %constant.868.clone.1), kind=kCustom, calls=%fused_computation.43 | custom fusion | bytes 786944 | tf_op jit(solution)/shard_map/scatter | solution.py:151
  128.7 4.5 copy.64
  134.6 14.0 %all-to-all-start.1 = ((bf16[24,128,128]{2,0,1:T(8,128)(2,1)}), bf16[24,128,128]{2,0,1:T(8,128)(2,1)S(1)}, u32[]{:S(2)}, u32[]{:S(2)}) async-start(bf16[24,128,128]{2,0,1:T(8,128)(2,1)} %copy.64), calls=%async_computation.1 | async-start | bytes 1572864 | tf_op jit(solution)/shard_map/all_to_all | solution.py:159
  148.7 1.7 broadcast_select_fusion.1
  152.9 12.4 %all-to-all-done.1 = bf16[24,128,128]{2,0,1:T(8,128)(2,1)S(1)} async-done(((bf16[24,128,128]{2,0,1:T(8,128)(2,1)}), bf16[24,128,128]{2,0,1:T(8,128)(2,1)S(1)}, u32[]{:S(2)}, u32[]{:S(2)}) %all-to-all-start.1) | async-done | bytes 786464 | tf_op jit(solution)/shard_map/all_to_all | solution.py:159
  166.3 2.4 reshape_reshape.7
  168.8 1.6 copy.67
  170.4 21.6 %while.45 = (s32[]{:T(128)}, f32[384,128]{1,0:T(8,128)S(1)}, f32[4,2,4096]{2,0,1:T(4,128)S(1)}, bf16[4,24,4096]{2,1,0:T(8,128)(2,1)S(1)}, s32[]{:T(128)}, /*index=5*/s32[]{:T(128)}, s32[]{}) while((s32[]{:T(128)}, f32[384,128]{1,0:T(8,128)S(1)}, f32[4,2,4096]{2,0,1:T(4,128)S(1)}, bf16[4,24,4096]{2,1,0:T(8,128)(2,1)S(1)}, ...), condition=%wide.region_6.7_spmd.clone, body=%wide.region_5.6_spmd.clone.sunk | while | flops 408879264 | bytes 8291575 | solution.py:63
  170.6 2.1 multiply_convert_fusion.6
  172.8 3.0 convolution_add_fusion.28
  176.0 2.1 multiply_convert_fusion.6
  178.1 3.0 convolution_add_fusion.28
  181.4 2.1 multiply_convert_fusion.6
  183.5 3.0 convolution_add_fusion.28
  186.8 2.1 multiply_convert_fusion.6
  188.9 3.0 convolution_add_fusion.28
  197.1 2.3 collective-permute-start.3
  199.5 1.3 collective-permute-start.4
  200.8 1.4 collective-permute-start.2
  202.5 3.2 collective-permute-done.4
  209.0 2.2 fusion.26
  212.1 2.6 convolution_add_fusion.19
  223.1 6.0 %collective-permute-start.6 = (bf16[16,1,128]{2,1,0:T(2,128)(2,1)S(1)}, bf16[16,1,128]{2,1,0:T(2,128)(2,1)S(1)}, u32[]{:S(2)}, u32[]{:S(2)}) collective-permute-start(bf16[16,1,128]{2,1,0:T(2,128)(2,1)S(1)} %get-tuple-element.517), channel_id=1, source_target_pairs={{1,0},{2,1},{3,2},{4,3},{5,4},{6,5},{7,6},{8,7},{9,8},{10,9},{11,1... | collective-permute-start | bytes 12296 | tf_op jit(solution)/shard_map/ppermute | solution.py:19
  229.1 6.5 %scatter-add.144 = f32[18,130,128]{2,1,0:T(8,128)S(1)} dynamic-update-slice(f32[18,130,128]{2,1,0:T(8,128)S(1)} %scatter-add.141, f32[16,128,128]{2,1,0:T(8,128)} %convolution_add_fusion.19, s32[]{:T(128)} %bitcast.54, s32[]{:T(128)} %bitcast.55, s32[]{:T(128)} %constant.866.clone.1) | dynamic-update-slice | bytes 2097156 | tf_op jit(solution)/shard_map/scatter-add | solution.py:125
  235.6 3.2 add_select_fusion
  238.9 6.6 %scatter-add.145 = f32[18,130,128]{2,1,0:T(8,128)S(1)} dynamic-update-slice(f32[18,130,128]{2,1,0:T(8,128)S(1)} %scatter-add.144, f32[16,128,128]{2,1,0:T(8,128)} %add_select_fusion, s32[]{:T(128)} %bitcast.57, s32[]{:T(128)} %bitcast.58, s32[]{:T(128)} %constant.866.clone.1) | dynamic-update-slice | bytes 2097156 | tf_op jit(solution)/shard_map/scatter-add | solution.py:125
  245.8 1.3 convolution_add_fusion.17
  247.1 5.2 %scatter-add.149 = f32[18,130,128]{2,1,0:T(8,128)S(1)} dynamic-update-slice(f32[18,130,128]{2,1,0:T(8,128)S(1)} %fusion.22, f32[16,128,128]{2,1,0:T(8,128)} %convolution_add_fusion.17, s32[]{:T(128)} %constant.879.clone.1, s32[]{:T(128)} %constant.879.clone.1, s32[]{:T(128)} %constant.866.clone.1) | dynamic-update-slice | bytes 2097156 | tf_op jit(solution)/shard_map/scatter-add | solution.py:125
  252.3 1.3 convolution_add_fusion.16
  253.6 5.2 %scatter-add.150 = f32[18,130,128]{2,1,0:T(8,128)S(1)} dynamic-update-slice(f32[18,130,128]{2,1,0:T(8,128)S(1)} %scatter-add.149, f32[16,128,128]{2,1,0:T(8,128)} %convolution_add_fusion.16, s32[]{:T(128)} %constant.879.clone.1, s32[]{:T(128)} %constant.875.clone.1, s32[]{:T(128)} %constant.866.clone.1) | dynamic-update-slice | bytes 2097156 | tf_op jit(solution)/shard_map/scatter-add | solution.py:125
  259.1 1.3 convolution_add_fusion.14
  260.4 5.2 %scatter-add.154 = f32[18,130,128]{2,1,0:T(8,128)S(1)} dynamic-update-slice(f32[18,130,128]{2,1,0:T(8,128)S(1)} %fusion.21, f32[16,128,128]{2,1,0:T(8,128)} %convolution_add_fusion.14, s32[]{:T(128)} %constant.875.clone.1, s32[]{:T(128)} %constant.879.clone.1, s32[]{:T(128)} %constant.866.clone.1) | dynamic-update-slice | bytes 2097156 | tf_op jit(solution)/shard_map/scatter-add | solution.py:125
  265.6 1.3 convolution_add_fusion.13
  266.9 5.2 %scatter-add.155 = f32[18,130,128]{2,1,0:T(8,128)S(1)} dynamic-update-slice(f32[18,130,128]{2,1,0:T(8,128)S(1)} %scatter-add.154, f32[16,128,128]{2,1,0:T(8,128)} %convolution_add_fusion.13, s32[]{:T(128)} %constant.875.clone.1, s32[]{:T(128)} %constant.875.clone.1, s32[]{:T(128)} %constant.866.clone.1) | dynamic-update-slice | bytes 2097156 | tf_op jit(solution)/shard_map/scatter-add | solution.py:125
  275.2 5.6 %collective-permute-start.8 = (bf16[1,130,128]{2,1,0:T(8,128)(2,1)S(1)}, bf16[1,130,128]{2,1,0:T(8,128)(2,1)S(1)}, u32[]{:S(2)}, u32[]{:S(2)}) collective-permute-start(bf16[1,130,128]{2,1,0:T(8,128)(2,1)S(1)} %get-tuple-element.508), channel_id=1, source_target_pairs={{0,16},{16,32},{32,48},{48,64},{64,80},{80,96},{96,112},{1,17},{17... | collective-permute-start | bytes 99848 | tf_op jit(solution)/shard_map/ppermute | solution.py:17
  280.9 1.3 collective-permute-start.9
  283.7 5.5 %collective-permute-start.18 = (bf16[1,132,128]{2,1,0:T(8,128)(2,1)S(1)}, bf16[1,132,128]{2,1,0:T(8,128)(2,1)S(1)}, u32[]{:S(2)}, u32[]{:S(2)}) collective-permute-start(bf16[1,132,128]{2,1,0:T(8,128)(2,1)S(1)} %get-tuple-element.486), channel_id=1, source_target_pairs={{0,16},{16,32},{32,48},{48,64},{64,80},{80,96},{96,112},{1,17},{17... | collective-permute-start | bytes 101384 | tf_op jit(solution)/shard_map/ppermute | solution.py:17
  289.8 1.3 collective-permute-start.19
  291.1 2.7 collective-permute-start.17
  303.6 1.7 broadcast_select_fusion
  306.8 71.0 %psum.21 = f32[24,128]{1,0:T(8,128)} all-reduce(f32[24,128]{1,0:T(8,128)S(1)} %convolution_bitcast_fusion.18), channel_id=1, replica_groups=mesh['lat'=8,'lon'=16] {'lat','lon'}, use_global_device_ids=true, to_apply=%region_9.10 | all-reduce | flops 3072 | bytes 24576 | tf_op jit(solution)/shard_map/psum | solution.py:195
  377.8 75.8 %all-reduce.5.cloned.1.call-done = (f32[3,3,128,128]{3,2,1,0:T(8,128)}, f32[3,3,128,128]{3,2,1,0:T(8,128)}) async-done(((f32[3,3,128,128]{3,2,1,0:T(8,128)}, f32[3,3,128,128]{3,2,1,0:T(8,128)}), (f32[3,3,128,128]{3,2,1,0:T(8,128)}, f32[3,3,128,128]{3,2,1,0:T(8,128)})) %all-reduce.5.cloned.1.call-update) | async-done | bytes 1179664 | tf_op jit(solution)/shard_map/psum | solution.py:195
  453.7 2.0 copy.147
  (228 shorter events, 52.4 us)
Async XLA Ops:
  7.2 58.2 %copy-start = (bf16[16,128,128]{2,1,0:T(8,128)(2,1)S(1)}, bf16[16,128,128]{2,1,0:T(8,128)(2,1)}, u32[]{:S(2)}) copy-start(bf16[16,128,128]{2,1,0:T(8,128)(2,1)} %param.85) | copy-start | bytes 1572868
  9.3 2.0 copy-start.1
  14.0 2.5 copy-start.7
  16.5 3.0 copy-start.18
  16.5 3.0 copy-start.19
  19.4 2.8 copy-start.17
  46.8 18.6 %copy-start.3 = (bf16[3,3,128,128]{3,2,1,0:T(8,128)(2,1)S(1)}, bf16[3,3,128,128]{3,2,1,0:T(8,128)(2,1)}, u32[]{:S(2)}) copy-start(bf16[3,3,128,128]{3,2,1,0:T(8,128)(2,1)} %param.84) | copy-start | bytes 884740
  52.8 81.8 %all-to-all-start = ((f32[2,128,128]{2,0,1:T(2,128)}), f32[2,128,128]{2,0,1:T(2,128)}, u32[]{:S(2)}, u32[]{:S(2)}) async-start(f32[2,128,128]{2,0,1:T(2,128)} %copy.61), calls=%async_computation | async-start | bytes 262144 | tf_op jit(solution)/shard_map/all_to_all | solution.py:166
  68.7 3.4 copy-start.22
  88.9 2.0 copy-start.21
  89.0 3.2 collective-permute-start.11
  90.0 3.6 collective-permute-start.10
  93.6 39.6 %collective-permute-start.13 = (bf16[1,132,128]{2,1,0:T(8,128)(2,1)S(1)}, bf16[1,132,128]{2,1,0:T(8,128)(2,1)}, u32[]{:S(2)}, u32[]{:S(2)}) collective-permute-start(bf16[1,132,128]{2,1,0:T(8,128)(2,1)S(1)} %get-tuple-element.488), channel_id=1, source_target_pairs={{0,16},{16,32},{32,48},{48,64},{64,80},{80,96},{96,112},{1,17},{17... | collective-permute-start | bytes 101384 | tf_op jit(solution)/shard_map/ppermute | solution.py:17
  99.3 34.0 %collective-permute-start.14 = (bf16[1,132,128]{2,1,0:T(8,128)(2,1)S(1)}, bf16[1,132,128]{2,1,0:T(8,128)(2,1)}, u32[]{:S(2)}, u32[]{:S(2)}) collective-permute-start(bf16[1,132,128]{2,1,0:T(8,128)(2,1)S(1)} %get-tuple-element.489), channel_id=1, source_target_pairs={{16,0},{32,16},{48,32},{64,48},{80,64},{96,80},{112,96},{17,1},{33... | collective-permute-start | bytes 101384 | tf_op jit(solution)/shard_map/ppermute | solution.py:19
  100.6 32.7 %collective-permute-start.12 = (bf16[2,132,128]{2,1,0:T(8,128)(2,1)}, bf16[2,132,128]{2,1,0:T(8,128)(2,1)}, u32[]{:S(2)}, u32[]{:S(2)}) collective-permute-start(bf16[2,132,128]{2,1,0:T(8,128)(2,1)} %pad_maximum_fusion.10), channel_id=1, source_target_pairs={{0,8},{1,9},{2,10},{3,11},{4,12},{5,13},{6,14},{7,15},{8,0},{9,1},... | collective-permute-start | bytes 202760 | tf_op jit(solution)/shard_map/ppermute | solution.py:27
  134.6 30.6 %all-to-all-start.1 = ((bf16[24,128,128]{2,0,1:T(8,128)(2,1)}), bf16[24,128,128]{2,0,1:T(8,128)(2,1)S(1)}, u32[]{:S(2)}, u32[]{:S(2)}) async-start(bf16[24,128,128]{2,0,1:T(8,128)(2,1)} %copy.64), calls=%async_computation.1 | async-start | bytes 1572864 | tf_op jit(solution)/shard_map/all_to_all | solution.py:159
  148.6 305.1 %all-reduce.5.cloned.1.call-start = ((), (), s32[]{:S(2)}) async-start(), calls=%async_computation.2 | async-start | bytes 2359296 | tf_op jit(solution)/shard_map/psum | solution.py:195
  170.3 23.2 %copy-start.20 = (bf16[24,128]{1,0:T(8,128)(2,1)S(1)}, bf16[24,128]{1,0:T(8,128)(2,1)}, u32[]{:S(2)}) copy-start(bf16[24,128]{1,0:T(8,128)(2,1)} %param.82) | copy-start | bytes 18436
  170.4 25.4 %copy-start.2 = (bf16[3,3,128,128]{3,2,1,0:T(8,128)(2,1)S(1)}, bf16[3,3,128,128]{3,2,1,0:T(8,128)(2,1)}, u32[]{:S(2)}) copy-start(bf16[3,3,128,128]{3,2,1,0:T(8,128)(2,1)} %param.83) | copy-start | bytes 884740
  191.9 0.7 copy-start.12
  193.9 3.1 collective-permute-start.1
  194.5 2.6 collective-permute-start
  197.1 5.4 %collective-permute-start.3 = (bf16[1,130,128]{2,1,0:T(8,128)(2,1)S(1)}, bf16[1,130,128]{2,1,0:T(8,128)(2,1)S(1)}, u32[]{:S(2)}, u32[]{:S(2)}) collective-permute-start(bf16[1,130,128]{2,1,0:T(8,128)(2,1)S(1)} %get-tuple-element.512), channel_id=1, source_target_pairs={{0,16},{16,32},{32,48},{48,64},{64,80},{80,96},{96,112},{1,17},{17... | collective-permute-start | bytes 99848 | tf_op jit(solution)/shard_map/ppermute | solution.py:17
  199.5 6.2 %collective-permute-start.4 = (bf16[1,130,128]{2,1,0:T(8,128)(2,1)S(1)}, bf16[1,130,128]{2,1,0:T(8,128)(2,1)S(1)}, u32[]{:S(2)}, u32[]{:S(2)}) collective-permute-start(bf16[1,130,128]{2,1,0:T(8,128)(2,1)S(1)} %get-tuple-element.513), channel_id=1, source_target_pairs={{16,0},{32,16},{48,32},{64,48},{80,64},{96,80},{112,96},{17,1},{33... | collective-permute-start | bytes 99848 | tf_op jit(solution)/shard_map/ppermute | solution.py:19
  200.8 4.9 %collective-permute-start.2 = (bf16[2,130,128]{2,1,0:T(8,128)(2,1)S(1)}, bf16[2,130,128]{2,1,0:T(8,128)(2,1)S(1)}, u32[]{:S(2)}, u32[]{:S(2)}) collective-permute-start(bf16[2,130,128]{2,1,0:T(8,128)(2,1)S(1)} %pad_maximum_fusion.8), channel_id=1, source_target_pairs={{0,8},{1,9},{2,10},{3,11},{4,12},{5,13},{6,14},{7,15},{8,0},{9,1},... | collective-permute-start | bytes 199688 | tf_op jit(solution)/shard_map/ppermute | solution.py:27
  223.1 52.0 %collective-permute-start.6 = (bf16[16,1,128]{2,1,0:T(2,128)(2,1)S(1)}, bf16[16,1,128]{2,1,0:T(2,128)(2,1)S(1)}, u32[]{:S(2)}, u32[]{:S(2)}) collective-permute-start(bf16[16,1,128]{2,1,0:T(2,128)(2,1)S(1)} %get-tuple-element.517), channel_id=1, source_target_pairs={{1,0},{2,1},{3,2},{4,3},{5,4},{6,5},{7,6},{8,7},{9,8},{10,9},{11,1... | collective-permute-start | bytes 12296 | tf_op jit(solution)/shard_map/ppermute | solution.py:19
  229.1 46.1 %collective-permute-start.5 = (bf16[16,1,128]{2,1,0:T(2,128)(2,1)S(1)}, bf16[16,1,128]{2,1,0:T(2,128)(2,1)S(1)}, u32[]{:S(2)}, u32[]{:S(2)}) collective-permute-start(bf16[16,1,128]{2,1,0:T(2,128)(2,1)S(1)} %get-tuple-element.516), channel_id=1, source_target_pairs={{0,1},{1,2},{2,3},{3,4},{4,5},{5,6},{6,7},{7,8},{8,9},{9,10},{10,1... | collective-permute-start | bytes 12296 | tf_op jit(solution)/shard_map/ppermute | solution.py:17
  272.1 2.0 copy-start.13
  272.2 2.0 copy-start.14
  272.2 2.0 copy-start.8
  272.2 2.0 copy-start.9
  272.2 2.0 copy-start.10
  272.2 2.0 copy-start.11
  272.2 2.0 copy-start.15
  272.2 2.0 copy-start.16
  272.3 11.3 %collective-permute-start.16 = (bf16[18,1,128]{2,1,0:T(2,128)(2,1)S(1)}, bf16[18,1,128]{2,1,0:T(2,128)(2,1)S(1)}, u32[]{:S(2)}, u32[]{:S(2)}) collective-permute-start(bf16[18,1,128]{2,1,0:T(2,128)(2,1)S(1)} %get-tuple-element.491), channel_id=1, source_target_pairs={{1,0},{2,1},{3,2},{4,3},{5,4},{6,5},{7,6},{8,7},{9,8},{10,9},{11,1... | collective-permute-start | bytes 13832 | tf_op jit(solution)/shard_map/ppermute | solution.py:19
  272.9 10.7 %collective-permute-start.15 = (bf16[18,1,128]{2,1,0:T(2,128)(2,1)S(1)}, bf16[18,1,128]{2,1,0:T(2,128)(2,1)S(1)}, u32[]{:S(2)}, u32[]{:S(2)}) collective-permute-start(bf16[18,1,128]{2,1,0:T(2,128)(2,1)S(1)} %get-tuple-element.490), channel_id=1, source_target_pairs={{0,1},{1,2},{2,3},{3,4},{4,5},{5,6},{6,7},{7,8},{8,9},{9,10},{10,1... | collective-permute-start | bytes 13832 | tf_op jit(solution)/shard_map/ppermute | solution.py:17
  275.2 15.9 %collective-permute-start.8 = (bf16[1,130,128]{2,1,0:T(8,128)(2,1)S(1)}, bf16[1,130,128]{2,1,0:T(8,128)(2,1)S(1)}, u32[]{:S(2)}, u32[]{:S(2)}) collective-permute-start(bf16[1,130,128]{2,1,0:T(8,128)(2,1)S(1)} %get-tuple-element.508), channel_id=1, source_target_pairs={{0,16},{16,32},{32,48},{48,64},{64,80},{80,96},{96,112},{1,17},{17... | collective-permute-start | bytes 99848 | tf_op jit(solution)/shard_map/ppermute | solution.py:17
  280.9 13.0 %collective-permute-start.9 = (bf16[1,130,128]{2,1,0:T(8,128)(2,1)S(1)}, bf16[1,130,128]{2,1,0:T(8,128)(2,1)S(1)}, u32[]{:S(2)}, u32[]{:S(2)}) collective-permute-start(bf16[1,130,128]{2,1,0:T(8,128)(2,1)S(1)} %get-tuple-element.509), channel_id=1, source_target_pairs={{16,0},{32,16},{48,32},{64,48},{80,64},{96,80},{112,96},{17,1},{33... | collective-permute-start | bytes 99848 | tf_op jit(solution)/shard_map/ppermute | solution.py:19
  282.2 11.7 %collective-permute-start.7 = (bf16[2,130,128]{2,1,0:T(8,128)(2,1)S(1)}, bf16[2,130,128]{2,1,0:T(8,128)(2,1)S(1)}, u32[]{:S(2)}, u32[]{:S(2)}) collective-permute-start(bf16[2,130,128]{2,1,0:T(8,128)(2,1)S(1)} %pad_maximum_fusion.9), channel_id=1, source_target_pairs={{0,8},{1,9},{2,10},{3,11},{4,12},{5,13},{6,14},{7,15},{8,0},{9,1},... | collective-permute-start | bytes 199688 | tf_op jit(solution)/shard_map/ppermute | solution.py:27
  283.7 18.5 %collective-permute-start.18 = (bf16[1,132,128]{2,1,0:T(8,128)(2,1)S(1)}, bf16[1,132,128]{2,1,0:T(8,128)(2,1)S(1)}, u32[]{:S(2)}, u32[]{:S(2)}) collective-permute-start(bf16[1,132,128]{2,1,0:T(8,128)(2,1)S(1)} %get-tuple-element.486), channel_id=1, source_target_pairs={{0,16},{16,32},{32,48},{48,64},{64,80},{80,96},{96,112},{1,17},{17... | collective-permute-start | bytes 101384 | tf_op jit(solution)/shard_map/ppermute | solution.py:17
  289.8 12.3 %collective-permute-start.19 = (bf16[1,132,128]{2,1,0:T(8,128)(2,1)S(1)}, bf16[1,132,128]{2,1,0:T(8,128)(2,1)}, u32[]{:S(2)}, u32[]{:S(2)}) collective-permute-start(bf16[1,132,128]{2,1,0:T(8,128)(2,1)S(1)} %get-tuple-element.487), channel_id=1, source_target_pairs={{16,0},{32,16},{48,32},{64,48},{80,64},{96,80},{112,96},{17,1},{33... | collective-permute-start | bytes 101384 | tf_op jit(solution)/shard_map/ppermute | solution.py:19
  291.1 11.1 %collective-permute-start.17 = (bf16[2,132,128]{2,1,0:T(8,128)(2,1)}, bf16[2,132,128]{2,1,0:T(8,128)(2,1)}, u32[]{:S(2)}, u32[]{:S(2)}) collective-permute-start(bf16[2,132,128]{2,1,0:T(8,128)(2,1)} %pad_maximum_fusion.11), channel_id=1, source_target_pairs={{0,8},{1,9},{2,10},{3,11},{4,12},{5,13},{6,14},{7,15},{8,0},{9,1},... | collective-permute-start | bytes 202760 | tf_op jit(solution)/shard_map/ppermute | solution.py:27
  296.2 1.0 copy-start.4
  298.0 1.2 copy-start.5
  453.7 2.0 copy-start.6
Sparse Core Ops, SparseCore 0:
  302.3 151.3 all-reduce.4
where the time goes:
time: 472 us; the launch traced here: 464 us
  local copies, waits for them, and re-layouts  136 us (29%)
  waiting for transfers between devices  94.6 us (20%)
  blocking collectives  71 us (15%)
  starting transfers between devices  67.9 us (14%)
  matrix products  49.2 us (10%)
  other arithmetic  29.3 us (6%)
  between operations  15.5 us (3%)
    psum x1, waiting for transfers between devices, per_device(): lax.psum((grad_embed, grad_first, grad_second), ('lat', 'lon'))  75.8 us
    psum x1, blocking collectives, per_device(): lax.psum((grad_embed, grad_first, grad_second), ('lat', 'lon'))  71 us
    scatter-add x14, local copies, waits for them, and re-layouts, spread_back(): summed.at[row_off:row_off + tile_rows, col_off:col_off + tile_cols]  49.4 us
    scatter x1, local copies, waits for them, and re-layouts, per_device(): where_buffer = jnp.zeros((2, slot_total), jnp.float32).at[:, slot_index]....  24.6 us
    scatter x1, local copies, waits for them, and re-layouts, per_device(): jnp.zeros((value_count, slot_total), jnp.bfloat16).at[:, slot_index]  23.8 us
    ppermute x8, starting transfers between devices, with_halo(): lax.ppermute(tail, axis, [(i, (i + 1) % count) for i in range(ends)])  21.7 us
    dot_general x18, matrix products, spread_back(): lax.dot_general(flat_up, weight[row_off, col_off], (((1,), (1,)), ((), ()...  17.8 us
    all_to_all x1, starting transfers between devices, per_device(): lax.all_to_all(value_buffer.reshape(value_count, owners, capacity).astype...  14 us
  transfers between devices with their start and end apart: 23, of which 6 were waited for; matrix products, arithmetic and copies ran while one was open for 26% of the time, Pallas kernels for 0%

commit v1 on v0

v1 whole, which is shorter than its diff:
```python
import functools
import math
import jax
import jax.numpy as jnp
from jax import lax
from jax.experimental import pallas as pl
from jax.experimental.pallas import tpu as pltpu
from jax.sharding import PartitionSpec as P

F32 = jnp.float32
BF16 = jnp.bfloat16
spread_cells = 1.0
ALL = ("lat", "lon")

TR, TC, C = 16, 128, 128
PITCH = TC + 16
LEN = 3040
PART = 304
FIRST = PITCH
OWN = 16 + 2 * PITCH
FEAT = 32
RED = 24


def dot(a, b):
    return jnp.dot(a, b, preferred_element_type=F32)


def dot_nt(a, b):
    return lax.dot_general(a, b, (((1,), (1,)), ((), ())), preferred_element_type=F32)


def place(i):
    return 16 + (i + 2) * PITCH


def pack_kernel(ids_ref, rows_ref, cols_ref, vals_ref, out_ref, q_ref, v_ref, pair_ref, acc_ref):
    step = pl.program_id(0)
    count = ids_ref.shape[1]
    owners = out_ref.shape[0] * pl.num_programs(0)
    sub = 256
    part = 1024
    pairs = out_ref.shape[0] // 2

    @pl.when(step == 0)
    def _():
        owner = lax.broadcasted_iota(jnp.int32, (owners, sub), 0)
        slot = lax.broadcasted_iota(jnp.int32, (sub, sub), 0)
        upto = slot <= lax.broadcasted_iota(jnp.int32, (sub, sub), 1)
        upto = jnp.concatenate(
            [jnp.where(upto, 1.0, 0.0).astype(BF16), jnp.ones((sub, 128), BF16)], axis=1
        )

        def body(k, carry):
            at = pl.ds(pl.multiple_of(k * sub, sub), sub)
            ids = ids_ref[:, at]
            hot = owner == ids
            counted = dot(jnp.where(hot, 1.0, 0.0).astype(BF16), upto)
            before = counted[:, :sub] + jnp.concatenate([carry, carry], axis=1)
            rank = jnp.sum(jnp.where(hot, before, 0.0), axis=0, keepdims=True) - 1.0
            key = rank.astype(jnp.int32) + (ids & 1) * 128
            q_ref[:, at] = jnp.where(slot == key, 1.0, 0.0).astype(BF16)
            pair_ref[:, at] = jnp.broadcast_to((ids >> 1).astype(F32), (FEAT, sub)).astype(BF16)
            rows, cols = rows_ref[:, at], cols_ref[:, at]
            rows_hi, cols_hi = rows.astype(BF16).astype(F32), cols.astype(BF16).astype(F32)
            tail = jnp.concatenate(
                [rows_hi, rows - rows_hi, cols_hi, cols - cols_hi, jnp.zeros((4, sub), F32)], axis=0
            )
            v_ref[:, at] = jnp.concatenate([vals_ref[:, at].astype(F32), tail], axis=0).astype(BF16)
            return carry + counted[:, sub:]

        lax.fori_loop(0, count // sub, body, jnp.zeros((owners, 128), F32))

    acc_ref[...] = jnp.zeros_like(acc_ref)

    def body(k, carry):
        at = pl.ds(pl.multiple_of(k * part, part), part)
        base = jnp.full((FEAT, part), (step * pairs).astype(F32), F32).astype(BF16)
        pair = pair_ref[:, at] - base
        values = v_ref[:, at]
        none = jnp.zeros_like(values)
        left = jnp.concatenate([jnp.where(pair == p, values, none) for p in range(pairs)], axis=0)
        acc_ref[...] += dot_nt(left, q_ref[:, at])
        return carry

    lax.fori_loop(0, count // part, body, 0)
    for p in range(pairs):
        out_ref[2 * p] = acc_ref[p * FEAT : (p + 1) * FEAT, :128].astype(BF16)
        out_ref[2 * p + 1] = acc_ref[p * FEAT : (p + 1) * FEAT, 128:].astype(BF16)


def pack(ids, rows, cols, values):
    count = ids.shape[1]
    owners = 128
    steps = 8
    whole = lambda a: pl.BlockSpec(a.shape, lambda i: (0, 0))
    return pl.pallas_call(
        pack_kernel,
        grid=(steps,),
        in_specs=[whole(ids), whole(rows), whole(cols), whole(values)],
        out_specs=pl.BlockSpec((owners // steps, FEAT, 128), lambda i: (i, 0, 0)),
        out_shape=jax.ShapeDtypeStruct((owners, FEAT, 128), BF16),
        scratch_shapes=[
            pltpu.VMEM((256, count), BF16),
            pltpu.VMEM((FEAT, count), BF16),
            pltpu.VMEM((FEAT, count), BF16),
            pltpu.VMEM((owners // steps // 2 * FEAT, 256), F32),
        ],
        compiler_params=pltpu.CompilerParams(vmem_limit_bytes=32 << 20),
        cost_estimate=pl.CostEstimate(flops=2 * 2048 * 256 * 8192, bytes_accessed=3 << 20, transcendentals=0),
        name="pack",
    )(ids, rows, cols, values)


def setconv_kernel(where_ref, got_ref, s_ref, left_ref, right_ref, v1_ref, v2_ref,
                   c1l_ref, c1r_ref, c2l_ref, c2r_ref, acc_ref):
    step = pl.program_id(0)
    x = jnp.concatenate([got_ref[k] for k in range(got_ref.shape[0])], axis=1).astype(F32)
    n = x.shape[1]
    alpha = math.sqrt(0.5 / math.log(2.0)) / spread_cells
    row = (x[24:25] + x[25:26]) * alpha
    col = (x[26:27] + x[27:28]) * alpha
    row_mid = (lax.broadcasted_iota(jnp.int32, (TR, n), 0).astype(F32) + 0.5) * alpha
    col_mid = (lax.broadcasted_iota(jnp.int32, (TC, n), 0).astype(F32) + 0.5) * alpha
    row_weight = jnp.exp2(-jnp.square(row - row_mid))
    col_weight = jnp.exp2(-jnp.square(col - col_mid)).astype(BF16)
    weighted = jnp.concatenate([(x * row_weight[i : i + 1]).astype(BF16) for i in range(TR)], axis=0)
    term = dot_nt(col_weight, weighted)

    @pl.when(step == 0)
    def _():
        acc_ref[...] = term

    @pl.when(step > 0)
    def _():
        acc_ref[...] += term

    @pl.when(step == pl.num_programs(0) - 1)
    def _():
        s = acc_ref[...].astype(BF16)
        s_ref[...] = s
        left_ref[...] = s[:16]
        right_ref[...] = s[TC - 16 :]
        low = where_ref[1] < where_ref[3] // 2
        top, bottom = s[:, :128], s[:, -128:]
        v1 = jnp.where(low, bottom, top)
        v2 = jnp.where(low, top, bottom)
        v1_ref[...] = v1
        v2_ref[...] = v2
        c1l_ref[...] = v1[TC - 16 :]
        c1r_ref[...] = v1[:16]
        c2l_ref[...] = v2[TC - 16 :]
        c2r_ref[...] = v2[:16]


def setconv(where, got):
    steps = 16
    fixed = lambda *shape: pl.BlockSpec(shape, lambda i: (0,) * len(shape))
    lanes = TR * FEAT
    shapes = [(TC, lanes), (16, lanes), (16, lanes), (TC, 128), (TC, 128)] + [(16, 128)] * 4
    return pl.pallas_call(
        setconv_kernel,
        grid=(steps,),
        in_specs=[
            pl.BlockSpec(memory_space=pltpu.SMEM),
            pl.BlockSpec((got.shape[0] // steps, FEAT, 128), lambda i: (i, 0, 0)),
        ],
        out_specs=[fixed(*s) for s in shapes],
        out_shape=[jax.ShapeDtypeStruct(s, BF16) for s in shapes],
        scratch_shapes=[pltpu.VMEM((TC, lanes), F32)],
        compiler_params=pltpu.CompilerParams(vmem_limit_bytes=32 << 20),
        cost_estimate=pl.CostEstimate(
            flops=2 * 512 * 256 * 16384, bytes_accessed=2 << 20, transcendentals=144 * 16384
        ),
        name="setconv",
    )(where, got)


def shifted_copies(flat_ref, out_ref, begin, parts):
    def body(k, carry):
        at = pl.multiple_of(begin + k * PART, 16)
        for s in range(3):
            piece = flat_ref[pl.ds(at, PART + 16), :]
            out_ref[pl.ds(at, PART), s * C : (s + 1) * C] = piece[7 + s : 7 + s + PART].astype(BF16)
        return carry

    lax.fori_loop(0, parts, body, 0)


def conv_rows(src_ref, at, rows, weights):
    total = dot(src_ref[pl.ds(at - PITCH, rows), :], weights[0])
    total += dot(src_ref[pl.ds(at, rows), :], weights[1])
    total += dot(src_ref[pl.ds(at + PITCH, rows), :], weights[2])
    return total


def back_rows(src_ref, at, rows, weights):
    total = dot_nt(src_ref[pl.ds(at - PITCH, rows), :], weights[0])
    total += dot_nt(src_ref[pl.ds(at, rows), :], weights[1])
    total += dot_nt(src_ref[pl.ds(at + PITCH, rows), :], weights[2])
    return total


def fill_flat(flat_ref, centre, left, right):
    first = lax.broadcasted_iota(jnp.int32, (16, C), 0) < 8
    flat_ref[:8] = jnp.zeros((8, C), F32)
    flat_ref[8:24] = left(-2)
    for i in range(-2, TR + 2):
        at = 8 + place(i)
        flat_ref[at : at + TC] = centre(i)
        after = jnp.where(first, right(i), left(i + 1)) if i < TR + 1 else right(i)
        flat_ref[at + TC : at + PITCH] = after
    end = 8 + place(TR + 2)
    flat_ref[end:] = jnp.zeros((flat_ref.shape[0] - end, C), F32)


def sides(where_ref):
    lon, lon_size = where_ref[1], where_ref[3]
    half = lon_size // 2
    own = lon < half
    left = jnp.where(lon == 0, lon_size - 1, lon - 1) < half
    right = jnp.where(lon == lon_size - 1, 0, lon + 1) < half
    return own, left, right


def arrange_back(w_ref, out_ref):
    for r in range(3):
        for s in range(3):
            out_ref[r, :, s * C : (s + 1) * C] = w_ref[2 - r, 2 - s]


def edges_kernel(where_ref, cot_ref, left_ref, right_ref, v1_ref, v2_ref, c1l_ref, c1r_ref, c2l_ref, c2r_ref):
    low, _, _ = sides(where_ref)
    left_ref[...] = cot_ref[:, :16, :]
    right_ref[...] = cot_ref[:, TC - 16 :, :]
    top, bottom = cot_ref[:2], cot_ref[TR - 2 :]
    v1 = jnp.where(low, bottom, top)
    v2 = jnp.where(low, top, bottom)
    v1_ref[...] = v1
    v2_ref[...] = v2
    c1l_ref[...] = v1[:, TC - 16 :]
    c1r_ref[...] = v1[:, :16]
    c2l_ref[...] = v2[:, TC - 16 :]
    c2r_ref[...] = v2[:, :16]


def edges(where, cot):
    shapes = [(TR, 16, C), (TR, 16, C), (2, TC, C), (2, TC, C)] + [(2, 16, C)] * 4
    return pl.pallas_call(
        edges_kernel,
        in_specs=[pl.BlockSpec(memory_space=pltpu.SMEM), pl.BlockSpec(memory_space=pltpu.VMEM)],
        out_specs=[pl.BlockSpec(memory_space=pltpu.VMEM)] * len(shapes),
        out_shape=[jax.ShapeDtypeStruct(s, BF16) for s in shapes],
        cost_estimate=pl.CostEstimate(flops=0, bytes_accessed=1 << 20, transcendentals=0),
        name="edges",
    )(where, cot)


def cot_kernel(where_ref, cot_ref, left_ref, right_ref, v1_ref, v2_ref, c1l_ref, c1r_ref, c2l_ref, c2r_ref,
               w_ref, hg_ref, cot_t_ref, flat_ref, copies_ref, back_ref, own_ref):
    low, low_left, low_right = sides(where_ref)
    north = where_ref[0] == 0
    south = where_ref[0] == where_ref[2] - 1
    up = jnp.where(low, v1_ref[...], v2_ref[...]).astype(F32)
    down = jnp.where(low, v2_ref[...], v1_ref[...]).astype(F32)
    up_l = jnp.where(low_left, c1l_ref[...], c2l_ref[...]).astype(F32)
    down_l = jnp.where(low_left, c2l_ref[...], c1l_ref[...]).astype(F32)
    up_r = jnp.where(low_right, c1r_ref[...], c2r_ref[...]).astype(F32)
    down_r = jnp.where(low_right, c2r_ref[...], c1r_ref[...]).astype(F32)

    def pick(inner, up, down):
        def get(i):
            if i < 0:
                near, far = jnp.where(north, up[0], up[1]), jnp.where(north, up[1], up[0])
                return near if i == -1 else far
            if i >= TR:
                near, far = jnp.where(south, down[1], down[0]), jnp.where(south, down[0], down[1])
                return near if i == TR else far
            return inner[i].astype(F32)

        return get

    fill_flat(flat_ref, pick(cot_ref, up, down), pick(left_ref, up_l, down_l), pick(right_ref, up_r, down_r))
    shifted_copies(flat_ref, copies_ref, 0, LEN // PART)
    arrange_back(w_ref, back_ref)

    def body(k, carry):
        at = pl.multiple_of(FIRST + k * PART, 16)
        hg_ref[pl.ds(at, PART), :] = back_rows(copies_ref, at, PART, [back_ref[0], back_ref[1], back_ref[2]])
        return carry

    lax.fori_loop(0, 9, body, 0)

    @pl.when(north)
    def _():
        at = place(-1) - 16
        got = back_rows(copies_ref, at, PART, [back_ref[2], back_ref[1], back_ref[2]])
        hg_ref[at + 8 : at + PART - 8] = got[8:-8]

    @pl.when(south)
    def _():
        at = place(TR - 1) - 16
        got = back_rows(copies_ref, at, PART, [back_ref[0], back_ref[1], back_ref[0]])
        hg_ref[at + 8 : at + PART - 8] = got[8:-8]

    for i in range(TR):
        own_ref[i * PITCH : i * PITCH + TC] = cot_ref[i]
        own_ref[i * PITCH + TC : (i + 1) * PITCH] = jnp.zeros((PITCH - TC, C), BF16)
    transpose_flat(own_ref, cot_t_ref)


def transpose_flat(own_ref, out_ref):
    def body(m, carry):
        at = pl.multiple_of(m * 128, 128)
        out_ref[:, pl.ds(at, 128)] = own_ref[pl.ds(at, 128), :].T
        return carry

    lax.fori_loop(0, own_ref.shape[0] // 128, body, 0)


def cot_back(where, cot, halo, w_second):
    vmem = pl.BlockSpec(memory_space=pltpu.VMEM)
    return pl.pallas_call(
        cot_kernel,
        in_specs=[pl.BlockSpec(memory_space=pltpu.SMEM)] + [vmem] * 10,
        out_specs=[vmem] * 2,
        out_shape=[
            jax.ShapeDtypeStruct((LEN, C), F32),
            jax.ShapeDtypeStruct((C, TR * PITCH), BF16),
        ],
        scratch_shapes=[
            pltpu.VMEM((LEN + 16, C), F32),
            pltpu.VMEM((LEN, 3 * C), BF16),
            pltpu.VMEM((3, C, 3 * C), BF16),
            pltpu.VMEM((TR * PITCH, C), BF16),
        ],
        compiler_params=pltpu.CompilerParams(vmem_limit_bytes=32 << 20),
        cost_estimate=pl.CostEstimate(flops=2 * 2736 * 1152 * 256, bytes_accessed=4 << 20, transcendentals=0),
        name="cot_back",
    )(where, cot, *halo, w_second)


def main_kernel(where_ref, s_ref, left_ref, right_ref, v1_ref, v2_ref, c1l_ref, c1r_ref, c2l_ref, c2r_ref,
                wide_ref, w1_ref, w2_ref, hg_ref, cot_t_ref,
                field_ref, red_ref,
                flat_ref, x_ref, pre_ref, h_ref, back_ref, own_ref, own_t_ref, eg_ref):
    low, low_left, low_right = sides(where_ref)
    north = where_ref[0] == 0
    south = where_ref[0] == where_ref[2] - 1
    wide = wide_ref[...]

    def embed(s):
        return [dot(s[:, g * 128 : (g + 1) * 128], wide) for g in range(s.shape[1] // 128)]

    def rows_of(inner, up, down):
        inner, up, down = embed(inner), embed(up)[0], embed(down)[0]

        def get(i):
            block = lambda a, k: a[:, k * C : (k + 1) * C]
            if i == -1:
                return jnp.where(north, block(up, 0), block(up, 3))
            if i == -2:
                return jnp.where(north, block(up, 1), block(up, 2))
            if i == TR:
                return jnp.where(south, block(down, 3), block(down, 0))
            if i == TR + 1:
                return jnp.where(south, block(down, 2), block(down, 1))
            return block(inner[i // 4], i % 4)

        return get

    centre = rows_of(
        s_ref[...],
        jnp.where(low, v1_ref[...], v2_ref[...]),
        jnp.where(low, v2_ref[...], v1_ref[...]),
    )
    left = rows_of(
        left_ref[...],
        jnp.where(low_left, c1l_ref[...], c2l_ref[...]),
        jnp.where(low_left, c2l_ref[...], c1l_ref[...]),
    )
    right = rows_of(
        right_ref[...],
        jnp.where(low_right, c1r_ref[...], c2r_ref[...]),
        jnp.where(low_right, c2r_ref[...], c1r_ref[...]),
    )
    fill_flat(flat_ref, centre, left, right)
    shifted_copies(flat_ref, x_ref, 0, LEN // PART)

    def weights(w_ref, order):
        return [w_ref[r].reshape(3 * C, C) for r in order]

    def pre_body(k, carry):
        at = pl.multiple_of(FIRST + k * PART, 16)
        pre_ref[pl.ds(at, PART), :] = conv_rows(x_ref, at, PART, weights(w1_ref, (0, 1, 2)))
        return carry

    lax.fori_loop(0, 9, pre_body, 0)

    def pole_pre(at):
        got = conv_rows(x_ref, at, PITCH + 16, weights(w1_ref, (2, 1, 0)))
        pre_ref[at + 8 : at + PITCH + 8] = got[8:-8]

    @pl.when(north)
    def _():
        pole_pre(place(-1) - 16)

    @pl.when(south)
    def _():
        pole_pre(place(TR) - 16)

    flat_ref[8 + FIRST - 16 : 8 + FIRST] = jnp.zeros((16, C), F32)
    flat_ref[8 + FIRST + 9 * PART : 24 + FIRST + 9 * PART] = jnp.zeros((16, C), F32)

    def hidden_body(k, carry):
        at = pl.multiple_of(FIRST + k * PART, 16)
        pre = pre_ref[pl.ds(at, PART), :]
        flat_ref[pl.ds(at + 8, PART), :] = pre / (1.0 + jnp.exp(-pre))
        return carry

    lax.fori_loop(0, 9, hidden_body, 0)
    shifted_copies(flat_ref, h_ref, FIRST, 9)

    def field_body(k, carry):
        at = pl.multiple_of(OWN + k * 2 * PITCH, 16)
        got = conv_rows(h_ref, at, 2 * PITCH, weights(w2_ref, (0, 1, 2))).astype(BF16)
        field_ref[2 * k] = got[:TC]
        field_ref[2 * k + 1] = got[PITCH : PITCH + TC]
        return carry

    lax.fori_loop(0, TR // 2, field_body, 0)

    def weight_grad(src_ref, grad_t_ref, begin):
        for r in range(3):
            at = OWN + (r - 1) * PITCH
            got = dot(grad_t_ref[...], src_ref[at : at + TR * PITCH]).astype(BF16)
            for s in range(3):
                to = begin + (3 * r + s) * C
                red_ref[to : to + C] = got[:, s * C : (s + 1) * C]

    weight_grad(h_ref, cot_t_ref, 9 * C)

    def grad_body(k, carry):
        at = pl.multiple_of(FIRST + k * PART, 16)
        pre = pre_ref[pl.ds(at, PART), :]
        sig = 1.0 / (1.0 + jnp.exp(-pre))
        flat_ref[pl.ds(at + 8, PART), :] = hg_ref[pl.ds(at, PART), :] * (sig * (1.0 + pre * (1.0 - sig)))
        return carry

    lax.fori_loop(0, 9, grad_body, 0)
    shifted_copies(flat_ref, h_ref, FIRST, 9)
    for i in range(TR):
        at = 8 + place(i)
        own_ref[i * PITCH : i * PITCH + TC] = flat_ref[at : at + TC].astype(BF16)
        own_ref[i * PITCH + TC : (i + 1) * PITCH] = jnp.zeros((PITCH - TC, C), BF16)
    transpose_flat(own_ref, own_t_ref)
    weight_grad(x_ref, own_t_ref, 0)

    arrange_back(w1_ref, back_ref)

    def eg_body(k, carry):
        at = pl.multiple_of(OWN + k * 2 * PITCH, 16)
        got = back_rows(h_ref, at, 2 * PITCH, [back_ref[0], back_ref[1], back_ref[2]])
        eg_ref[pl.ds(pl.multiple_of(k * 2 * PITCH, 16), 2 * PITCH), :] = got.astype(BF16)
        return carry

    lax.fori_loop(0, TR // 2, eg_body, 0)

    @pl.when(north)
    def _():
        got = back_rows(h_ref, OWN, PITCH, [back_ref[2], back_ref[1], back_ref[2]])
        eg_ref[:PITCH] = got.astype(BF16)

    @pl.when(south)
    def _():
        got = back_rows(h_ref, place(TR - 1), PITCH, [back_ref[0], back_ref[1], back_ref[0]])
        eg_ref[(TR - 1) * PITCH :] = got.astype(BF16)

    total = jnp.zeros((FEAT, C), F32)
    for g in range(TR // 4):
        s_t = s_ref[:, g * 128 : (g + 1) * 128].T
        for k in range(4):
            i = 4 * g + k
            total += dot(s_t[k * FEAT : (k + 1) * FEAT], eg_ref[i * PITCH : i * PITCH + TC])
    red_ref[18 * C : 18 * C + FEAT] = total.astype(BF16)
    red_ref[18 * C + FEAT :] = jnp.zeros((red_ref.shape[0] - 18 * C - FEAT, C), BF16)


def main(where, s, halo, wide, w_first, w_second, hg, cot_t, owners):
    vmem = pl.BlockSpec(memory_space=pltpu.VMEM)
    return pl.pallas_call(
        main_kernel,
        in_specs=[pl.BlockSpec(memory_space=pltpu.SMEM)] + [vmem] * 14,
        out_specs=[vmem] * 2,
        out_shape=[
            jax.ShapeDtypeStruct((TR, TC, C), BF16),
            jax.ShapeDtypeStruct((owners * RED, C), BF16),
        ],
        scratch_shapes=[
            pltpu.VMEM((LEN + 16, C), F32),
            pltpu.VMEM((LEN, 3 * C), BF16),
            pltpu.VMEM((LEN, C), F32),
            pltpu.VMEM((LEN, 3 * C), BF16),
            pltpu.VMEM((3, C, 3 * C), BF16),
            pltpu.VMEM((TR * PITCH, C), BF16),
            pltpu.VMEM((C, TR * PITCH), BF16),
            pltpu.VMEM((TR * PITCH, C), BF16),
        ],
        compiler_params=pltpu.CompilerParams(vmem_limit_bytes=48 << 20),
        cost_estimate=pl.CostEstimate(flops=8 << 30, bytes_accessed=6 << 20, transcendentals=1 << 20),
        name="main",
    )(where, s, *halo, wide, w_first, w_second, hg, cot_t)


def sum_kernel(got_ref, out_ref):
    step = pl.program_id(0)

    @pl.when(step == 0)
    def _():
        out_ref[...] = jnp.sum(got_ref[...].astype(F32), axis=0)

    @pl.when(step > 0)
    def _():
        out_ref[...] += jnp.sum(got_ref[...].astype(F32), axis=0)


def unpack_kernel(got_ref, embed_ref, first_ref, second_ref):
    for r in range(3):
        for s in range(3):
            at = (3 * r + s) * C
            first_ref[r, s] = got_ref[at : at + C].astype(F32).T
            second_ref[r, s] = got_ref[at + 9 * C : at + 10 * C].astype(F32).T
    embed_ref[...] = got_ref[18 * C : 18 * C + 24].astype(F32)


def unpack(got, values):
    vmem = pl.BlockSpec(memory_space=pltpu.VMEM)
    return pl.pallas_call(
        unpack_kernel,
        in_specs=[vmem],
        out_specs=[vmem] * 3,
        out_shape=[
            jax.ShapeDtypeStruct((values, C), F32),
            jax.ShapeDtypeStruct((3, 3, C, C), F32),
            jax.ShapeDtypeStruct((3, 3, C, C), F32),
        ],
        name="unpack",
    )(got)


def exchange(bands, sectors, left, right, v1, v2, c1l, c1r, c2l, c2r):
    half = sectors // 2
    number = lambda a, b: a * sectors + b % sectors

    def above(a, b):
        return number(a - 1, b) if a > 0 else number(0, b + half)

    def below(a, b):
        return number(a + 1, b) if a < bands - 1 else number(a, b + half)

    def source(kind, a, b):
        b = b % sectors
        return above(a, b) if (b < half) == (kind == 1) else below(a, b)

    def perm(of):
        return [(of(a, b), number(a, b)) for a in range(bands) for b in range(sectors)]

    move = lambda x, of: lax.ppermute(x, ALL, perm(of))
    return (
        move(right, lambda a, b: number(a, b - 1)),
        move(left, lambda a, b: number(a, b + 1)),
        move(v1, lambda a, b: source(1, a, b)),
        move(v2, lambda a, b: source(2, a, b)),
        move(c1l, lambda a, b: source(1, a, b - 1)),
        move(c1r, lambda a, b: source(1, a, b + 1)),
        move(c2l, lambda a, b: source(2, a, b - 1)),
        move(c2r, lambda a, b: source(2, a, b + 1)),
    )


def per_device(obs_values, tile_ids, obs_rows, obs_cols, w_embed, w_first, w_second, cotangent):
    bands, sectors = lax.axis_size("lat"), lax.axis_size("lon")
    owners = bands * sectors
    count, values = obs_values.shape
    where = jnp.stack(
        [lax.axis_index("lat"), lax.axis_index("lon"), jnp.int32(bands), jnp.int32(sectors)]
    ).astype(jnp.int32)
    cot_edges = edges(where, cotangent)
    cot_halo = exchange(bands, sectors, *cot_edges)

    packed = pack(tile_ids.T, obs_rows.reshape(1, count), obs_cols.reshape(1, count), obs_values.T)
    got = lax.all_to_all(packed, ALL, 0, 0, tiled=True)
    hg, cot_t = cot_back(where, cotangent, cot_halo, w_second)

    s, *s_edges = setconv(where, got)
    s_halo = exchange(bands, sectors, *s_edges)
    padded = jnp.concatenate([w_embed, jnp.zeros((FEAT - values, C), BF16)], axis=0)
    wide = jnp.kron(jnp.eye(4, dtype=BF16), padded)
    field, red = main(where, s, s_halo, wide, w_first, w_second, hg, cot_t, owners)

    parts = lax.all_to_all(red.reshape(owners, RED, C), ALL, 0, 0, tiled=True)
    summed = jnp.sum(parts.astype(F32), axis=0).astype(BF16)
    spread = jnp.broadcast_to(summed[None], (owners, RED, C))
    whole = lax.all_to_all(spread, ALL, 0, 0, tiled=True)
    grad_embed, grad_first, grad_second = unpack(whole.reshape(owners * RED, C), values)
    return (field, grad_embed, grad_first, grad_second)


def solution(mesh):
    in_specs = (
        P(ALL, None),
        P(ALL, None),
        P(ALL),
        P(ALL),
        P(),
        P(),
        P(),
        P("lat", "lon", None),
    )
    out_specs = (P("lat", "lon", None), P(), P(), P())
    return jax.shard_map(
        per_device, mesh=mesh, in_specs=in_specs, out_specs=out_specs, check_vma=False
    )
```

time: 472 us -> 168 us (0.36); the launches traced: 464 us -> 167 us
  local copies, waits for them, and re-layouts: 136 us -> 4.04 us
  waiting for transfers between devices: 94.6 us -> 6.83 us
  Pallas kernels: 0 us -> 70.3 us
  matrix products: 49.2 us -> 0 us
  starting transfers between devices: 67.9 us -> 36.9 us
  other arithmetic: 29.3 us -> 0.9 us
  blocking collectives: 71 us -> 47.6 us
  between operations: 15.5 us -> 0.79 us
    psum x1 -> x0, waiting for transfers between devices: 75.8 us -> none  [per_device(): lax.psum((grad_embed, grad_first, grad_second), ('lat', 'lon'))]
    psum x1 -> x0, blocking collectives: 71 us -> none  [per_device(): lax.psum((grad_embed, grad_first, grad_second), ('lat', 'lon'))]
    pallas_call x0 -> x6, Pallas kernels: none -> 70.3 us  [the longest x1 31.1 us: pack(): pl.pallas_call(pack_kernel, grid=(steps,), in_specs=[whole(ids), whole(ro...]
    scatter-add x26 -> x0, local copies, waits for them, and re-layouts: 52.4 us -> none  [the longest x14 49.4 us: spread_back(): summed.at[row_off:row_off + tile_rows, col_off:col_off + tile_cols]]
    dot_general x60 -> x0, matrix products: 49.2 us -> none  [the longest x18 17.8 us: spread_back(): lax.dot_general(flat_up, weight[row_off, col_off], (((1,), (1,)), ((), ()...]
    scatter x2 -> x0, local copies, waits for them, and re-layouts: 48.4 us -> none  [the longest x1 24.6 us: per_device(): where_buffer = jnp.zeros((2, slot_total), jnp.float32).at[:, slot_index]....]
    all_to_all x0 -> x2, blocking collectives: none -> 47.6 us  [the longest x1 26.9 us: per_device(): parts = lax.all_to_all(red.reshape(owners, RED, C), ALL, 0, 0, tiled=True)]
    ppermute x20 -> x16, starting transfers between devices: 41.3 us -> 25.4 us  [exchange(): move = lambda x, of: lax.ppermute(x, ALL, perm(of))]
  transfers between devices with their start and end apart: 23 -> 17, of which waited for: 6 -> 2; matrix products, arithmetic and copies ran while one was open for 26% -> 0% of each run, Pallas kernels for 0% -> 11%
where the time goes in v1:
time: 168 us; the launch traced here: 167 us
  Pallas kernels  70.3 us (42%)
  blocking collectives  47.6 us (28%)
  starting transfers between devices  36.9 us (22%)
  waiting for transfers between devices  6.83 us (4%)
  local copies, waits for them, and re-layouts  4.04 us (2%)
    pallas_call x1, Pallas kernels, pack(): pl.pallas_call(pack_kernel, grid=(steps,), in_specs=[whole(ids), whole(ro...  31.1 us
    all_to_all x1, blocking collectives, per_device(): parts = lax.all_to_all(red.reshape(owners, RED, C), ALL, 0, 0, tiled=True)  26.9 us
    ppermute x16, starting transfers between devices, exchange(): move = lambda x, of: lax.ppermute(x, ALL, perm(of))  25.4 us
    all_to_all x1, blocking collectives, per_device(): whole = lax.all_to_all(spread, ALL, 0, 0, tiled=True)  20.7 us
    pallas_call x1, Pallas kernels, main(): pl.pallas_call(main_kernel, in_specs=[pl.BlockSpec(memory_space=pltpu.SME...  18.8 us
    all_to_all x1, starting transfers between devices, per_device(): got = lax.all_to_all(packed, ALL, 0, 0, tiled=True)  11.5 us
    pallas_call x1, Pallas kernels, setconv(): pl.pallas_call(setconv_kernel, grid=(steps,), in_specs=[pl.BlockSpec(memo...  9.26 us
    pallas_call x1, Pallas kernels, cot_back(): pl.pallas_call(cot_kernel, in_specs=[pl.BlockSpec(memory_space=pltpu.SMEM...  6.98 us
  transfers between devices with their start and end apart: 17, of which 2 were waited for; matrix products, arithmetic and copies ran while one was open for 0% of the time, Pallas kernels for 11%

profile of v1, /device:TPU:1, one launch (start us, length us, event | category | flops | bytes accessed | tf_op | source)
XLA Modules:
  0.0 167.4 jit_solution(1601041008617762604)
XLA Ops:
  0.6 0.0 copy-start.3
  0.6 1.0 copy-done.3
  1.6 0.0 copy-start.6
  1.6 0.8 copy-done.6
  2.4 0.0 copy-start.7
  2.4 0.8 copy-done.7
  3.1 0.0 copy-start.8
  3.1 0.8 copy-done.8
  3.9 31.1 %pack.1 = bf16[128,32,128]{2,1,0:T(8,128)(2,1)} custom-call(s32[1,8192]{1,0:T(1,128)S(1)} %bitcast.16, f32[1,8192]{1,0:T(1,128)S(1)} %bitcast.17, f32[1,8192]{1,0:T(1,128)S(1)} %bitcast.18, bf16[24,8192]{1,0:T(8,128)(2,1)S(1)} %bitcast.15), custom_call_target="tpu_custom_call" | custom-call | flops 8589934592 | bytes 3145728 | tf_op jit(solution)/shard_map/pack/pallas_call | solution.py:97
  35.0 11.5 %all-to-all-start = ((bf16[128,32,128]{2,1,0:T(8,128)(2,1)}), bf16[128,32,128]{2,1,0:T(8,128)(2,1)S(1)}, u32[]{:S(2)}, u32[]{:S(2)}) async-start(bf16[128,32,128]{2,1,0:T(8,128)(2,1)} %pack.1), calls=%async_computation | async-start | bytes 2097152 | tf_op jit(solution)/shard_map/all_to_all | solution.py:592
  46.5 0.6 pad_add_fusion.where_ref
  47.1 1.8 %edges.1 = (bf16[16,16,128]{2,1,0:T(8,128)(2,1)}, bf16[16,16,128]{2,1,0:T(8,128)(2,1)}, bf16[2,128,128]{2,1,0:T(8,128)(2,1)}, bf16[2,128,128]{2,1,0:T(8,128)(2,1...) custom-call(s32[4]{0:T(128)} %pad_add_fusion.where_ref, ...), custom_call_target="tpu_custom_call" | custom-call | bytes 1048576 | tf_op jit(solution)/shard_map/edges/pallas_call | solution.py:249
  48.9 2.9 %collective-permute-start.12 = (bf16[2,16,128]{2,1,0:T(8,128)(2,1)}, bf16[2,16,128]{2,1,0:T(8,128)(2,1)S(1)}, u32[]{:S(2)}, u32[]{:S(2)}) collective-permute-start(bf16[2,16,128]{2,1,0:T(8,128)(2,1)} %get-tuple-element.41), channel_id=1, source_target_pairs={{31,0},{8,1},{9,2},{10,3},{11,4},{12,5},{13,6},{14,7},{15,8},{24,9... | collective-permute-start | bytes 24584 | tf_op jit(solution)/shard_map/ppermute | solution.py:568
  51.8 1.6 collective-permute-start.13
  53.4 2.6 %collective-permute-start.14 = (bf16[2,16,128]{2,1,0:T(8,128)(2,1)}, bf16[2,16,128]{2,1,0:T(8,128)(2,1)S(1)}, u32[]{:S(2)}, u32[]{:S(2)}) collective-permute-start(bf16[2,16,128]{2,1,0:T(8,128)(2,1)} %get-tuple-element.43), channel_id=1, source_target_pairs={{7,0},{16,1},{17,2},{18,3},{19,4},{20,5},{21,6},{22,7},{23,8},{0,9... | collective-permute-start | bytes 24584 | tf_op jit(solution)/shard_map/ppermute | solution.py:568
  56.0 0.0 collective-permute-start.15
  56.0 1.7 %collective-permute-start.8 = (bf16[16,16,128]{2,1,0:T(8,128)(2,1)}, bf16[16,16,128]{2,1,0:T(8,128)(2,1)S(1)}, u32[]{:S(2)}, u32[]{:S(2)}) collective-permute-start(bf16[16,16,128]{2,1,0:T(8,128)(2,1)} %get-tuple-element.37), channel_id=1, source_target_pairs={{15,0},{0,1},{1,2},{2,3},{3,4},{4,5},{5,6},{6,7},{7,8},{8,9},{9,10... | collective-permute-start | bytes 196616 | tf_op jit(solution)/shard_map/ppermute | solution.py:568
  57.7 0.0 copy-done.9
  57.7 3.8 %collective-permute-done.12.c1l_ref = bf16[2,16,128]{2,1,0:T(8,128)(2,1)S(1)} collective-permute-done((bf16[2,16,128]{2,1,0:T(8,128)(2,1)}, bf16[2,16,128]{2,1,0:T(8,128)(2,1)S(1)}, u32[]{:S(2)}, u32[]{:S(2)}) %collective-permute-start.12) | collective-permute-done | bytes 8224 | tf_op jit(solution)/shard_map/ppermute | solution.py:568
  61.5 0.0 copy-start
  61.5 1.4 collective-permute-start.9
  62.9 3.0 %all-to-all-done.got_ref = bf16[128,32,128]{2,1,0:T(8,128)(2,1)S(1)} async-done(((bf16[128,32,128]{2,1,0:T(8,128)(2,1)}), bf16[128,32,128]{2,1,0:T(8,128)(2,1)S(1)}, u32[]{:S(2)}, u32[]{:S(2)}) %all-to-all-start) | async-done | bytes 1048608 | tf_op jit(solution)/shard_map/all_to_all | solution.py:592
  65.9 0.0 copy-start.1
  65.9 0.6 copy-done.1
  66.5 9.3 %setconv.1 = (bf16[128,512]{1,0:T(8,128)(2,1)S(1)}, bf16[16,512]{1,0:T(8,128)(2,1)S(1)}, bf16[16,512]{1,0:T(8,128)(2,1)S(1)}, bf16[128,128]{1,0:T(8,128)(2,1)S(1...) custom-call(s32[4]{0:T(128)S(1)} %copy-done.1, ...), custom_call_target="tpu_custom_call" | custom-call | flops 4294967296 | bytes 2097152 | tf_op jit(solution)/shard_map/setconv/pallas_call | solution.py:161
  75.8 0.0 collective-permute-done.13.c1r_ref
  75.8 0.0 copy-done.11
  75.8 0.5 collective-permute-start.10
  76.2 0.0 collective-permute-done.14.c2l_ref
  76.2 0.0 copy-done.10
  76.2 2.6 %collective-permute-start.11 = (bf16[2,128,128]{2,1,0:T(8,128)(2,1)S(1)}, bf16[2,128,128]{2,1,0:T(8,128)(2,1)S(1)}, u32[]{:S(2)}, u32[]{:S(2)}) collective-permute-start(bf16[2,128,128]{2,1,0:T(8,128)(2,1)S(1)} %copy-done.10), channel_id=1, source_target_pairs={{16,0},{17,1},{18,2},{19,3},{20,4},{21,5},{22,6},{23,7},{0,8},{1,9... | collective-permute-start | bytes 196616 | tf_op jit(solution)/shard_map/ppermute | solution.py:568
  78.8 0.0 collective-permute-done.15.c2r_ref
  78.8 1.3 collective-permute-start.4
  80.2 0.0 collective-permute-done.8.left_ref
  80.2 3.1 %collective-permute-start.5 = (bf16[16,128]{1,0:T(8,128)(2,1)S(1)}, bf16[16,128]{1,0:T(8,128)(2,1)S(1)}, u32[]{:S(2)}, u32[]{:S(2)}) collective-permute-start(bf16[16,128]{1,0:T(8,128)(2,1)S(1)} %get-tuple-element.34), channel_id=1, source_target_pairs={{9,0},{10,1},{11,2},{12,3},{13,4},{14,5},{15,6},{24,7},{25,8},{26,... | collective-permute-start | bytes 12296 | tf_op jit(solution)/shard_map/ppermute | solution.py:568
  83.3 0.0 collective-permute-done.9.right_ref
  83.3 1.0 collective-permute-start.6
  84.3 0.1 broadcast_multiply_fusion
  84.5 0.0 collective-permute-done.10.v1_ref
  84.5 1.1 collective-permute-start.7
  85.6 0.0 collective-permute-done.11.v2_ref
  85.6 2.6 %collective-permute-start = (bf16[16,512]{1,0:T(8,128)(2,1)S(1)}, bf16[16,512]{1,0:T(8,128)(2,1)S(1)}, u32[]{:S(2)}, u32[]{:S(2)}) collective-permute-start(bf16[16,512]{1,0:T(8,128)(2,1)S(1)} %get-tuple-element.29), channel_id=1, source_target_pairs={{15,0},{0,1},{1,2},{2,3},{3,4},{4,5},{5,6},{6,7},{7,8},{8,9},{9,10... | collective-permute-start | bytes 49160 | tf_op jit(solution)/shard_map/ppermute | solution.py:568
  88.2 0.0 collective-permute-done.4.c1l_ref
  88.2 0.0 collective-permute-start.1
  88.2 0.0 collective-permute-done.5.c1r_ref
  88.2 1.9 %collective-permute-start.2 = (bf16[128,128]{1,0:T(8,128)(2,1)S(1)}, bf16[128,128]{1,0:T(8,128)(2,1)S(1)}, u32[]{:S(2)}, u32[]{:S(2)}) collective-permute-start(bf16[128,128]{1,0:T(8,128)(2,1)S(1)} %get-tuple-element.31), channel_id=1, source_target_pairs={{8,0},{9,1},{10,2},{11,3},{12,4},{13,5},{14,6},{15,7},{24,8},{25,9... | collective-permute-start | bytes 98312 | tf_op jit(solution)/shard_map/ppermute | solution.py:568
  90.2 0.0 collective-permute-done.6.c2l_ref
  90.2 1.1 collective-permute-start.3
  91.3 0.0 copy-done
  91.3 0.0 copy-done.5
  91.3 7.0 %cot_back.1 = (f32[3040,128]{1,0:T(8,128)S(1)}, bf16[128,2304]{1,0:T(8,128)(2,1)S(1)}) custom-call(s32[4]{0:T(128)S(1)} %copy-done.1, bf16[16,128,128]{2,1,0:T(8,128)(2,1)S(1)} %copy-done, bf16[16,16,128]{2,1,0:T(8,128)(2,1)S(1)} %collective-permute-done.8.left_ref, bf16[16,16,128]{2,1,0:T(8,128)(2,1)S(1)} %collective-permute-done.9.right_ref, ...), custom_call_target="tpu_custom_call" | custom-call | flops 1613758464 | bytes 4194304 | tf_op jit(solution)/shard_map/cot_back/pallas_call | solution.py:323
  98.3 0.0 collective-permute-done.7.c2r_ref
  98.3 0.0 collective-permute-done.left_ref
  98.3 0.0 collective-permute-done.1.right_ref
  98.3 0.0 collective-permute-done.2.v1_ref
  98.3 0.0 collective-permute-done.3.v2_ref
  98.3 0.0 copy-done.2
  98.3 0.0 copy-done.4
  98.3 18.8 %main.1 = (bf16[16,128,128]{2,1,0:T(8,128)(2,1)}, bf16[3072,128]{1,0:T(8,128)(2,1)S(1)}) custom-call(s32[4]{0:T(128)S(1)} %copy-done.2, bf16[128,512]{1,0:T(8,128)(2,1)S(1)} %get-tuple-element.28.s_ref, bf16[16,512]{1,0:T(8,128)(2,1)S(1)} %collective-permute-done.left_ref, bf16[16,512]{1,0:T(8,128)(2,1)S(1)} %collective-permute-done.1.right_ref, ...), custom_call_target="tpu_custom_call" | custom-call | flops 8589934592 | bytes 6291456 | tf_op jit(solution)/shard_map/main/pallas_call | solution.py:491
  117.2 26.9 %all_to_all.15 = bf16[128,24,128]{2,1,0:T(8,128)(2,1)S(1)} all-to-all(bf16[128,24,128]{2,1,0:T(8,128)(2,1)S(1)} %bitcast.13), channel_id=1, replica_groups=mesh['lat'=8,'lon'=16] {'lat','lon'}, dimensions={0} | all-to-all | bytes 1572864 | tf_op jit(solution)/shard_map/all_to_all | solution.py:601
  144.1 0.2 reduce_sum.12
  144.2 0.1 broadcast_in_dim.6
  144.3 20.7 %all_to_all.16 = bf16[128,24,128]{2,1,0:T(8,128)(2,1)} all-to-all(bf16[128,24,128]{2,1,0:T(8,128)(2,1)S(1)} %broadcast_in_dim.6), channel_id=1, replica_groups=mesh['lat'=8,'lon'=16] {'lat','lon'}, dimensions={0} | all-to-all | bytes 1572864 | tf_op jit(solution)/shard_map/all_to_all | solution.py:604
  165.1 2.4 %unpack.1 = (f32[24,128]{1,0:T(8,128)}, f32[3,3,128,128]{3,2,1,0:T(8,128)}, f32[3,3,128,128]{3,2,1,0:T(8,128)}) custom-call(bf16[3072,128]{1,0:T(8,128)(2,1)} %bitcast.19), custom_call_target="tpu_custom_call" | custom-call | tf_op jit(solution)/shard_map/unpack/pallas_call | solution.py:538
  (9 shorter events, 0.0 us)
Async XLA Ops:
  0.6 1.0 copy-start.3
  1.6 0.8 copy-start.6
  2.4 0.8 copy-start.7
  3.1 0.8 copy-start.8
  35.0 22.7 %copy-start.9 = (bf16[24,128]{1,0:T(8,128)(2,1)S(1)}, bf16[24,128]{1,0:T(8,128)(2,1)}, u32[]{:S(2)}) copy-start(bf16[24,128]{1,0:T(8,128)(2,1)} %param.12) | copy-start | bytes 18436
  35.0 30.8 %all-to-all-start = ((bf16[128,32,128]{2,1,0:T(8,128)(2,1)}), bf16[128,32,128]{2,1,0:T(8,128)(2,1)S(1)}, u32[]{:S(2)}, u32[]{:S(2)}) async-start(bf16[128,32,128]{2,1,0:T(8,128)(2,1)} %pack.1), calls=%async_computation | async-start | bytes 2097152 | tf_op jit(solution)/shard_map/all_to_all | solution.py:592
  48.9 12.6 %collective-permute-start.12 = (bf16[2,16,128]{2,1,0:T(8,128)(2,1)}, bf16[2,16,128]{2,1,0:T(8,128)(2,1)S(1)}, u32[]{:S(2)}, u32[]{:S(2)}) collective-permute-start(bf16[2,16,128]{2,1,0:T(8,128)(2,1)} %get-tuple-element.41), channel_id=1, source_target_pairs={{31,0},{8,1},{9,2},{10,3},{11,4},{12,5},{13,6},{14,7},{15,8},{24,9... | collective-permute-start | bytes 24584 | tf_op jit(solution)/shard_map/ppermute | solution.py:568
  51.8 24.0 %collective-permute-start.13 = (bf16[2,16,128]{2,1,0:T(8,128)(2,1)}, bf16[2,16,128]{2,1,0:T(8,128)(2,1)S(1)}, u32[]{:S(2)}, u32[]{:S(2)}) collective-permute-start(bf16[2,16,128]{2,1,0:T(8,128)(2,1)} %get-tuple-element.42), channel_id=1, source_target_pairs={{9,0},{10,1},{11,2},{12,3},{13,4},{14,5},{15,6},{24,7},{25,8},{26,... | collective-permute-start | bytes 24584 | tf_op jit(solution)/shard_map/ppermute | solution.py:568
  53.4 22.9 %collective-permute-start.14 = (bf16[2,16,128]{2,1,0:T(8,128)(2,1)}, bf16[2,16,128]{2,1,0:T(8,128)(2,1)S(1)}, u32[]{:S(2)}, u32[]{:S(2)}) collective-permute-start(bf16[2,16,128]{2,1,0:T(8,128)(2,1)} %get-tuple-element.43), channel_id=1, source_target_pairs={{7,0},{16,1},{17,2},{18,3},{19,4},{20,5},{21,6},{22,7},{23,8},{0,9... | collective-permute-start | bytes 24584 | tf_op jit(solution)/shard_map/ppermute | solution.py:568
  56.0 22.9 %collective-permute-start.15 = (bf16[2,16,128]{2,1,0:T(8,128)(2,1)}, bf16[2,16,128]{2,1,0:T(8,128)(2,1)S(1)}, u32[]{:S(2)}, u32[]{:S(2)}) collective-permute-start(bf16[2,16,128]{2,1,0:T(8,128)(2,1)} %get-tuple-element.44), channel_id=1, source_target_pairs={{17,0},{18,1},{19,2},{20,3},{21,4},{22,5},{23,6},{0,7},{1,8},{2,9}... | collective-permute-start | bytes 24584 | tf_op jit(solution)/shard_map/ppermute | solution.py:568
  56.0 24.2 %collective-permute-start.8 = (bf16[16,16,128]{2,1,0:T(8,128)(2,1)}, bf16[16,16,128]{2,1,0:T(8,128)(2,1)S(1)}, u32[]{:S(2)}, u32[]{:S(2)}) collective-permute-start(bf16[16,16,128]{2,1,0:T(8,128)(2,1)} %get-tuple-element.37), channel_id=1, source_target_pairs={{15,0},{0,1},{1,2},{2,3},{3,4},{4,5},{5,6},{6,7},{7,8},{8,9},{9,10... | collective-permute-start | bytes 196616 | tf_op jit(solution)/shard_map/ppermute | solution.py:568
  61.5 29.8 %copy-start = (bf16[16,128,128]{2,1,0:T(8,128)(2,1)S(1)}, bf16[16,128,128]{2,1,0:T(8,128)(2,1)}, u32[]{:S(2)}) copy-start(bf16[16,128,128]{2,1,0:T(8,128)(2,1)} %cot_ref.3) | copy-start | bytes 1572868
  61.5 21.8 %collective-permute-start.9 = (bf16[16,16,128]{2,1,0:T(8,128)(2,1)}, bf16[16,16,128]{2,1,0:T(8,128)(2,1)S(1)}, u32[]{:S(2)}, u32[]{:S(2)}) collective-permute-start(bf16[16,16,128]{2,1,0:T(8,128)(2,1)} %get-tuple-element.38), channel_id=1, source_target_pairs={{1,0},{2,1},{3,2},{4,3},{5,4},{6,5},{7,6},{8,7},{9,8},{10,9},{11,1... | collective-permute-start | bytes 196616 | tf_op jit(solution)/shard_map/ppermute | solution.py:568
  65.9 0.6 copy-start.1
  66.5 9.3 %copy-start.11 = (bf16[2,128,128]{2,1,0:T(8,128)(2,1)S(1)}, bf16[2,128,128]{2,1,0:T(8,128)(2,1)}, u32[]{:S(2)}) copy-start(bf16[2,128,128]{2,1,0:T(8,128)(2,1)} %get-tuple-element.39) | copy-start | bytes 196612
  66.5 9.8 %copy-start.10 = (bf16[2,128,128]{2,1,0:T(8,128)(2,1)S(1)}, bf16[2,128,128]{2,1,0:T(8,128)(2,1)}, u32[]{:S(2)}) copy-start(bf16[2,128,128]{2,1,0:T(8,128)(2,1)} %get-tuple-element.40) | copy-start | bytes 196612
  66.5 24.8 %copy-start.5 = (bf16[3,3,128,128]{3,2,1,0:T(8,128)(2,1)S(1)}, bf16[3,3,128,128]{3,2,1,0:T(8,128)(2,1)}, u32[]{:S(2)}) copy-start(bf16[3,3,128,128]{3,2,1,0:T(8,128)(2,1)} %w2_ref.1) | copy-start | bytes 884740
  75.8 8.7 %collective-permute-start.10 = (bf16[2,128,128]{2,1,0:T(8,128)(2,1)S(1)}, bf16[2,128,128]{2,1,0:T(8,128)(2,1)S(1)}, u32[]{:S(2)}, u32[]{:S(2)}) collective-permute-start(bf16[2,128,128]{2,1,0:T(8,128)(2,1)S(1)} %copy-done.11), channel_id=1, source_target_pairs={{8,0},{9,1},{10,2},{11,3},{12,4},{13,5},{14,6},{15,7},{24,8},{25,9... | collective-permute-start | bytes 196616 | tf_op jit(solution)/shard_map/ppermute | solution.py:568
  76.2 9.3 %collective-permute-start.11 = (bf16[2,128,128]{2,1,0:T(8,128)(2,1)S(1)}, bf16[2,128,128]{2,1,0:T(8,128)(2,1)S(1)}, u32[]{:S(2)}, u32[]{:S(2)}) collective-permute-start(bf16[2,128,128]{2,1,0:T(8,128)(2,1)S(1)} %copy-done.10), channel_id=1, source_target_pairs={{16,0},{17,1},{18,2},{19,3},{20,4},{21,5},{22,6},{23,7},{0,8},{1,9... | collective-permute-start | bytes 196616 | tf_op jit(solution)/shard_map/ppermute | solution.py:568
  78.8 9.4 %collective-permute-start.4 = (bf16[16,128]{1,0:T(8,128)(2,1)S(1)}, bf16[16,128]{1,0:T(8,128)(2,1)S(1)}, u32[]{:S(2)}, u32[]{:S(2)}) collective-permute-start(bf16[16,128]{1,0:T(8,128)(2,1)S(1)} %get-tuple-element.33), channel_id=1, source_target_pairs={{31,0},{8,1},{9,2},{10,3},{11,4},{12,5},{13,6},{14,7},{15,8},{24,9... | collective-permute-start | bytes 12296 | tf_op jit(solution)/shard_map/ppermute | solution.py:568
  80.2 8.1 %collective-permute-start.5 = (bf16[16,128]{1,0:T(8,128)(2,1)S(1)}, bf16[16,128]{1,0:T(8,128)(2,1)S(1)}, u32[]{:S(2)}, u32[]{:S(2)}) collective-permute-start(bf16[16,128]{1,0:T(8,128)(2,1)S(1)} %get-tuple-element.34), channel_id=1, source_target_pairs={{9,0},{10,1},{11,2},{12,3},{13,4},{14,5},{15,6},{24,7},{25,8},{26,... | collective-permute-start | bytes 12296 | tf_op jit(solution)/shard_map/ppermute | solution.py:568
  83.3 6.9 %collective-permute-start.6 = (bf16[16,128]{1,0:T(8,128)(2,1)S(1)}, bf16[16,128]{1,0:T(8,128)(2,1)S(1)}, u32[]{:S(2)}, u32[]{:S(2)}) collective-permute-start(bf16[16,128]{1,0:T(8,128)(2,1)S(1)} %get-tuple-element.35), channel_id=1, source_target_pairs={{7,0},{16,1},{17,2},{18,3},{19,4},{20,5},{21,6},{22,7},{23,8},{0,9... | collective-permute-start | bytes 12296 | tf_op jit(solution)/shard_map/ppermute | solution.py:568
  84.5 13.8 %collective-permute-start.7 = (bf16[16,128]{1,0:T(8,128)(2,1)S(1)}, bf16[16,128]{1,0:T(8,128)(2,1)S(1)}, u32[]{:S(2)}, u32[]{:S(2)}) collective-permute-start(bf16[16,128]{1,0:T(8,128)(2,1)S(1)} %get-tuple-element.36), channel_id=1, source_target_pairs={{17,0},{18,1},{19,2},{20,3},{21,4},{22,5},{23,6},{0,7},{1,8},{2,9}... | collective-permute-start | bytes 12296 | tf_op jit(solution)/shard_map/ppermute | solution.py:568
  85.6 12.7 %collective-permute-start = (bf16[16,512]{1,0:T(8,128)(2,1)S(1)}, bf16[16,512]{1,0:T(8,128)(2,1)S(1)}, u32[]{:S(2)}, u32[]{:S(2)}) collective-permute-start(bf16[16,512]{1,0:T(8,128)(2,1)S(1)} %get-tuple-element.29), channel_id=1, source_target_pairs={{15,0},{0,1},{1,2},{2,3},{3,4},{4,5},{5,6},{6,7},{7,8},{8,9},{9,10... | collective-permute-start | bytes 49160 | tf_op jit(solution)/shard_map/ppermute | solution.py:568
  88.2 10.1 %collective-permute-start.1 = (bf16[16,512]{1,0:T(8,128)(2,1)S(1)}, bf16[16,512]{1,0:T(8,128)(2,1)S(1)}, u32[]{:S(2)}, u32[]{:S(2)}) collective-permute-start(bf16[16,512]{1,0:T(8,128)(2,1)S(1)} %get-tuple-element.30), channel_id=1, source_target_pairs={{1,0},{2,1},{3,2},{4,3},{5,4},{6,5},{7,6},{8,7},{9,8},{10,9},{11,1... | collective-permute-start | bytes 49160 | tf_op jit(solution)/shard_map/ppermute | solution.py:568
  88.2 10.1 %collective-permute-start.2 = (bf16[128,128]{1,0:T(8,128)(2,1)S(1)}, bf16[128,128]{1,0:T(8,128)(2,1)S(1)}, u32[]{:S(2)}, u32[]{:S(2)}) collective-permute-start(bf16[128,128]{1,0:T(8,128)(2,1)S(1)} %get-tuple-element.31), channel_id=1, source_target_pairs={{8,0},{9,1},{10,2},{11,3},{12,4},{13,5},{14,6},{15,7},{24,8},{25,9... | collective-permute-start | bytes 98312 | tf_op jit(solution)/shard_map/ppermute | solution.py:568
  90.2 8.1 %copy-start.2 = (s32[4]{0:T(128)S(1)}, s32[4]{0:T(128)}, u32[]{:S(2)}) copy-start(s32[4]{0:T(128)} %pad_add_fusion.where_ref) | copy-start | bytes 52
  90.2 8.2 %copy-start.4 = (bf16[3,3,128,128]{3,2,1,0:T(8,128)(2,1)S(1)}, bf16[3,3,128,128]{3,2,1,0:T(8,128)(2,1)}, u32[]{:S(2)}) copy-start(bf16[3,3,128,128]{3,2,1,0:T(8,128)(2,1)} %w1_ref.1) | copy-start | bytes 884740
  90.2 8.1 %collective-permute-start.3 = (bf16[128,128]{1,0:T(8,128)(2,1)S(1)}, bf16[128,128]{1,0:T(8,128)(2,1)S(1)}, u32[]{:S(2)}, u32[]{:S(2)}) collective-permute-start(bf16[128,128]{1,0:T(8,128)(2,1)S(1)} %get-tuple-element.32), channel_id=1, source_target_pairs={{16,0},{17,1},{18,2},{19,3},{20,4},{21,5},{22,6},{23,7},{0,8},{1,9... | collective-permute-start | bytes 98312 | tf_op jit(solution)/shard_map/ppermute | solution.py:568

commit v2 on v1

--- a/solution.py
+++ b/solution.py
@@ -34,56 +34,68 @@
     return 16 + (i + 2) * PITCH
 
 
-def pack_kernel(ids_ref, rows_ref, cols_ref, vals_ref, out_ref, q_ref, v_ref, pair_ref, acc_ref):
+def pack_kernel(ids_hbm, rows_hbm, cols_hbm, vals_hbm, out_ref,
+                ids_ref, rows_ref, cols_ref, vals_ref, q_ref, v_ref, pair_ref, acc_ref, sems):
     step = pl.program_id(0)
     count = ids_ref.shape[1]
     owners = out_ref.shape[0] * pl.num_programs(0)
     sub = 256
-    part = 1024
+    part = 2048
     pairs = out_ref.shape[0] // 2
 
     @pl.when(step == 0)
     def _():
+        moves = [
+            pltpu.make_async_copy(a, b, sems.at[k])
+            for k, (a, b) in enumerate(
+                [(ids_hbm, ids_ref), (rows_hbm, rows_ref), (cols_hbm, cols_ref), (vals_hbm, vals_ref)]
+            )
+        ]
+        for move in moves:
+            move.start()
         owner = lax.broadcasted_iota(jnp.int32, (owners, sub), 0)
         slot = lax.broadcasted_iota(jnp.int32, (sub, sub), 0)
         upto = slot <= lax.broadcasted_iota(jnp.int32, (sub, sub), 1)
         upto = jnp.concatenate(
             [jnp.where(upto, 1.0, 0.0).astype(BF16), jnp.ones((sub, 128), BF16)], axis=1
         )
+        for move in moves:
+            move.wait()
 
         def body(k, carry):
-            at = pl.ds(pl.multiple_of(k * sub, sub), sub)
-            ids = ids_ref[:, at]
-            hot = owner == ids
-            counted = dot(jnp.where(hot, 1.0, 0.0).astype(BF16), upto)
-            before = counted[:, :sub] + jnp.concatenate([carry, carry], axis=1)
-            rank = jnp.sum(jnp.where(hot, before, 0.0), axis=0, keepdims=True) - 1.0
-            key = rank.astype(jnp.int32) + (ids & 1) * 128
-            q_ref[:, at] = jnp.where(slot == key, 1.0, 0.0).astype(BF16)
-            pair_ref[:, at] = jnp.broadcast_to((ids >> 1).astype(F32), (FEAT, sub)).astype(BF16)
-            rows, cols = rows_ref[:, at], cols_ref[:, at]
-            rows_hi, cols_hi = rows.astype(BF16).astype(F32), cols.astype(BF16).astype(F32)
-            tail = jnp.concatenate(
-                [rows_hi, rows - rows_hi, cols_hi, cols - cols_hi, jnp.zeros((4, sub), F32)], axis=0
-            )
-            v_ref[:, at] = jnp.concatenate([vals_ref[:, at].astype(F32), tail], axis=0).astype(BF16)
-            return carry + counted[:, sub:]
-
-        lax.fori_loop(0, count // sub, body, jnp.zeros((owners, 128), F32))
-
-    acc_ref[...] = jnp.zeros_like(acc_ref)
-
-    def body(k, carry):
-        at = pl.ds(pl.multiple_of(k * part, part), part)
-        base = jnp.full((FEAT, part), (step * pairs).astype(F32), F32).astype(BF16)
+            for u in range(4):
+                at = pl.ds(pl.multiple_of(k * 4 * sub + u * sub, sub), sub)
+                ids = ids_ref[:, at]
+                hot = owner == ids
+                counted = dot(jnp.where(hot, 1.0, 0.0).astype(BF16), upto)
+                before = counted[:, :sub] + jnp.concatenate([carry, carry], axis=1)
+                rank = jnp.sum(jnp.where(hot, before, 0.0), axis=0, keepdims=True) - 1.0
+                key = rank.astype(jnp.int32) + (ids & 1) * 128
+                q_ref[:, at] = jnp.where(slot == key, 1.0, 0.0).astype(BF16)
+                pair_ref[:, at] = jnp.broadcast_to((ids >> 1).astype(F32), (FEAT, sub)).astype(BF16)
+                rows, cols = rows_ref[:, at], cols_ref[:, at]
+                rows_hi, cols_hi = rows.astype(BF16).astype(F32), cols.astype(BF16).astype(F32)
+                tail = jnp.concatenate(
+                    [rows_hi, rows - rows_hi, cols_hi, cols - cols_hi, jnp.zeros((4, sub), F32)], axis=0
+                )
+                v_ref[:, at] = jnp.concatenate([vals_ref[:, at].astype(F32), tail], axis=0).astype(BF16)
+                carry = carry + counted[:, sub:]
+            return carry
+
+        lax.fori_loop(0, count // sub // 4, body, jnp.zeros((owners, 128), F32))
+
+    base = jnp.full((FEAT, part), (step * pairs).astype(F32), F32).astype(BF16)
+    for k in range(count // part):
+        at = pl.ds(k * part, part)
         pair = pair_ref[:, at] - base
         values = v_ref[:, at]
         none = jnp.zeros_like(values)
         left = jnp.concatenate([jnp.where(pair == p, values, none) for p in range(pairs)], axis=0)
-        acc_ref[...] += dot_nt(left, q_ref[:, at])
-        return carry
-
-    lax.fori_loop(0, count // part, body, 0)
+        term = dot_nt(left, q_ref[:, at])
+        if k == 0:
+            acc_ref[...] = term
+        else:
+            acc_ref[...] += term
     for p in range(pairs):
         out_ref[2 * p] = acc_ref[p * FEAT : (p + 1) * FEAT, :128].astype(BF16)
         out_ref[2 * p + 1] = acc_ref[p * FEAT : (p + 1) * FEAT, 128:].astype(BF16)
@@ -92,28 +104,31 @@
 def pack(ids, rows, cols, values):
     count = ids.shape[1]
     owners = 128
-    steps = 8
-    whole = lambda a: pl.BlockSpec(a.shape, lambda i: (0, 0))
+    steps = 4
     return pl.pallas_call(
         pack_kernel,
         grid=(steps,),
-        in_specs=[whole(ids), whole(rows), whole(cols), whole(values)],
+        in_specs=[pl.BlockSpec(memory_space=pl.ANY)] * 4,
         out_specs=pl.BlockSpec((owners // steps, FEAT, 128), lambda i: (i, 0, 0)),
         out_shape=jax.ShapeDtypeStruct((owners, FEAT, 128), BF16),
         scratch_shapes=[
+            pltpu.VMEM(ids.shape, ids.dtype),
+            pltpu.VMEM(rows.shape, rows.dtype),
+            pltpu.VMEM(cols.shape, cols.dtype),
+            pltpu.VMEM(values.shape, values.dtype),
             pltpu.VMEM((256, count), BF16),
             pltpu.VMEM((FEAT, count), BF16),
             pltpu.VMEM((FEAT, count), BF16),
             pltpu.VMEM((owners // steps // 2 * FEAT, 256), F32),
+            pltpu.SemaphoreType.DMA((4,)),
         ],
-        compiler_params=pltpu.CompilerParams(vmem_limit_bytes=32 << 20),
+        compiler_params=pltpu.CompilerParams(vmem_limit_bytes=56 << 20),
         cost_estimate=pl.CostEstimate(flops=2 * 2048 * 256 * 8192, bytes_accessed=3 << 20, transcendentals=0),
         name="pack",
     )(ids, rows, cols, values)
 
 
-def setconv_kernel(where_ref, got_ref, s_ref, left_ref, right_ref, v1_ref, v2_ref,
-                   c1l_ref, c1r_ref, c2l_ref, c2r_ref, acc_ref):
+def setconv_kernel(where_ref, got_ref, s_ref, a_ref, b_ref, c_ref, d_ref, acc_ref):
     step = pl.program_id(0)
     x = jnp.concatenate([got_ref[k] for k in range(got_ref.shape[0])], axis=1).astype(F32)
     n = x.shape[1]
@@ -124,8 +139,9 @@
     col_mid = (lax.broadcasted_iota(jnp.int32, (TC, n), 0).astype(F32) + 0.5) * alpha
     row_weight = jnp.exp2(-jnp.square(row - row_mid))
     col_weight = jnp.exp2(-jnp.square(col - col_mid)).astype(BF16)
-    weighted = jnp.concatenate([(x * row_weight[i : i + 1]).astype(BF16) for i in range(TR)], axis=0)
-    term = dot_nt(col_weight, weighted)
+    values = x[:24]
+    weighted = jnp.concatenate([values * row_weight[i : i + 1] for i in range(TR)], axis=0).astype(BF16)
+    term = dot_nt(weighted, col_weight)
 
     @pl.when(step == 0)
     def _():
@@ -137,27 +153,26 @@
 
     @pl.when(step == pl.num_programs(0) - 1)
     def _():
-        s = acc_ref[...].astype(BF16)
-        s_ref[...] = s
-        left_ref[...] = s[:16]
-        right_ref[...] = s[TC - 16 :]
-        low = where_ref[1] < where_ref[3] // 2
-        top, bottom = s[:, :128], s[:, -128:]
-        v1 = jnp.where(low, bottom, top)
-        v2 = jnp.where(low, top, bottom)
-        v1_ref[...] = v1
-        v2_ref[...] = v2
-        c1l_ref[...] = v1[TC - 16 :]
-        c1r_ref[...] = v1[:16]
-        c2l_ref[...] = v2[TC - 16 :]
-        c2r_ref[...] = v2[:16]
+        none = jnp.zeros((FEAT - 24, TC), F32)
+        for g in range(TR // 4):
+            rows = []
+            for i in range(4 * g, 4 * g + 4):
+                rows += [acc_ref[24 * i : 24 * i + 24], none]
+            s_ref[:, g * 128 : (g + 1) * 128] = jnp.concatenate(rows, axis=0).T.astype(BF16)
+        left, right = s_ref[:16], s_ref[TC - 16 :]
+        top, bottom = s_ref[:, :128], s_ref[:, -128:]
+        even_lon, even_lat = evens(where_ref)
+        a_ref[...] = jnp.where(even_lon, right, left)
+        b_ref[...] = jnp.where(even_lon, left, right)
+        c_ref[...] = jnp.where(even_lat, bottom, top)
+        d_ref[...] = jnp.where(even_lat, top, bottom)
 
 
 def setconv(where, got):
-    steps = 16
+    steps = 8
     fixed = lambda *shape: pl.BlockSpec(shape, lambda i: (0,) * len(shape))
     lanes = TR * FEAT
-    shapes = [(TC, lanes), (16, lanes), (16, lanes), (TC, 128), (TC, 128)] + [(16, 128)] * 4
+    shapes = [(TC, lanes), (16, lanes), (16, lanes), (TC, 128), (TC, 128)]
     return pl.pallas_call(
         setconv_kernel,
         grid=(steps,),
@@ -167,38 +182,73 @@
         ],
         out_specs=[fixed(*s) for s in shapes],
         out_shape=[jax.ShapeDtypeStruct(s, BF16) for s in shapes],
-        scratch_shapes=[pltpu.VMEM((TC, lanes), F32)],
+        scratch_shapes=[pltpu.VMEM((TR * 24, TC), F32)],
         compiler_params=pltpu.CompilerParams(vmem_limit_bytes=32 << 20),
         cost_estimate=pl.CostEstimate(
-            flops=2 * 512 * 256 * 16384, bytes_accessed=2 << 20, transcendentals=144 * 16384
+            flops=2 * 384 * 256 * 16384, bytes_accessed=2 << 20, transcendentals=144 * 16384
         ),
         name="setconv",
     )(where, got)
+
+
+def join_kernel(where_ref, a_ref, b_ref, c_ref, d_ref, c_out, d_out):
+    even_lon, even_lat = evens(where_ref)
+    right = jnp.where(even_lon, a_ref[...], b_ref[...])
+    left = jnp.where(even_lon, b_ref[...], a_ref[...])
+    left_c = jnp.where(even_lat, left[:, -128:], left[:, :128])
+    left_d = jnp.where(even_lat, left[:, :128], left[:, -128:])
+    right_c = jnp.where(even_lat, right[:, -128:], right[:, :128])
+    right_d = jnp.where(even_lat, right[:, :128], right[:, -128:])
+    c_out[:16], c_out[16 : 16 + TC], c_out[16 + TC :] = left_c, c_ref[...], right_c
+    d_out[:16], d_out[16 : 16 + TC], d_out[16 + TC :] = left_d, d_ref[...], right_d
+
+
+def join_cot_kernel(where_ref, a_ref, b_ref, c_ref, d_ref, c_out, d_out):
+    even_lon, even_lat = evens(where_ref)
+    right = jnp.where(even_lon, a_ref[...], b_ref[...])
+    left = jnp.where(even_lon, b_ref[...], a_ref[...])
+    left_c = jnp.where(even_lat, left[-2:], left[:2])
+    left_d = jnp.where(even_lat, left[:2], left[-2:])
+    right_c = jnp.where(even_lat, right[-2:], right[:2])
+    right_d = jnp.where(even_lat, right[:2], right[-2:])
+    c_out[:, :16], c_out[:, 16 : 16 + TC], c_out[:, 16 + TC :] = left_c, c_ref[...], right_c
+    d_out[:, :16], d_out[:, 16 : 16 + TC], d_out[:, 16 + TC :] = left_d, d_ref[...], right_d
+
+
+def join(kernel, where, a, b, c, d, shape, name):
+    vmem = pl.BlockSpec(memory_space=pltpu.VMEM)
+    return pl.pallas_call(
+        kernel,
+        in_specs=[pl.BlockSpec(memory_space=pltpu.SMEM)] + [vmem] * 4,
+        out_specs=[vmem] * 2,
+        out_shape=[jax.ShapeDtypeStruct(shape, BF16)] * 2,
+        cost_estimate=pl.CostEstimate(flops=0, bytes_accessed=1 << 18, transcendentals=0),
+        name=name,
+    )(where, a, b, c, d)
 
 
 def shifted_copies(flat_ref, out_ref, begin, parts):
     def body(k, carry):
         at = pl.multiple_of(begin + k * PART, 16)
         for s in range(3):
-            piece = flat_ref[pl.ds(at, PART + 16), :]
-            out_ref[pl.ds(at, PART), s * C : (s + 1) * C] = piece[7 + s : 7 + s + PART].astype(BF16)
+            out_ref[pl.ds(at, PART), s * C : (s + 1) * C] = flat_ref[pl.ds(at + 7 + s, PART), :].astype(BF16)
         return carry
 
     lax.fori_loop(0, parts, body, 0)
 
 
+def three_rows(src_ref, at, rows):
+    return jnp.concatenate(
+        [src_ref[pl.ds(at + (r - 1) * PITCH, rows), :] for r in range(3)], axis=1
+    )
+
+
 def conv_rows(src_ref, at, rows, weights):
-    total = dot(src_ref[pl.ds(at - PITCH, rows), :], weights[0])
-    total += dot(src_ref[pl.ds(at, rows), :], weights[1])
-    total += dot(src_ref[pl.ds(at + PITCH, rows), :], weights[2])
-    return total
+    return dot(three_rows(src_ref, at, rows), jnp.concatenate(weights, axis=0))
 
 
 def back_rows(src_ref, at, rows, weights):
-    total = dot_nt(src_ref[pl.ds(at - PITCH, rows), :], weights[0])
-    total += dot_nt(src_ref[pl.ds(at, rows), :], weights[1])
-    total += dot_nt(src_ref[pl.ds(at + PITCH, rows), :], weights[2])
-    return total
+    return dot_nt(three_rows(src_ref, at, rows), jnp.concatenate(weights, axis=1))
 
 
 def fill_flat(flat_ref, centre, left, right):
@@ -214,13 +264,8 @@
     flat_ref[end:] = jnp.zeros((flat_ref.shape[0] - end, C), F32)
 
 
-def sides(where_ref):
-    lon, lon_size = where_ref[1], where_ref[3]
-    half = lon_size // 2
-    own = lon < half
-    left = jnp.where(lon == 0, lon_size - 1, lon - 1) < half
-    right = jnp.where(lon == lon_size - 1, 0, lon + 1) < half
-    return own, left, right
+def evens(where_ref):
+    return where_ref[1] % 2 == 0, where_ref[0] % 2 == 0
 
 
 def arrange_back(w_ref, out_ref):
@@ -229,23 +274,18 @@
             out_ref[r, :, s * C : (s + 1) * C] = w_ref[2 - r, 2 - s]
 
 
-def edges_kernel(where_ref, cot_ref, left_ref, right_ref, v1_ref, v2_ref, c1l_ref, c1r_ref, c2l_ref, c2r_ref):
-    low, _, _ = sides(where_ref)
-    left_ref[...] = cot_ref[:, :16, :]
-    right_ref[...] = cot_ref[:, TC - 16 :, :]
+def edges_kernel(where_ref, cot_ref, a_ref, b_ref, c_ref, d_ref):
+    even_lon, even_lat = evens(where_ref)
+    left, right = cot_ref[:, :16, :], cot_ref[:, TC - 16 :, :]
     top, bottom = cot_ref[:2], cot_ref[TR - 2 :]
-    v1 = jnp.where(low, bottom, top)
-    v2 = jnp.where(low, top, bottom)
-    v1_ref[...] = v1
-    v2_ref[...] = v2
-    c1l_ref[...] = v1[:, TC - 16 :]
-    c1r_ref[...] = v1[:, :16]
-    c2l_ref[...] = v2[:, TC - 16 :]
-    c2r_ref[...] = v2[:, :16]
+    a_ref[...] = jnp.where(even_lon, right, left)
+    b_ref[...] = jnp.where(even_lon, left, right)
+    c_ref[...] = jnp.where(even_lat, bottom, top)
+    d_ref[...] = jnp.where(even_lat, top, bottom)
 
 
 def edges(where, cot):
-    shapes = [(TR, 16, C), (TR, 16, C), (2, TC, C), (2, TC, C)] + [(2, 16, C)] * 4
+    shapes = [(TR, 16, C), (TR, 16, C), (2, TC, C), (2, TC, C)]
     return pl.pallas_call(
         edges_kernel,
         in_specs=[pl.BlockSpec(memory_space=pltpu.SMEM), pl.BlockSpec(memory_space=pltpu.VMEM)],
@@ -256,17 +296,18 @@
     )(where, cot)
 
 
-def cot_kernel(where_ref, cot_ref, left_ref, right_ref, v1_ref, v2_ref, c1l_ref, c1r_ref, c2l_ref, c2r_ref,
+def cot_kernel(where_ref, cot_ref, a_ref, b_ref, c_ref, d_ref,
                w_ref, hg_ref, cot_t_ref, flat_ref, copies_ref, back_ref, own_ref):
-    low, low_left, low_right = sides(where_ref)
+    even_lon, even_lat = evens(where_ref)
     north = where_ref[0] == 0
     south = where_ref[0] == where_ref[2] - 1
-    up = jnp.where(low, v1_ref[...], v2_ref[...]).astype(F32)
-    down = jnp.where(low, v2_ref[...], v1_ref[...]).astype(F32)
-    up_l = jnp.where(low_left, c1l_ref[...], c2l_ref[...]).astype(F32)
-    down_l = jnp.where(low_left, c2l_ref[...], c1l_ref[...]).astype(F32)
-    up_r = jnp.where(low_right, c1r_ref[...], c2r_ref[...]).astype(F32)
-    down_r = jnp.where(low_right, c2r_ref[...], c1r_ref[...]).astype(F32)
+    left = jnp.where(even_lon, b_ref[...], a_ref[...])
+    right = jnp.where(even_lon, a_ref[...], b_ref[...])
+    up = jnp.where(even_lat, d_ref[...], c_ref[...]).astype(F32)
+    down = jnp.where(even_lat, c_ref[...], d_ref[...]).astype(F32)
+    up_l, up_r = up[:, :16], up[:, 16 + TC :]
+    down_l, down_r = down[:, :16], down[:, 16 + TC :]
+    up, down = up[:, 16 : 16 + TC], down[:, 16 : 16 + TC]
 
     def pick(inner, up, down):
         def get(i):
@@ -280,7 +321,7 @@
 
         return get
 
-    fill_flat(flat_ref, pick(cot_ref, up, down), pick(left_ref, up_l, down_l), pick(right_ref, up_r, down_r))
+    fill_flat(flat_ref, pick(cot_ref, up, down), pick(left, up_l, down_l), pick(right, up_r, down_r))
     shifted_copies(flat_ref, copies_ref, 0, LEN // PART)
     arrange_back(w_ref, back_ref)
 
@@ -322,7 +363,7 @@
     vmem = pl.BlockSpec(memory_space=pltpu.VMEM)
     return pl.pallas_call(
         cot_kernel,
-        in_specs=[pl.BlockSpec(memory_space=pltpu.SMEM)] + [vmem] * 10,
+        in_specs=[pl.BlockSpec(memory_space=pltpu.SMEM)] + [vmem] * 6,
         out_specs=[vmem] * 2,
         out_shape=[
             jax.ShapeDtypeStruct((LEN, C), F32),
@@ -340,11 +381,11 @@
     )(where, cot, *halo, w_second)
 
 
-def main_kernel(where_ref, s_ref, left_ref, right_ref, v1_ref, v2_ref, c1l_ref, c1r_ref, c2l_ref, c2r_ref,
+def main_kernel(where_ref, s_ref, a_ref, b_ref, c_ref, d_ref,
                 wide_ref, w1_ref, w2_ref, hg_ref, cot_t_ref,
                 field_ref, red_ref,
                 flat_ref, x_ref, pre_ref, h_ref, back_ref, own_ref, own_t_ref, eg_ref):
-    low, low_left, low_right = sides(where_ref)
+    even_lon, even_lat = evens(where_ref)
     north = where_ref[0] == 0
     south = where_ref[0] == where_ref[2] - 1
     wide = wide_ref[...]
@@ -369,21 +410,11 @@
 
         return get
 
-    centre = rows_of(
-        s_ref[...],
-        jnp.where(low, v1_ref[...], v2_ref[...]),
-        jnp.where(low, v2_ref[...], v1_ref[...]),
-    )
-    left = rows_of(
-        left_ref[...],
-        jnp.where(low_left, c1l_ref[...], c2l_ref[...]),
-        jnp.where(low_left, c2l_ref[...], c1l_ref[...]),
-    )
-    right = rows_of(
-        right_ref[...],
-        jnp.where(low_right, c1r_ref[...], c2r_ref[...]),
-        jnp.where(low_right, c2r_ref[...], c1r_ref[...]),
-    )
+    up = jnp.where(even_lat, d_ref[...], c_ref[...])
+    down = jnp.where(even_lat, c_ref[...], d_ref[...])
+    centre = rows_of(s_ref[...], up[16 : 16 + TC], down[16 : 16 + TC])
+    left = rows_of(jnp.where(even_lon, b_ref[...], a_ref[...]), up[:16], down[:16])
+    right = rows_of(jnp.where(even_lon, a_ref[...], b_ref[...]), up[16 + TC :], down[16 + TC :])
     fill_flat(flat_ref, centre, left, right)
     shifted_copies(flat_ref, x_ref, 0, LEN // PART)
 
@@ -490,7 +521,7 @@
     vmem = pl.BlockSpec(memory_space=pltpu.VMEM)
     return pl.pallas_call(
         main_kernel,
-        in_specs=[pl.BlockSpec(memory_space=pltpu.SMEM)] + [vmem] * 14,
+        in_specs=[pl.BlockSpec(memory_space=pltpu.SMEM)] + [vmem] * 10,
         out_specs=[vmem] * 2,
         out_shape=[
             jax.ShapeDtypeStruct((TR, TC, C), BF16),
@@ -548,34 +579,22 @@
     )(got)
 
 
-def exchange(bands, sectors, left, right, v1, v2, c1l, c1r, c2l, c2r):
-    half = sectors // 2
-    number = lambda a, b: a * sectors + b % sectors
-
-    def above(a, b):
-        return number(a - 1, b) if a > 0 else number(0, b + half)
-
-    def below(a, b):
-        return number(a + 1, b) if a < bands - 1 else number(a, b + half)
-
-    def source(kind, a, b):
-        b = b % sectors
-        return above(a, b) if (b < half) == (kind == 1) else below(a, b)
-
-    def perm(of):
-        return [(of(a, b), number(a, b)) for a in range(bands) for b in range(sectors)]
-
-    move = lambda x, of: lax.ppermute(x, ALL, perm(of))
-    return (
-        move(right, lambda a, b: number(a, b - 1)),
-        move(left, lambda a, b: number(a, b + 1)),
-        move(v1, lambda a, b: source(1, a, b)),
-        move(v2, lambda a, b: source(2, a, b)),
-        move(c1l, lambda a, b: source(1, a, b - 1)),
-        move(c1r, lambda a, b: source(1, a, b + 1)),
-        move(c2l, lambda a, b: source(2, a, b - 1)),
-        move(c2r, lambda a, b: source(2, a, b + 1)),
-    )
+def exchange(bands, sectors, a, b, c, d, joined):
+    number = lambda lat, lon: lat * sectors + lon % sectors
+
+    def across(lat, lon):
+        if lat % 2:
+            return number(lat + 1, lon) if lat < bands - 1 else number(lat, lon + sectors // 2)
+        return number(lat - 1, lon) if lat > 0 else number(lat, lon + sectors // 2)
+
+    def swap(x, of):
+        pairs = [(number(i, j), of(i, j)) for i in range(bands) for j in range(sectors)]
+        return lax.ppermute(x, ALL, pairs)
+
+    a = swap(a, lambda i, j: number(i, j ^ 1))
+    b = swap(b, lambda i, j: number(i, j + 1 if j % 2 else j - 1))
+    c, d = joined(a, b, c, d)
+    return a, b, swap(c, lambda i, j: number(i ^ 1, j)), swap(d, across)
 
 
 def per_device(obs_values, tile_ids, obs_rows, obs_cols, w_embed, w_first, w_second, cotangent):
@@ -585,15 +604,16 @@
     where = jnp.stack(
         [lax.axis_index("lat"), lax.axis_index("lon"), jnp.int32(bands), jnp.int32(sectors)]
     ).astype(jnp.int32)
-    cot_edges = edges(where, cotangent)
-    cot_halo = exchange(bands, sectors, *cot_edges)
+    join_cot = lambda *x: join(join_cot_kernel, where, *x, (2, TC + 32, C), "join_cot")
+    cot_halo = exchange(bands, sectors, *edges(where, cotangent), join_cot)
 
     packed = pack(tile_ids.T, obs_rows.reshape(1, count), obs_cols.reshape(1, count), obs_values.T)
     got = lax.all_to_all(packed, ALL, 0, 0, tiled=True)
     hg, cot_t = cot_back(where, cotangent, cot_halo, w_second)
 
     s, *s_edges = setconv(where, got)
-    s_halo = exchange(bands, sectors, *s_edges)
+    join_s = lambda *x: join(join_kernel, where, *x, (TC + 32, 128), "join")
+    s_halo = exchange(bands, sectors, *s_edges, join_s)
     padded = jnp.concatenate([w_embed, jnp.zeros((FEAT - values, C), BF16)], axis=0)
     wide = jnp.kron(jnp.eye(4, dtype=BF16), padded)
     field, red = main(where, s, s_halo, wide, w_first, w_second, hg, cot_t, owners)

time: 168 us -> 137 us (0.82)
  Pallas kernels: 70.3 us -> 51.4 us
  starting transfers between devices: 36.9 us -> 26.4 us
  waiting for transfers between devices: 6.83 us -> 10.3 us
  blocking collectives: 47.6 us -> 45.1 us
  local copies, waits for them, and re-layouts: 4.04 us -> 2.06 us
    pallas_call x1 -> x3, Pallas kernels: 31.1 us -> 18.2 us  [the longest x1 15.1 us: pack(): pl.pallas_call(pack_kernel, grid=(steps,), in_specs=[pl.BlockSpec(memory_...]
    ppermute x16 -> x8, starting transfers between devices: 25.4 us -> 14.9 us  [swap(): return lax.ppermute(x, ALL, pairs)]
    ppermute x16 -> x8, waiting for transfers between devices: 3.85 us -> 10.3 us  [swap(): return lax.ppermute(x, ALL, pairs)]
    pallas_call x1, Pallas kernels: 9.26 us -> 5.8 us  [setconv(): pl.pallas_call(setconv_kernel, grid=(steps,), in_specs=[pl.BlockSpec(memo...]
    all_to_all x1, waiting for transfers between devices: 2.97 us -> 0.01 us  [per_device(): got = lax.all_to_all(packed, ALL, 0, 0, tiled=True)]
    all_to_all x1, blocking collectives: 26.9 us -> 24.4 us  [per_device(): parts = lax.all_to_all(red.reshape(owners, RED, C), ALL, 0, 0, tiled=True)]
    unnamed x25 -> x33, local copies, waits for them, and re-layouts: 3.94 us -> 1.96 us
    pallas_call x1, Pallas kernels: 18.8 us -> 17.1 us  [main(): pl.pallas_call(main_kernel, in_specs=[pl.BlockSpec(memory_space=pltpu.SME...]
  transfers between devices with their start and end apart: 17 -> 9, of which waited for: 2 -> 4; matrix products, arithmetic and copies ran while one was open for 0% -> 1% of each run, Pallas kernels for 11% -> 12%
where the time goes in v2:
time: 137 us
  Pallas kernels  51.4 us (38%)
  blocking collectives  45.1 us (33%)
  starting transfers between devices  26.4 us (19%)
  waiting for transfers between devices  10.3 us (8%)
  local copies, waits for them, and re-layouts  2.06 us (2%)
    all_to_all x1, blocking collectives, per_device(): parts = lax.all_to_all(red.reshape(owners, RED, C), ALL, 0, 0, tiled=True)  24.4 us
    all_to_all x1, blocking collectives, per_device(): whole = lax.all_to_all(spread, ALL, 0, 0, tiled=True)  20.7 us
    pallas_call x1, Pallas kernels, main(): pl.pallas_call(main_kernel, in_specs=[pl.BlockSpec(memory_space=pltpu.SME...  17.1 us
    pallas_call x1, Pallas kernels, pack(): pl.pallas_call(pack_kernel, grid=(steps,), in_specs=[pl.BlockSpec(memory_...  15.1 us
    ppermute x8, starting transfers between devices, swap(): return lax.ppermute(x, ALL, pairs)  14.9 us
    all_to_all x1, starting transfers between devices, per_device(): got = lax.all_to_all(packed, ALL, 0, 0, tiled=True)  11.5 us
    ppermute x8, waiting for transfers between devices, swap(): return lax.ppermute(x, ALL, pairs)  10.3 us
    pallas_call x1, Pallas kernels, cot_back(): pl.pallas_call(cot_kernel, in_specs=[pl.BlockSpec(memory_space=pltpu.SMEM...  6.13 us
  transfers between devices with their start and end apart: 9, of which 4 were waited for; matrix products, arithmetic and copies ran while one was open for 1% of the time, Pallas kernels for 12%

profile of v2, /device:TPU:1, one launch (start us, length us, event | category | flops | bytes accessed | tf_op | source)
XLA Modules:
  0.0 136.9 jit_solution(11351912601876069629)
XLA Ops:
  0.6 15.1 %pack.1 = bf16[128,32,128]{2,1,0:T(8,128)(2,1)} custom-call(s32[1,8192]{1,0:T(1,128)} %bitcast.18, f32[1,8192]{1,0:T(1,128)} %bitcast.19, f32[1,8192]{1,0:T(1,128)} %bitcast.20, bf16[24,8192]{1,0:T(8,128)(2,1)} %bitcast.17), custom_call_target="tpu_custom_call" | custom-call | flops 8589934592 | bytes 3145728 | tf_op jit(solution)/shard_map/pack/pallas_call | solution.py:108
  15.8 0.0 copy-start.15
  15.8 11.5 %all-to-all-start = ((bf16[128,32,128]{2,1,0:T(8,128)(2,1)}), bf16[128,32,128]{2,1,0:T(8,128)(2,1)S(1)}, u32[]{:S(2)}, u32[]{:S(2)}) async-start(bf16[128,32,128]{2,1,0:T(8,128)(2,1)} %pack.1), calls=%async_computation | async-start | bytes 2097152 | tf_op jit(solution)/shard_map/all_to_all | solution.py:611
  27.3 0.6 pad_add_fusion.where_ref
  27.9 1.8 %edges.1 = (bf16[16,16,128]{2,1,0:T(8,128)(2,1)}, bf16[16,16,128]{2,1,0:T(8,128)(2,1)}, bf16[2,128,128]{2,1,0:T(8,128)(2,1)}, bf16[2,128,128]{2,1,0:T(8,128)(2,1)}) custom-call(s32[4]{0:T(128)} %pad_add_fusion.where_ref, bf16[16,128,128]{2,1,0:T(8,128)(2,1)} %cot_ref.3), custom_call_target="tpu_custom_call" | custom-call | bytes 1048576 | tf_op jit(solution)/shard_map/edges/pallas_call | solution.py:289
  29.6 1.1 collective-permute-start.4
  30.7 0.7 collective-permute-start.5
  31.4 0.0 copy-done.15
  31.4 0.4 collective-permute-done.4.a_ref
  31.8 0.0 copy-start.1
  31.8 7.0 %collective-permute-done.5.b_ref = bf16[16,16,128]{2,1,0:T(8,128)(2,1)S(1)} collective-permute-done((bf16[16,16,128]{2,1,0:T(8,128)(2,1)}, bf16[16,16,128]{2,1,0:T(8,128)(2,1)S(1)}, u32[]{:S(2)}, u32[]{:S(2)}) %collective-permute-start.5) | collective-permute-done | bytes 65568 | tf_op jit(solution)/shard_map/ppermute | solution.py:592
  38.8 0.0 copy-start.3
  38.8 0.0 copy-done.1
  38.8 0.6 copy-done.3
  39.5 1.6 %join_cot.1 = (bf16[2,160,128]{2,1,0:T(8,128)(2,1)}, bf16[2,160,128]{2,1,0:T(8,128)(2,1)}) custom-call(s32[4]{0:T(128)} %pad_add_fusion.where_ref, bf16[16,16,128]{2,1,0:T(8,128)(2,1)} %copy-done.1, bf16[16,16,128]{2,1,0:T(8,128)(2,1)} %copy-done.3, bf16[2,128,128]{2,1,0:T(8,128)(2,1)} %get-tuple-element.33.c_ref, bf16[2,128,128]{2,1,0:T(8,128)(2,1)} %get-tuple-element.34.d_ref), custom_call_target="tpu_custom_call" | custom-call | bytes 262144 | tf_op jit(solution)/shard_map/join_cot/pallas_call | solution.py:220
  41.1 2.4 %collective-permute-start.6 = (bf16[2,160,128]{2,1,0:T(8,128)(2,1)}, bf16[2,160,128]{2,1,0:T(8,128)(2,1)S(1)}, u32[]{:S(2)}, u32[]{:S(2)}) collective-permute-start(bf16[2,160,128]{2,1,0:T(8,128)(2,1)} %get-tuple-element.35), channel_id=1, source_target_pairs={{0,16},{1,17},{2,18},{3,19},{4,20},{5,21},{6,22},{7,23},{8,24},{9,... | collective-permute-start | bytes 245768 | tf_op jit(solution)/shard_map/ppermute | solution.py:592
  43.5 0.0 copy-start.12
  43.5 0.0 copy-start
  43.5 0.0 copy-start.2
  43.5 0.0 copy-start.4
  43.5 5.8 %collective-permute-start.7 = (bf16[2,160,128]{2,1,0:T(8,128)(2,1)}, bf16[2,160,128]{2,1,0:T(8,128)(2,1)S(1)}, u32[]{:S(2)}, u32[]{:S(2)}) collective-permute-start(bf16[2,160,128]{2,1,0:T(8,128)(2,1)} %get-tuple-element.36), channel_id=1, source_target_pairs={{0,8},{1,9},{2,10},{3,11},{4,12},{5,13},{6,14},{7,15},{8,0},{9,1},... | collective-permute-start | bytes 245768 | tf_op jit(solution)/shard_map/ppermute | solution.py:592
  49.4 0.0 all-to-all-done.got_ref
  49.4 0.0 copy-start.11
  49.4 0.6 copy-done.11
  50.0 0.0 copy-start.14
  50.0 5.8 %setconv.1 = (bf16[128,512]{1,0:T(8,128)(2,1)S(1)}, bf16[16,512]{1,0:T(8,128)(2,1)S(1)}, bf16[16,512]{1,0:T(8,128)(2,1)S(1)}, bf16[128,128]{1,0:T(8,128)(2,1)S(1)}, bf16[128,128]{1,0:T(8,128)(2,1)S(1)}) custom-call(s32[4]{0:T(128)S(1)} %copy-done.11, bf16[128,32,128]{2,1,0:T(8,128)(2,1)S(1)} %all-to-all-done.got_ref), custom_call_target="tpu_custom_call" | custom-call | flops 3221225472 | bytes 2097152 | tf_op jit(solution)/shard_map/setconv/pallas_call | solution.py:176
  55.8 0.0 copy-start.5
  55.8 0.0 copy-start.6
  55.8 0.4 collective-permute-start
  56.2 0.0 collective-permute-start.1
  56.2 0.1 broadcast_multiply_fusion
  56.3 0.1 copy-done.5
  56.4 0.0 copy-done.6
  56.4 0.6 collective-permute-done.a_ref
  57.1 0.0 copy-start.7
  57.1 2.3 %collective-permute-done.1.b_ref = bf16[16,512]{1,0:T(8,128)(2,1)S(1)} collective-permute-done((bf16[16,512]{1,0:T(8,128)(2,1)S(1)}, bf16[16,512]{1,0:T(8,128)(2,1)S(1)}, u32[]{:S(2)}, u32[]{:S(2)}) %collective-permute-start.1) | collective-permute-done | bytes 16416 | tf_op jit(solution)/shard_map/ppermute | solution.py:592
  59.3 0.0 copy-start.9
  59.3 0.0 copy-done.7
  59.3 0.6 copy-done.9
  59.9 1.5 %join.1 = (bf16[160,128]{1,0:T(8,128)(2,1)}, bf16[160,128]{1,0:T(8,128)(2,1)}) custom-call(s32[4]{0:T(128)} %pad_add_fusion.where_ref, bf16[16,512]{1,0:T(8,128)(2,1)} %copy-done.7, bf16[16,512]{1,0:T(8,128)(2,1)} %copy-done.9, bf16[128,128]{1,0:T(8,128)(2,1)} %copy-done.5, bf16[128,128]{1,0:T(8,128)(2,1)} %copy-done.6), custom_call_target="tpu_custom_call" | custom-call | bytes 262144 | tf_op jit(solution)/shard_map/join/pallas_call | solution.py:220
  61.4 3.6 %collective-permute-start.2 = (bf16[160,128]{1,0:T(8,128)(2,1)}, bf16[160,128]{1,0:T(8,128)(2,1)S(1)}, u32[]{:S(2)}, u32[]{:S(2)}) collective-permute-start(bf16[160,128]{1,0:T(8,128)(2,1)} %get-tuple-element.29), channel_id=1, source_target_pairs={{0,16},{1,17},{2,18},{3,19},{4,20},{5,21},{6,22},{7,23},{8,24},{9,... | collective-permute-start | bytes 122888 | tf_op jit(solution)/shard_map/ppermute | solution.py:592
  65.0 0.0 copy-start.8
  65.0 0.0 copy-start.10
  65.0 0.0 copy-start.13
  65.0 0.9 collective-permute-start.3
  65.8 0.0 collective-permute-done.6.c_ref
  65.8 0.0 collective-permute-done.7.d_ref
  65.8 0.0 copy-done.12
  65.8 0.0 copy-done
  65.8 0.0 copy-done.2
  65.9 0.0 copy-done.4
  65.9 0.0 copy-done.14
  65.9 6.1 %cot_back.1 = (f32[3040,128]{1,0:T(8,128)S(1)}, bf16[128,2304]{1,0:T(8,128)(2,1)S(1)}) custom-call(s32[4]{0:T(128)S(1)} %copy-done.12, bf16[16,128,128]{2,1,0:T(8,128)(2,1)S(1)} %copy-done, bf16[16,16,128]{2,1,0:T(8,128)(2,1)S(1)} %copy-done.2, bf16[16,16,128]{2,1,0:T(8,128)(2,1)S(1)} %copy-done.4, bf16[2,160,128]{2,1,0:T(8,128)(2,1)S(1)} %collective-permute-done.6.c_ref, ...), custom_call_target="tpu_custom_call" | custom-call | flops 1613758464 | bytes 4194304 | tf_op jit(solution)/shard_map/cot_back/pallas_call | solution.py:364
  72.0 0.0 collective-permute-done.2.c_ref
  72.0 0.0 collective-permute-done.3.d_ref
  72.0 0.0 copy-done.8
  72.0 0.0 copy-done.10
  72.1 0.0 copy-done.13
  72.1 17.1 %main.1 = (bf16[16,128,128]{2,1,0:T(8,128)(2,1)}, bf16[3072,128]{1,0:T(8,128)(2,1)S(1)}) custom-call(s32[4]{0:T(128)S(1)} %copy-done.12, bf16[128,512]{1,0:T(8,128)(2,1)S(1)} %get-tuple-element.24.s_ref, bf16[16,512]{1,0:T(8,128)(2,1)S(1)} %copy-done.8, bf16[16,512]{1,0:T(8,128)(2,1)S(1)} %copy-done.10, bf16[160,128]{1,0:T(8,128)(2,1)S(1)} %collective-permute-done.2.c_ref, ...), custom_call_target="tpu_custom_call" | custom-call | flops 8589934592 | bytes 6291456 | tf_op jit(solution)/shard_map/main/pallas_call | solution.py:522
  89.1 24.4 %all_to_all.15 = bf16[128,24,128]{2,1,0:T(8,128)(2,1)S(1)} all-to-all(bf16[128,24,128]{2,1,0:T(8,128)(2,1)S(1)} %bitcast.13), channel_id=1, replica_groups=mesh['lat'=8,'lon'=16] {'lat','lon'}, dimensions={0} | all-to-all | bytes 1572864 | tf_op jit(solution)/shard_map/all_to_all | solution.py:621
  113.5 0.2 reduce_sum.12
  113.7 0.1 broadcast_in_dim.6
  113.8 20.7 %all_to_all.16 = bf16[128,24,128]{2,1,0:T(8,128)(2,1)} all-to-all(bf16[128,24,128]{2,1,0:T(8,128)(2,1)S(1)} %broadcast_in_dim.6), channel_id=1, replica_groups=mesh['lat'=8,'lon'=16] {'lat','lon'}, dimensions={0} | all-to-all | bytes 1572864 | tf_op jit(solution)/shard_map/all_to_all | solution.py:624
  134.5 2.4 %unpack.1 = (f32[24,128]{1,0:T(8,128)}, f32[3,3,128,128]{3,2,1,0:T(8,128)}, f32[3,3,128,128]{3,2,1,0:T(8,128)}) custom-call(bf16[3072,128]{1,0:T(8,128)(2,1)} %bitcast.15), custom_call_target="tpu_custom_call" | custom-call | tf_op jit(solution)/shard_map/unpack/pallas_call | solution.py:569
  (3 shorter events, 0.0 us)
Async XLA Ops:
  15.8 15.6 %copy-start.15 = (bf16[24,128]{1,0:T(8,128)(2,1)S(1)}, bf16[24,128]{1,0:T(8,128)(2,1)}, u32[]{:S(2)}) copy-start(bf16[24,128]{1,0:T(8,128)(2,1)} %param.12) | copy-start | bytes 18436
  15.8 33.6 %all-to-all-start = ((bf16[128,32,128]{2,1,0:T(8,128)(2,1)}), bf16[128,32,128]{2,1,0:T(8,128)(2,1)S(1)}, u32[]{:S(2)}, u32[]{:S(2)}) async-start(bf16[128,32,128]{2,1,0:T(8,128)(2,1)} %pack.1), calls=%async_computation | async-start | bytes 2097152 | tf_op jit(solution)/shard_map/all_to_all | solution.py:611
  29.6 2.2 %collective-permute-start.4 = (bf16[16,16,128]{2,1,0:T(8,128)(2,1)}, bf16[16,16,128]{2,1,0:T(8,128)(2,1)S(1)}, u32[]{:S(2)}, u32[]{:S(2)}) collective-permute-start(bf16[16,16,128]{2,1,0:T(8,128)(2,1)} %get-tuple-element.31), channel_id=1, source_target_pairs={{0,1},{1,0},{2,3},{3,2},{4,5},{5,4},{6,7},{7,6},{8,9},{9,8},{10,11... | collective-permute-start | bytes 196616 | tf_op jit(solution)/shard_map/ppermute | solution.py:592
  30.7 8.1 %collective-permute-start.5 = (bf16[16,16,128]{2,1,0:T(8,128)(2,1)}, bf16[16,16,128]{2,1,0:T(8,128)(2,1)S(1)}, u32[]{:S(2)}, u32[]{:S(2)}) collective-permute-start(bf16[16,16,128]{2,1,0:T(8,128)(2,1)} %get-tuple-element.32), channel_id=1, source_target_pairs={{0,15},{1,2},{2,1},{3,4},{4,3},{5,6},{6,5},{7,8},{8,7},{9,10},{10,... | collective-permute-start | bytes 196616 | tf_op jit(solution)/shard_map/ppermute | solution.py:592
  31.8 7.0 %copy-start.1 = (bf16[16,16,128]{2,1,0:T(8,128)(2,1)}, bf16[16,16,128]{2,1,0:T(8,128)(2,1)S(1)}, u32[]{:S(2)}) copy-start(bf16[16,16,128]{2,1,0:T(8,128)(2,1)S(1)} %collective-permute-done.4.a_ref) | copy-start | bytes 196612
  38.8 0.6 copy-start.3
  41.1 24.7 %collective-permute-start.6 = (bf16[2,160,128]{2,1,0:T(8,128)(2,1)}, bf16[2,160,128]{2,1,0:T(8,128)(2,1)S(1)}, u32[]{:S(2)}, u32[]{:S(2)}) collective-permute-start(bf16[2,160,128]{2,1,0:T(8,128)(2,1)} %get-tuple-element.35), channel_id=1, source_target_pairs={{0,16},{1,17},{2,18},{3,19},{4,20},{5,21},{6,22},{7,23},{8,24},{9,... | collective-permute-start | bytes 245768 | tf_op jit(solution)/shard_map/ppermute | solution.py:592
  43.5 22.3 %copy-start.12 = (s32[4]{0:T(128)S(1)}, s32[4]{0:T(128)}, u32[]{:S(2)}) copy-start(s32[4]{0:T(128)} %pad_add_fusion.where_ref) | copy-start | bytes 52
  43.5 22.3 %copy-start = (bf16[16,128,128]{2,1,0:T(8,128)(2,1)S(1)}, bf16[16,128,128]{2,1,0:T(8,128)(2,1)}, u32[]{:S(2)}) copy-start(bf16[16,128,128]{2,1,0:T(8,128)(2,1)} %cot_ref.3) | copy-start | bytes 1572868
  43.5 22.3 %copy-start.2 = (bf16[16,16,128]{2,1,0:T(8,128)(2,1)S(1)}, bf16[16,16,128]{2,1,0:T(8,128)(2,1)}, u32[]{:S(2)}) copy-start(bf16[16,16,128]{2,1,0:T(8,128)(2,1)} %copy-done.1) | copy-start | bytes 196612
  43.5 22.3 %copy-start.4 = (bf16[16,16,128]{2,1,0:T(8,128)(2,1)S(1)}, bf16[16,16,128]{2,1,0:T(8,128)(2,1)}, u32[]{:S(2)}) copy-start(bf16[16,16,128]{2,1,0:T(8,128)(2,1)} %copy-done.3) | copy-start | bytes 196612
  43.5 22.3 %collective-permute-start.7 = (bf16[2,160,128]{2,1,0:T(8,128)(2,1)}, bf16[2,160,128]{2,1,0:T(8,128)(2,1)S(1)}, u32[]{:S(2)}, u32[]{:S(2)}) collective-permute-start(bf16[2,160,128]{2,1,0:T(8,128)(2,1)} %get-tuple-element.36), channel_id=1, source_target_pairs={{0,8},{1,9},{2,10},{3,11},{4,12},{5,13},{6,14},{7,15},{8,0},{9,1},... | collective-permute-start | bytes 245768 | tf_op jit(solution)/shard_map/ppermute | solution.py:592
  49.4 0.6 copy-start.11
  50.0 15.9 %copy-start.14 = (bf16[3,3,128,128]{3,2,1,0:T(8,128)(2,1)S(1)}, bf16[3,3,128,128]{3,2,1,0:T(8,128)(2,1)}, u32[]{:S(2)}) copy-start(bf16[3,3,128,128]{3,2,1,0:T(8,128)(2,1)} %w2_ref.1) | copy-start | bytes 884740
  55.8 0.6 copy-start.5
  55.8 0.6 copy-start.6
  55.8 1.3 collective-permute-start
  56.2 3.2 %collective-permute-start.1 = (bf16[16,512]{1,0:T(8,128)(2,1)S(1)}, bf16[16,512]{1,0:T(8,128)(2,1)S(1)}, u32[]{:S(2)}, u32[]{:S(2)}) collective-permute-start(bf16[16,512]{1,0:T(8,128)(2,1)S(1)} %get-tuple-element.26), channel_id=1, source_target_pairs={{0,15},{1,2},{2,1},{3,4},{4,3},{5,6},{6,5},{7,8},{8,7},{9,10},{10,... | collective-permute-start | bytes 49160 | tf_op jit(solution)/shard_map/ppermute | solution.py:592
  57.1 2.3 %copy-start.7 = (bf16[16,512]{1,0:T(8,128)(2,1)}, bf16[16,512]{1,0:T(8,128)(2,1)S(1)}, u32[]{:S(2)}) copy-start(bf16[16,512]{1,0:T(8,128)(2,1)S(1)} %collective-permute-done.a_ref) | copy-start | bytes 49156
  59.3 0.6 copy-start.9
  61.4 10.6 %collective-permute-start.2 = (bf16[160,128]{1,0:T(8,128)(2,1)}, bf16[160,128]{1,0:T(8,128)(2,1)S(1)}, u32[]{:S(2)}, u32[]{:S(2)}) collective-permute-start(bf16[160,128]{1,0:T(8,128)(2,1)} %get-tuple-element.29), channel_id=1, source_target_pairs={{0,16},{1,17},{2,18},{3,19},{4,20},{5,21},{6,22},{7,23},{8,24},{9,... | collective-permute-start | bytes 122888 | tf_op jit(solution)/shard_map/ppermute | solution.py:592
  65.0 7.1 %copy-start.8 = (bf16[16,512]{1,0:T(8,128)(2,1)S(1)}, bf16[16,512]{1,0:T(8,128)(2,1)}, u32[]{:S(2)}) copy-start(bf16[16,512]{1,0:T(8,128)(2,1)} %copy-done.7) | copy-start | bytes 49156
  65.0 7.1 %copy-start.10 = (bf16[16,512]{1,0:T(8,128)(2,1)S(1)}, bf16[16,512]{1,0:T(8,128)(2,1)}, u32[]{:S(2)}) copy-start(bf16[16,512]{1,0:T(8,128)(2,1)} %copy-done.9) | copy-start | bytes 49156
  65.0 7.1 %copy-start.13 = (bf16[3,3,128,128]{3,2,1,0:T(8,128)(2,1)S(1)}, bf16[3,3,128,128]{3,2,1,0:T(8,128)(2,1)}, u32[]{:S(2)}) copy-start(bf16[3,3,128,128]{3,2,1,0:T(8,128)(2,1)} %w1_ref.1) | copy-start | bytes 884740
  65.0 7.1 %collective-permute-start.3 = (bf16[160,128]{1,0:T(8,128)(2,1)}, bf16[160,128]{1,0:T(8,128)(2,1)S(1)}, u32[]{:S(2)}, u32[]{:S(2)}) collective-permute-start(bf16[160,128]{1,0:T(8,128)(2,1)} %get-tuple-element.30), channel_id=1, source_target_pairs={{0,8},{1,9},{2,10},{3,11},{4,12},{5,13},{6,14},{7,15},{8,0},{9,1},... | collective-permute-start | bytes 122888 | tf_op jit(solution)/shard_map/ppermute | solution.py:592

commit v3 on v2

v3 whole, which is shorter than its diff:
```python
import functools
import math
import jax
import jax.numpy as jnp
from jax import lax
from jax.experimental import pallas as pl
from jax.experimental.pallas import tpu as pltpu
from jax.sharding import PartitionSpec as P

F32 = jnp.float32
BF16 = jnp.bfloat16
spread_cells = 1.0
ALL = ("lat", "lon")

TR, TC, C = 16, 128, 128
PITCH = TC + 16
LEN = 3040
PART = 304
FIRST = PITCH
OWN = 16 + 2 * PITCH
FEAT = 32
RED = 24
HALF = 9 * C + FEAT
SG = TR * FEAT // 128
WIDE = 8


def dot(a, b):
    return jnp.dot(a, b, preferred_element_type=F32)


def dot_nt(a, b):
    return lax.dot_general(a, b, (((1,), (1,)), ((), ())), preferred_element_type=F32)


def place(i):
    return 16 + (i + 2) * PITCH


def pack_kernel(where_ref, ids_hbm, rows_hbm, cols_hbm, vals_hbm, out_ref,
                ids_ref, rows_ref, cols_ref, vals_ref, q_ref, v_ref, pair_ref, acc_ref, sems):
    step = pl.program_id(0)
    count = ids_ref.shape[1]
    owners = out_ref.shape[0] * pl.num_programs(0)
    sub = 256
    part = 2048
    pairs = out_ref.shape[0] // 2

    @pl.when(step == 0)
    def _():
        moves = [
            pltpu.make_async_copy(a, b, sems.at[k])
            for k, (a, b) in enumerate(
                [(ids_hbm, ids_ref), (rows_hbm, rows_ref), (cols_hbm, cols_ref), (vals_hbm, vals_ref)]
            )
        ]
        for move in moves:
            move.start()
        owner = lax.broadcasted_iota(jnp.int32, (owners, sub), 0)
        slot = lax.broadcasted_iota(jnp.int32, (sub, sub), 0)
        upto = slot <= lax.broadcasted_iota(jnp.int32, (sub, sub), 1)
        upto = jnp.concatenate(
            [jnp.where(upto, 1.0, 0.0).astype(BF16), jnp.ones((sub, 128), BF16)], axis=1
        )
        for move in moves:
            move.wait()

        def body(k, carry):
            for u in range(4):
                at = pl.ds(pl.multiple_of(k * 4 * sub + u * sub, sub), sub)
                ids = ids_ref[:, at]
                hot = owner == ids
                counted = dot(jnp.where(hot, 1.0, 0.0).astype(BF16), upto)
                before = counted[:, :sub] + jnp.concatenate([carry, carry], axis=1)
                rank = jnp.sum(jnp.where(hot, before, 0.0), axis=0, keepdims=True) - 1.0
                key = rank.astype(jnp.int32) + (ids & 1) * 128
                q_ref[:, at] = jnp.where(slot == key, 1.0, 0.0).astype(BF16)
                pair_ref[:, at] = jnp.broadcast_to((ids >> 1).astype(F32), (FEAT, sub)).astype(BF16)
                rows, cols = rows_ref[:, at], cols_ref[:, at]
                rows_hi, cols_hi = rows.astype(BF16).astype(F32), cols.astype(BF16).astype(F32)
                tail = jnp.concatenate(
                    [rows_hi, rows - rows_hi, cols_hi, cols - cols_hi, jnp.zeros((4, sub), F32)], axis=0
                )
                v_ref[:, at] = jnp.concatenate([vals_ref[:, at].astype(F32), tail], axis=0).astype(BF16)
                carry = carry + counted[:, sub:]
            return carry

        lax.fori_loop(0, count // sub // 4, body, jnp.zeros((owners, 128), F32))

    base = jnp.full((FEAT, part), (step * pairs).astype(F32), F32).astype(BF16)
    for k in range(count // part):
        at = pl.ds(k * part, part)
        pair = pair_ref[:, at] - base
        values = v_ref[:, at]
        none = jnp.zeros_like(values)
        left = jnp.concatenate([jnp.where(pair == p, values, none) for p in range(pairs)], axis=0)
        term = dot_nt(left, q_ref[:, at])
        if k == 0:
            acc_ref[...] = term
        else:
            acc_ref[...] += term
    for p in range(pairs):
        out_ref[2 * p] = acc_ref[p * FEAT : (p + 1) * FEAT, :128].astype(BF16)
        out_ref[2 * p + 1] = acc_ref[p * FEAT : (p + 1) * FEAT, 128:].astype(BF16)


def pack(where, ids, rows, cols, values):
    count = ids.shape[1]
    owners = 128
    steps = 4
    return pl.pallas_call(
        pack_kernel,
        grid=(steps,),
        in_specs=[pl.BlockSpec(memory_space=pltpu.SMEM)] + [pl.BlockSpec(memory_space=pl.ANY)] * 4,
        out_specs=pl.BlockSpec((owners // steps, FEAT, 128), lambda i: (i, 0, 0)),
        out_shape=jax.ShapeDtypeStruct((owners, FEAT, 128), BF16),
        scratch_shapes=[
            pltpu.VMEM(ids.shape, ids.dtype),
            pltpu.VMEM(rows.shape, rows.dtype),
            pltpu.VMEM(cols.shape, cols.dtype),
            pltpu.VMEM(values.shape, values.dtype),
            pltpu.VMEM((256, count), BF16),
            pltpu.VMEM((FEAT, count), BF16),
            pltpu.VMEM((FEAT, count), BF16),
            pltpu.VMEM((owners // steps // 2 * FEAT, 256), F32),
            pltpu.SemaphoreType.DMA((4,)),
        ],
        compiler_params=pltpu.CompilerParams(vmem_limit_bytes=58 << 20),
        cost_estimate=pl.CostEstimate(flops=2 * 2048 * 256 * 8192, bytes_accessed=3 << 20, transcendentals=0),
        name="pack",
    )(where, ids, rows, cols, values)


def setconv_kernel(where_ref, got_ref, cot_ref, s_ref, a_ref, b_ref, acc_ref):
    step = pl.program_id(0)
    x = jnp.concatenate([got_ref[k] for k in range(got_ref.shape[0])], axis=1).astype(F32)
    n = x.shape[1]
    alpha = math.sqrt(0.5 / math.log(2.0)) / spread_cells
    row = (x[24:25] + x[25:26]) * alpha
    col = (x[26:27] + x[27:28]) * alpha
    row_mid = (lax.broadcasted_iota(jnp.int32, (TR, n), 0).astype(F32) + 0.5) * alpha
    col_mid = (lax.broadcasted_iota(jnp.int32, (TC, n), 0).astype(F32) + 0.5) * alpha
    row_weight = jnp.exp2(-jnp.square(row - row_mid))
    col_weight = jnp.exp2(-jnp.square(col - col_mid)).astype(BF16)
    values = x[:24]
    weighted = jnp.concatenate([values * row_weight[i : i + 1] for i in range(TR)], axis=0).astype(BF16)
    term = dot_nt(weighted, col_weight)

    @pl.when(step == 0)
    def _():
        acc_ref[...] = term

    @pl.when(step > 0)
    def _():
        acc_ref[...] += term

    @pl.when(step == pl.num_programs(0) - 1)
    def _():
        none = jnp.zeros((FEAT - 24, TC), F32)
        for g in range(TR // 4):
            rows = []
            for i in range(4 * g, 4 * g + 4):
                rows += [acc_ref[24 * i : 24 * i + 24], none]
            s_ref[:, g * 128 : (g + 1) * 128] = jnp.concatenate(rows, axis=0).T.astype(BF16)
        even_lon, _ = evens(where_ref)
        for g in range(SG):
            left, right = s_ref[:16, g * 128 : (g + 1) * 128], s_ref[TC - 16 :, g * 128 : (g + 1) * 128]
            a_ref[g] = jnp.where(even_lon, right, left)
            b_ref[g] = jnp.where(even_lon, left, right)
        left, right = cot_ref[:, :16, :], cot_ref[:, TC - 16 :, :]
        a_ref[SG:] = jnp.where(even_lon, right, left)
        b_ref[SG:] = jnp.where(even_lon, left, right)


def setconv(where, got, cot):
    steps = 8
    fixed = lambda *shape: pl.BlockSpec(shape, lambda i: (0,) * len(shape))
    lanes = TR * FEAT
    shapes = [(TC, lanes), (SG + TR, 16, C), (SG + TR, 16, C)]
    return pl.pallas_call(
        setconv_kernel,
        grid=(steps,),
        in_specs=[
            pl.BlockSpec(memory_space=pltpu.SMEM),
            pl.BlockSpec((got.shape[0] // steps, FEAT, 128), lambda i: (i, 0, 0)),
            fixed(*cot.shape),
        ],
        out_specs=[fixed(*s) for s in shapes],
        out_shape=[jax.ShapeDtypeStruct(s, BF16) for s in shapes],
        scratch_shapes=[pltpu.VMEM((TR * 24, TC), F32)],
        compiler_params=pltpu.CompilerParams(vmem_limit_bytes=16 << 20),
        cost_estimate=pl.CostEstimate(
            flops=2 * 384 * 256 * 16384, bytes_accessed=2 << 20, transcendentals=144 * 16384
        ),
        name="setconv",
    )(where, got, cot)


def join_kernel(where_ref, a_ref, b_ref, s_ref, cot_ref, c_out, d_out):
    even_lon, even_lat = evens(where_ref)
    right = jnp.where(even_lon, a_ref[...], b_ref[...])
    left = jnp.where(even_lon, b_ref[...], a_ref[...])
    centre = slice(16, 16 + TC)
    for out, first in ((c_out, ~even_lat), (d_out, even_lat)):
        out[0, :16] = jnp.where(first, left[0], left[SG - 1])
        out[0, centre] = jnp.where(first, s_ref[:, :128], s_ref[:, -128:])
        out[0, 16 + TC :] = jnp.where(first, right[0], right[SG - 1])
        out[1:, :16] = jnp.where(first, left[SG : SG + 2], left[-2:])
        out[1:, centre] = jnp.where(first, cot_ref[:2], cot_ref[TR - 2 :])
        out[1:, 16 + TC :] = jnp.where(first, right[SG : SG + 2], right[-2:])


def join(where, a, b, s, cot):
    vmem = pl.BlockSpec(memory_space=pltpu.VMEM)
    return pl.pallas_call(
        join_kernel,
        in_specs=[pl.BlockSpec(memory_space=pltpu.SMEM)] + [vmem] * 4,
        out_specs=[vmem] * 2,
        out_shape=[jax.ShapeDtypeStruct((3, TC + 32, C), BF16)] * 2,
        cost_estimate=pl.CostEstimate(flops=0, bytes_accessed=1 << 18, transcendentals=0),
        compiler_params=pltpu.CompilerParams(vmem_limit_bytes=8 << 20),
        name="join",
    )(where, a, b, s, cot)


def shifted_copies(flat_ref, out_ref, begin, parts):
    def body(k, carry):
        at = pl.multiple_of(begin + k * PART, 16)
        for s in range(3):
            out_ref[pl.ds(at, PART), s * C : (s + 1) * C] = flat_ref[pl.ds(at + 7 + s, PART), :].astype(BF16)
        return carry

    lax.fori_loop(0, parts, body, 0)


def three_rows(src_ref, at, rows):
    return jnp.concatenate(
        [src_ref[pl.ds(at + (r - 1) * PITCH, rows), :] for r in range(3)], axis=1
    )


def conv_rows(src_ref, at, rows, weights):
    return dot(three_rows(src_ref, at, rows), jnp.concatenate(weights, axis=0))


def back_rows(src_ref, at, rows, weights):
    return dot_nt(three_rows(src_ref, at, rows), jnp.concatenate(weights, axis=1))


def fill_flat(flat_ref, begin, end, centre, left, right):
    first = lax.broadcasted_iota(jnp.int32, (16, C), 0) < 8
    flat_ref[place(begin) - 8 : place(begin) + 8] = left(begin)
    for i in range(begin, end):
        at = 8 + place(i)
        flat_ref[at : at + TC] = centre(i)
        after = jnp.where(first, right(i), left(i + 1)) if i < end - 1 else right(i)
        flat_ref[at + TC : at + PITCH] = after


def clear_flat(flat_ref, begin, end):
    flat_ref[begin:end] = jnp.zeros((end - begin, C), F32)


def evens(where_ref):
    return where_ref[1] % 2 == 0, where_ref[0] % 2 == 0


def arrange_back(w_ref, out_ref):
    for r in range(3):
        for s in range(3):
            out_ref[r, :, s * C : (s + 1) * C] = w_ref[2 - r, 2 - s]


def mid_kernel(where_ref, cot_ref, s_ref, a_ref, b_ref, w_ref, embed_ref,
               hg_ref, cot_t_ref, x_ref, flat_ref, copies_ref, back_ref, own_ref, wide_ref):
    even_lon, _ = evens(where_ref)
    left = jnp.where(even_lon, b_ref[SG:], a_ref[SG:])
    right = jnp.where(even_lon, a_ref[SG:], b_ref[SG:])
    row = lambda rows: lambda i: rows[i].astype(F32)
    clear_flat(flat_ref, 0, place(0) - 8)
    clear_flat(flat_ref, 8 + place(TR), flat_ref.shape[0])
    fill_flat(flat_ref, 0, TR, row(cot_ref), row(left), row(right))
    shifted_copies(flat_ref, copies_ref, 0, LEN // PART)
    arrange_back(w_ref, back_ref)

    def body(k, carry):
        at = pl.multiple_of(FIRST + k * 3 * PART, 16)
        hg_ref[pl.ds(at, 3 * PART), :] = back_rows(copies_ref, at, 3 * PART, [back_ref[0], back_ref[1], back_ref[2]])
        return carry

    lax.fori_loop(0, 3, body, 0)

    for i in range(TR):
        own_ref[i * PITCH : i * PITCH + TC] = cot_ref[i]
        own_ref[i * PITCH + TC : (i + 1) * PITCH] = jnp.zeros((PITCH - TC, C), BF16)
    transpose_flat(own_ref, cot_t_ref)

    wide = spread_weights(embed_ref, wide_ref)

    def rows_of(groups):
        groups = [dot(group, wide) for group in groups]
        return lambda i: groups[i // 4][:, i % 4 * C : (i % 4 + 1) * C]

    centre = rows_of([s_ref[:, g * 128 : (g + 1) * 128] for g in range(SG)])
    left = rows_of([jnp.where(even_lon, b_ref[g], a_ref[g]) for g in range(SG)])
    right = rows_of([jnp.where(even_lon, a_ref[g], b_ref[g]) for g in range(SG)])
    fill_flat(flat_ref, 0, TR, centre, left, right)
    shifted_copies(flat_ref, x_ref, 0, LEN // PART)


def spread_weights(embed_ref, wide_ref):
    values = embed_ref.shape[0]
    wide_ref[...] = jnp.zeros_like(wide_ref)
    for k in range(4):
        wide_ref[k * FEAT : k * FEAT + values, k * C : (k + 1) * C] = embed_ref[...].astype(F32)
    return wide_ref[...].astype(BF16)


def transpose_flat(own_ref, out_ref):
    out_ref[...] = own_ref[...].T


def mid(where, cot, s, a, b, w_second, w_embed):
    vmem = pl.BlockSpec(memory_space=pltpu.VMEM)
    return pl.pallas_call(
        mid_kernel,
        in_specs=[pl.BlockSpec(memory_space=pltpu.SMEM)] + [vmem] * 6,
        out_specs=[vmem] * 3,
        out_shape=[
            jax.ShapeDtypeStruct((LEN, C), F32),
            jax.ShapeDtypeStruct((C, TR * PITCH), BF16),
            jax.ShapeDtypeStruct((LEN, 3 * C), BF16),
        ],
        scratch_shapes=[
            pltpu.VMEM((LEN + 16, C), F32),
            pltpu.VMEM((LEN, 3 * C), BF16),
            pltpu.VMEM((3, C, 3 * C), BF16),
            pltpu.VMEM((TR * PITCH, C), BF16),
            pltpu.VMEM((4 * FEAT, 4 * C), F32),
        ],
        compiler_params=pltpu.CompilerParams(vmem_limit_bytes=24 << 20),
        cost_estimate=pl.CostEstimate(flops=2 * 2736 * 1152 * 256, bytes_accessed=4 << 20, transcendentals=0),
        name="mid",
    )(where, cot, s, a, b, w_second, w_embed)


def main_kernel(where_ref, cot_ref, s_ref, a_ref, b_ref, c_ref, d_ref,
                embed_ref, w1_ref, w2_ref, cot_t_ref, hg_in, x_in,
                field_ref, red_ref, hg_ref, x_ref,
                flat_ref, pre_ref, h_ref, back_ref, own_ref, own_t_ref, eg_ref, wide_ref):
    even_lon, even_lat = evens(where_ref)
    north = where_ref[0] == 0
    south = where_ref[0] == where_ref[2] - 1
    north_row, south_row = jnp.where(north, 2, 0), jnp.where(south, 0, 2)
    pad, centre, tail = slice(0, 16), slice(16, 16 + TC), slice(16 + TC, 32 + TC)

    def edge(k):
        up = jnp.where(even_lat, d_ref[k], c_ref[k])
        down = jnp.where(even_lat, c_ref[k], d_ref[k])
        left = lambda i: jnp.where(even_lon, b_ref[i], a_ref[i])
        right = lambda i: jnp.where(even_lon, a_ref[i], b_ref[i])
        return up, down, left, right

    up0, down0, left, right = edge(1)
    up1, down1, _, _ = edge(2)

    def cot_rows(part, inner):
        near_up, far_up = jnp.where(north, up0[part], up1[part]), jnp.where(north, up1[part], up0[part])
        near_down, far_down = jnp.where(south, down1[part], down0[part]), jnp.where(south, down0[part], down1[part])
        outer = {-1: near_up, -2: far_up, TR: near_down, TR + 1: far_down}
        return lambda i: (outer[i] if i in outer else inner(i)).astype(F32)

    rows = (
        cot_rows(centre, lambda i: cot_ref[i]),
        cot_rows(pad, lambda i: left(SG + i)),
        cot_rows(tail, lambda i: right(SG + i)),
    )
    fill_flat(flat_ref, -2, 2, *rows)
    fill_flat(flat_ref, TR - 2, TR + 2, *rows)
    shifted_copies(flat_ref, h_ref, 0, 2)
    shifted_copies(flat_ref, h_ref, place(TR - 2) - 32, 2)
    arrange_back(w2_ref, back_ref)
    at = place(-1) - 16
    got = back_rows(h_ref, at, PART, [back_ref[north_row], back_ref[1], back_ref[2]])
    hg_ref[at + 8 : at + PART - 8] = got[8:-8]
    at = place(TR - 1) - 16
    got = back_rows(h_ref, at, PART, [back_ref[0], back_ref[1], back_ref[south_row]])
    hg_ref[at + 8 : at + PART - 8] = got[8:-8]

    wide = spread_weights(embed_ref, wide_ref)
    up, down, left, right = edge(0)

    def embed_rows(part, first, last):
        block = lambda rows, k: rows[:, k * C : (k + 1) * C]
        up_, down_ = dot(up[part], wide), dot(down[part], wide)
        first, last = dot(first, wide), dot(last, wide)
        outer = {
            -1: jnp.where(north, block(up_, 0), block(up_, 3)),
            -2: jnp.where(north, block(up_, 1), block(up_, 2)),
            TR: jnp.where(south, block(down_, 3), block(down_, 0)),
            TR + 1: jnp.where(south, block(down_, 2), block(down_, 1)),
        }
        return lambda i: outer[i] if i in outer else block(first, i) if i < 4 else block(last, i - TR + 4)

    rows = (
        embed_rows(centre, s_ref[:, :128], s_ref[:, -128:]),
        embed_rows(pad, left(0), left(SG - 1)),
        embed_rows(tail, right(0), right(SG - 1)),
    )
    clear_flat(flat_ref, 0, 8)
    fill_flat(flat_ref, -2, 1, *rows)
    fill_flat(flat_ref, TR - 1, TR + 2, *rows)
    clear_flat(flat_ref, 8 + place(TR + 2), flat_ref.shape[0])
    shifted_copies(flat_ref, x_ref, 0, 1)
    shifted_copies(flat_ref, x_ref, place(TR) - 16, 1)

    def weights(w_ref, order):
        return [w_ref[r].reshape(3 * C, C) for r in order]

    def pre_body(k, carry):
        at = pl.multiple_of(FIRST + k * 3 * PART, 16)
        pre_ref[pl.ds(at, 3 * PART), :] = conv_rows(x_ref, at, 3 * PART, weights(w1_ref, (0, 1, 2)))
        return carry

    lax.fori_loop(0, 3, pre_body, 0)

    def pole_pre(at):
        got = conv_rows(x_ref, at, PITCH + 16, weights(w1_ref, (2, 1, 0)))
        pre_ref[at + 8 : at + PITCH + 8] = got[8:-8]

    @pl.when(north)
    def _():
        pole_pre(place(-1) - 16)

    @pl.when(south)
    def _():
        pole_pre(place(TR) - 16)

    flat_ref[8 + FIRST - 16 : 8 + FIRST] = jnp.zeros((16, C), F32)
    flat_ref[8 + FIRST + 9 * PART : 24 + FIRST + 9 * PART] = jnp.zeros((16, C), F32)

    def hidden_body(k, carry):
        at = pl.multiple_of(FIRST + k * PART, 16)
        pre = pre_ref[pl.ds(at, PART), :]
        flat_ref[pl.ds(at + 8, PART), :] = pre / (1.0 + jnp.exp(-pre))
        return carry

    lax.fori_loop(0, 9, hidden_body, 0)
    shifted_copies(flat_ref, h_ref, FIRST, 9)

    def field_body(k, carry):
        at = pl.multiple_of(OWN + k * WIDE * PITCH, 16)
        got = conv_rows(h_ref, at, WIDE * PITCH, weights(w2_ref, (0, 1, 2))).astype(BF16)
        for u in range(WIDE):
            field_ref[WIDE * k + u] = got[u * PITCH : u * PITCH + TC]
        return carry

    lax.fori_loop(0, TR // WIDE, field_body, 0)

    def weight_grad(src_ref, grad_t_ref, half):
        for r in range(3):
            at = OWN + (r - 1) * PITCH
            got = dot(grad_t_ref[...], src_ref[at : at + TR * PITCH]).astype(BF16)
            for s in range(3):
                to = (3 * r + s) * C
                red_ref[half, to : to + C] = got[:, s * C : (s + 1) * C]

    weight_grad(h_ref, cot_t_ref, 0)

    def grad_body(k, carry):
        at = pl.multiple_of(FIRST + k * PART, 16)
        pre = pre_ref[pl.ds(at, PART), :]
        sig = 1.0 / (1.0 + jnp.exp(-pre))
        flat_ref[pl.ds(at + 8, PART), :] = hg_ref[pl.ds(at, PART), :] * (sig * (1.0 + pre * (1.0 - sig)))
        return carry

    lax.fori_loop(0, 9, grad_body, 0)
    shifted_copies(flat_ref, h_ref, FIRST, 9)
    for i in range(TR):
        at = 8 + place(i)
        own_ref[i * PITCH : i * PITCH + TC] = flat_ref[at : at + TC].astype(BF16)
        own_ref[i * PITCH + TC : (i + 1) * PITCH] = jnp.zeros((PITCH - TC, C), BF16)
    transpose_flat(own_ref, own_t_ref)
    weight_grad(x_ref, own_t_ref, 1)

    arrange_back(w1_ref, back_ref)

    def eg_body(k, carry):
        at = pl.multiple_of(OWN + k * WIDE * PITCH, 16)
        got = back_rows(h_ref, at, WIDE * PITCH, [back_ref[0], back_ref[1], back_ref[2]])
        eg_ref[pl.ds(pl.multiple_of(k * WIDE * PITCH, 16), WIDE * PITCH), :] = got.astype(BF16)
        return carry

    lax.fori_loop(0, TR // WIDE, eg_body, 0)

    @pl.when(north)
    def _():
        got = back_rows(h_ref, OWN, PITCH, [back_ref[2], back_ref[1], back_ref[2]])
        eg_ref[:PITCH] = got.astype(BF16)

    @pl.when(south)
    def _():
        got = back_rows(h_ref, place(TR - 1), PITCH, [back_ref[0], back_ref[1], back_ref[0]])
        eg_ref[(TR - 1) * PITCH :] = got.astype(BF16)

    total = jnp.zeros((FEAT, C), F32)
    for g in range(TR // 4):
        s_t = s_ref[:, g * 128 : (g + 1) * 128].T
        for k in range(4):
            i = 4 * g + k
            total += dot(s_t[k * FEAT : (k + 1) * FEAT], eg_ref[i * PITCH : i * PITCH + TC])
    red_ref[0, 9 * C :] = jnp.zeros((FEAT, C), BF16)
    red_ref[1, 9 * C :] = total.astype(BF16)


def main(where, cot, s, halo, w_embed, w_first, w_second, cot_t, hg, x):
    vmem = pl.BlockSpec(memory_space=pltpu.VMEM)
    return pl.pallas_call(
        main_kernel,
        in_specs=[pl.BlockSpec(memory_space=pltpu.SMEM)] + [vmem] * 12,
        out_specs=[vmem] * 4,
        out_shape=[
            jax.ShapeDtypeStruct((TR, TC, C), BF16),
            jax.ShapeDtypeStruct((2, HALF, C), BF16),
            jax.ShapeDtypeStruct(hg.shape, hg.dtype),
            jax.ShapeDtypeStruct(x.shape, x.dtype),
        ],
        input_output_aliases={11: 2, 12: 3},
        scratch_shapes=[
            pltpu.VMEM((LEN + 16, C), F32),
            pltpu.VMEM((LEN, C), F32),
            pltpu.VMEM((LEN, 3 * C), BF16),
            pltpu.VMEM((3, C, 3 * C), BF16),
            pltpu.VMEM((TR * PITCH, C), BF16),
            pltpu.VMEM((C, TR * PITCH), BF16),
            pltpu.VMEM((TR * PITCH, C), BF16),
            pltpu.VMEM((4 * FEAT, 4 * C), F32),
        ],
        compiler_params=pltpu.CompilerParams(vmem_limit_bytes=32 << 20),
        cost_estimate=pl.CostEstimate(flops=8 << 30, bytes_accessed=6 << 20, transcendentals=1 << 20),
        name="main",
    )(where, cot, s, *halo, w_embed, w_first, w_second, cot_t, hg, x)


def unpack_kernel(where_ref, own_ref, other_ref, embed_ref, first_ref, second_ref):
    first_core = where_ref[1] % 2 == 0

    def half(k, at, rows):
        own, other = own_ref[at : at + rows], other_ref[at : at + rows]
        return jnp.where(first_core, own, other) if k == 0 else jnp.where(first_core, other, own)

    for r in range(3):
        for s in range(3):
            at = (3 * r + s) * C
            first_ref[r, s] = half(1, at, C).T.astype(F32)
            second_ref[r, s] = half(0, at, C).T.astype(F32)
    embed_ref[...] = half(1, 9 * C, FEAT)[: embed_ref.shape[0]].astype(F32)


def unpack(where, own, other, values):
    vmem = pl.BlockSpec(memory_space=pltpu.VMEM)
    return pl.pallas_call(
        unpack_kernel,
        in_specs=[pl.BlockSpec(memory_space=pltpu.SMEM), vmem, vmem],
        out_specs=[vmem] * 3,
        out_shape=[
            jax.ShapeDtypeStruct((values, C), F32),
            jax.ShapeDtypeStruct((3, 3, C, C), F32),
            jax.ShapeDtypeStruct((3, 3, C, C), F32),
        ],
        compiler_params=pltpu.CompilerParams(vmem_limit_bytes=16 << 20),
        name="unpack",
    )(where, own, other)


def swaps(bands, sectors):
    number = lambda lat, lon: lat * sectors + lon % sectors

    def across(lat, lon):
        if lat % 2:
            return number(lat + 1, lon) if lat < bands - 1 else number(lat, lon + sectors // 2)
        return number(lat - 1, lon) if lat > 0 else number(lat, lon + sectors // 2)

    def swap(of):
        pairs = [(number(i, j), of(i, j)) for i in range(bands) for j in range(sectors)]
        return lambda x: lax.ppermute(x, ALL, pairs)

    return (
        swap(lambda i, j: number(i, j ^ 1)),
        swap(lambda i, j: number(i, j + 1 if j % 2 else j - 1)),
        swap(lambda i, j: number(i ^ 1, j)),
        swap(across),
    )


def per_device(obs_values, tile_ids, obs_rows, obs_cols, w_embed, w_first, w_second, cotangent):
    bands, sectors = lax.axis_size("lat"), lax.axis_size("lon")
    owners = bands * sectors
    count, values = obs_values.shape
    where = jnp.stack(
        [lax.axis_index("lat"), lax.axis_index("lon"), jnp.int32(bands), jnp.int32(sectors)]
    ).astype(jnp.int32)
    swap_a, swap_b, swap_c, swap_d = swaps(bands, sectors)
    packed = pack(where, tile_ids.T, obs_rows.reshape(1, count), obs_cols.reshape(1, count), obs_values.T)
    got = lax.all_to_all(packed, ALL, 0, 0, tiled=True)
    s, a, b = setconv(where, got, cotangent)
    a, b = swap_a(a), swap_b(b)
    c, d = join(where, a, b, s, cotangent)
    hg, cot_t, x = mid(where, cotangent, s, a, b, w_second, w_embed)
    halo = (a, b, swap_c(c), swap_d(d))
    field, red, _, _ = main(where, cotangent, s, halo, w_embed, w_first, w_second, cot_t, hg, x)

    chips = owners // 2
    groups = [[2 * k + core for k in range(chips)] for core in range(2)]
    mine = lax.axis_index("lon") % 2
    theirs = swap_a(red)
    half = red[mine].astype(F32) + theirs[mine].astype(F32)
    half = jnp.pad(half.astype(BF16), ((0, chips * RED - HALF), (0, 0))).reshape(chips, RED, C)
    parts = lax.all_to_all(half, ALL, 0, 0, axis_index_groups=groups, tiled=True)
    summed = jnp.sum(parts.astype(F32), axis=0).astype(BF16)
    spread = jnp.broadcast_to(summed[None], (chips, RED, C))
    own = lax.all_to_all(spread, ALL, 0, 0, axis_index_groups=groups, tiled=True).reshape(chips * RED, C)
    other = swap_a(own)
    grad_embed, grad_first, grad_second = unpack(where, own, other, values)
    return (field, grad_embed, grad_first, grad_second)


def solution(mesh):
    in_specs = (
        P(ALL, None),
        P(ALL, None),
        P(ALL),
        P(ALL),
        P(),
        P(),
        P(),
        P("lat", "lon", None),
    )
    out_specs = (P("lat", "lon", None), P(), P(), P())
    return jax.shard_map(
        per_device, mesh=mesh, in_specs=in_specs, out_specs=out_specs, check_vma=False
    )
```

time: 137 us -> 121 us (0.88)
  blocking collectives: 45.1 us -> 61.8 us
  starting transfers between devices: 26.4 us -> 10.1 us
  Pallas kernels: 51.4 us -> 41 us
  waiting for transfers between devices: 10.3 us -> 6.57 us
  local copies, waits for them, and re-layouts: 2.06 us -> 0.11 us
    all_to_all x2 -> x3, blocking collectives: 45.1 us -> 61.8 us  [the longest x1 30.8 us: per_device(): got = lax.all_to_all(packed, ALL, 0, 0, tiled=True)]
    all_to_all x1 -> x0, starting transfers between devices: 11.5 us -> none  [per_device(): got = lax.all_to_all(packed, ALL, 0, 0, tiled=True)]
    pallas_call x5 -> x3, Pallas kernels: 13.3 us -> 6.45 us  [the longest x1 4.1 us: mid(): pl.pallas_call(mid_kernel, in_specs=[pl.BlockSpec(memory_space=pltpu.SMEM...]
    ppermute x8 -> x6, starting transfers between devices: 14.9 us -> 10.1 us  [swap(): return lambda x: lax.ppermute(x, ALL, pairs)]
    pallas_call x1, Pallas kernels: 17.1 us -> 12.8 us  [main(): pl.pallas_call(main_kernel, in_specs=[pl.BlockSpec(memory_space=pltpu.SME...]
    ppermute x8 -> x6, waiting for transfers between devices: 10.3 us -> 6.57 us  [swap(): return lambda x: lax.ppermute(x, ALL, pairs)]
    unnamed x33 -> x10, local copies, waits for them, and re-layouts: 1.96 us -> 0.02 us
  transfers between devices with their start and end apart: 9 -> 6, of which waited for: 4 -> 4; matrix products, arithmetic and copies ran while one was open for 1% -> 0% of each run, Pallas kernels for 12% -> 3%
where the time goes in v3:
time: 121 us
  blocking collectives  61.8 us (51%)
  Pallas kernels  41 us (34%)
  starting transfers between devices  10.1 us (8%)
  waiting for transfers between devices  6.57 us (5%)
    all_to_all x1, blocking collectives, per_device(): got = lax.all_to_all(packed, ALL, 0, 0, tiled=True)  30.8 us
    all_to_all x1, blocking collectives, per_device(): lax.all_to_all(half, ALL, 0, 0, axis_index_groups=groups, tiled=True)  16.6 us
    pallas_call x1, Pallas kernels, pack(): pl.pallas_call(pack_kernel, grid=(steps,), in_specs=[pl.BlockSpec(memory_...  16 us
    all_to_all x1, blocking collectives, per_device(): lax.all_to_all(spread, ALL, 0, 0, axis_index_groups=groups, tiled=True)  14.4 us
    pallas_call x1, Pallas kernels, main(): pl.pallas_call(main_kernel, in_specs=[pl.BlockSpec(memory_space=pltpu.SME...  12.8 us
    ppermute x6, starting transfers between devices, swap(): return lambda x: lax.ppermute(x, ALL, pairs)  10.1 us
    ppermute x6, waiting for transfers between devices, swap(): return lambda x: lax.ppermute(x, ALL, pairs)  6.57 us
    pallas_call x1, Pallas kernels, setconv(): pl.pallas_call(setconv_kernel, grid=(steps,), in_specs=[pl.BlockSpec(memo...  5.8 us
  transfers between devices with their start and end apart: 6, of which 4 were waited for; matrix products, arithmetic and copies ran while one was open for 0% of the time, Pallas kernels for 3%

profile of v3, /device:TPU:1, one launch (start us, length us, event | category | flops | bytes accessed | tf_op | source)
XLA Modules:
  0.0 121.1 jit_solution(13248651123309302313)
XLA Ops:
  0.6 0.6 pad_add_fusion.where_ref
  1.2 0.0 copy-start
  1.2 0.0 copy-start.1
  1.2 16.0 %pack.1 = bf16[128,32,128]{2,1,0:T(8,128)(2,1)} custom-call(s32[4]{0:T(128)} %pad_add_fusion.where_ref, s32[1,8192]{1,0:T(1,128)} %bitcast.14, f32[1,8192]{1,0:T(1,128)} %bitcast.15, f32[1,8192]{1,0:T(1,128)} %bitcast.16, bf16[24,8192]{1,0:T(8,128)(2,1)} %bitcast.13), custom_call_target="tpu_custom_call" | custom-call | flops 8589934592 | bytes 3145728 | tf_op jit(solution)/shard_map/pack/pallas_call | solution.py:111
  17.2 30.8 %all_to_all.15.got_ref = bf16[128,32,128]{2,1,0:T(8,128)(2,1)S(1)} all-to-all(bf16[128,32,128]{2,1,0:T(8,128)(2,1)} %pack.1), channel_id=1, replica_groups=mesh['lat'=8,'lon'=16] {'lat','lon'}, dimensions={0} | all-to-all | bytes 2097152 | tf_op jit(solution)/shard_map/all_to_all | solution.py:605
  48.1 0.0 copy-done
  48.1 0.0 copy-done.1
  48.1 0.0 copy-start.3
  48.1 0.0 copy-start.4
  48.1 5.8 %setconv.1 = (bf16[128,512]{1,0:T(8,128)(2,1)S(1)}, bf16[20,16,128]{2,1,0:T(8,128)(2,1)S(1)}, bf16[20,16,128]{2,1,0:T(8,128)(2,1)S(1)}) custom-call(s32[4]{0:T(128)S(1)} %copy-done.1, bf16[128,32,128]{2,1,0:T(8,128)(2,1)S(1)} %all_to_all.15.got_ref, bf16[16,128,128]{2,1,0:T(8,128)(2,1)S(1)} %copy-done), custom_call_target="tpu_custom_call" | custom-call | flops 3221225472 | bytes 2097152 | tf_op jit(solution)/shard_map/setconv/pallas_call | solution.py:180
  53.9 0.7 collective-permute-start
  54.6 0.3 collective-permute-start.1
  54.9 0.6 collective-permute-done.a_ref
  55.5 2.9 %collective-permute-done.1.b_ref = bf16[20,16,128]{2,1,0:T(8,128)(2,1)S(1)} collective-permute-done((bf16[20,16,128]{2,1,0:T(8,128)(2,1)S(1)}, bf16[20,16,128]{2,1,0:T(8,128)(2,1)S(1)}, u32[]{:S(2)}, u32[]{:S(2)}) %collective-permute-start.1) | collective-permute-done | bytes 81952 | tf_op jit(solution)/shard_map/ppermute | solution.py:586
  58.4 0.6 join.1
  59.0 1.2 collective-permute-start.2
  60.3 0.0 copy-start.2
  60.3 1.5 %collective-permute-start.3 = (bf16[3,160,128]{2,1,0:T(8,128)(2,1)S(1)}, bf16[3,160,128]{2,1,0:T(8,128)(2,1)S(1)}, u32[]{:S(2)}, u32[]{:S(2)}) collective-permute-start(bf16[3,160,128]{2,1,0:T(8,128)(2,1)S(1)} %get-tuple-element.21), channel_id=1, source_target_pairs={{0,8},{1,9},{2,10},{3,11},{4,12},{5,13},{6,14},{7,15},{8,0},{9,1},... | collective-permute-start | bytes 368648 | tf_op jit(solution)/shard_map/ppermute | solution.py:586
  61.7 0.0 copy-done.3
  61.7 0.0 copy-done.4
  61.7 4.1 %mid.1 = (f32[3040,128]{1,0:T(8,128)S(1)}, bf16[128,2304]{1,0:T(8,128)(2,1)S(1)}, bf16[3040,384]{1,0:T(8,128)(2,1)S(1)}) custom-call(s32[4]{0:T(128)S(1)} %copy-done.1, bf16[16,128,128]{2,1,0:T(8,128)(2,1)S(1)} %copy-done, bf16[128,512]{1,0:T(8,128)(2,1)S(1)} %get-tuple-element.17.s_ref, bf16[20,16,128]{2,1,0:T(8,128)(2,1)S(1)} %collective-permute-done.a_ref, ...), custom_call_target="tpu_custom_call" | custom-call | flops 1613758464 | bytes 4194304 | tf_op jit(solution)/shard_map/mid/pallas_call | solution.py:325
  65.9 0.0 collective-permute-done.2.c_ref
  65.9 0.0 collective-permute-done.3.d_ref
  65.9 0.0 copy-done.2
  65.9 12.8 %main.1 = (bf16[16,128,128]{2,1,0:T(8,128)(2,1)}, bf16[2,1184,128]{2,1,0:T(8,128)(2,1)S(1)}, f32[3040,128]{1,0:T(8,128)S(1)}, bf16[3040,384]{1,0:T(8,128)(2,1)S(1)}) custom-call(s32[4]{0:T(128)S(1)} %copy-done.1, bf16[16,128,128]{2,1,0:T(8,128)(2,1)S(1)} %copy-done, ...), custom_call_target="tpu_custom_call", output_to_operand_aliasing={{2}: (11, {}), {3}: (12, {})} | custom-call | flops 8589934592 | bytes 6291456 | tf_op jit(solution)/shard_map/main/pallas_call | solution.py:518
  78.7 3.2 %collective-permute-start.4 = (bf16[2,1184,128]{2,1,0:T(8,128)(2,1)S(1)}, bf16[2,1184,128]{2,1,0:T(8,128)(2,1)S(1)}, u32[]{:S(2)}, u32[]{:S(2)}) collective-permute-start(bf16[2,1184,128]{2,1,0:T(8,128)(2,1)S(1)} %get-tuple-element.26), channel_id=1, source_target_pairs={{0,1},{1,0},{2,3},{3,2},{4,5},{5,4},{6,7},{7,6},{8,9},{9,8},{10,11... | collective-permute-start | bytes 1818632 | tf_op jit(solution)/shard_map/ppermute | solution.py:586
  81.9 1.7 %collective-permute-done.4 = bf16[2,1184,128]{2,1,0:T(8,128)(2,1)S(1)} collective-permute-done((bf16[2,1184,128]{2,1,0:T(8,128)(2,1)S(1)}, bf16[2,1184,128]{2,1,0:T(8,128)(2,1)S(1)}, u32[]{:S(2)}, u32[]{:S(2)}) %collective-permute-start.4) | collective-permute-done | bytes 606240 | tf_op jit(solution)/shard_map/ppermute | solution.py:586
  83.5 0.1 fusion
  83.7 16.6 %all_to_all.16 = bf16[64,24,128]{2,1,0:T(8,128)(2,1)S(1)} all-to-all(bf16[64,24,128]{2,1,0:T(8,128)(2,1)S(1)} %bitcast.12), channel_id=1, replica_groups={{0,2,4,6,8,10,12,14,16,18,20,22,24,26,28,30,32,34,36,38,40,42,44,46,48,..., dimensions={0} | all-to-all | bytes 786432 | tf_op jit(solution)/shard_map/all_to_all | solution.py:619
  100.2 0.1 reduce_sum.12
  100.3 0.1 broadcast_in_dim.2
  100.4 14.4 %all_to_all.17 = bf16[64,24,128]{2,1,0:T(8,128)(2,1)S(1)} all-to-all(bf16[64,24,128]{2,1,0:T(8,128)(2,1)S(1)} %broadcast_in_dim.2), channel_id=1, replica_groups={{0,2,4,6,8,10,12,14,16,18,20,22,24,26,28,30,32,34,36,38,40,42,44,46,48,..., dimensions={0} | all-to-all | bytes 786432 | tf_op jit(solution)/shard_map/all_to_all | solution.py:622
  114.7 3.2 %collective-permute-start.5 = (bf16[1536,128]{1,0:T(8,128)(2,1)S(1)}, bf16[1536,128]{1,0:T(8,128)(2,1)S(1)}, u32[]{:S(2)}, u32[]{:S(2)}) collective-permute-start(bf16[1536,128]{1,0:T(8,128)(2,1)S(1)} %bitcast.10), channel_id=1, source_target_pairs={{0,1},{1,0},{2,3},{3,2},{4,5},{5,4},{6,7},{7,6},{8,9},{9,8},{10,11... | collective-permute-start | bytes 1179656 | tf_op jit(solution)/shard_map/ppermute | solution.py:586
  118.0 1.3 %collective-permute-done.5.other_ref = bf16[1536,128]{1,0:T(8,128)(2,1)S(1)} collective-permute-done((bf16[1536,128]{1,0:T(8,128)(2,1)S(1)}, bf16[1536,128]{1,0:T(8,128)(2,1)S(1)}, u32[]{:S(2)}, u32[]{:S(2)}) %collective-permute-start.5) | collective-permute-done | bytes 393248 | tf_op jit(solution)/shard_map/ppermute | solution.py:586
  119.3 1.7 %unpack.1 = (f32[24,128]{1,0:T(8,128)}, f32[3,3,128,128]{3,2,1,0:T(8,128)}, f32[3,3,128,128]{3,2,1,0:T(8,128)}) custom-call(s32[4]{0:T(128)S(1)} %copy-done.1, bf16[1536,128]{1,0:T(8,128)(2,1)S(1)} %bitcast.11, bf16[1536,128]{1,0:T(8,128)(2,1)S(1)} %collective-permute-done.5.other_ref), custom_call_target="tpu_custom_call" | custom-call | tf_op jit(solution)/shard_map/unpack/pallas_call | solution.py:562
  (1 shorter events, 0.0 us)
Async XLA Ops:
  1.2 46.8 %copy-start = (bf16[16,128,128]{2,1,0:T(8,128)(2,1)S(1)}, bf16[16,128,128]{2,1,0:T(8,128)(2,1)}, u32[]{:S(2)}) copy-start(bf16[16,128,128]{2,1,0:T(8,128)(2,1)} %cot_ref.7) | copy-start | bytes 1572868
  1.2 46.8 %copy-start.1 = (s32[4]{0:T(128)S(1)}, s32[4]{0:T(128)}, u32[]{:S(2)}) copy-start(s32[4]{0:T(128)} %pad_add_fusion.where_ref) | copy-start | bytes 52
  48.1 13.7 %copy-start.3 = (bf16[3,3,128,128]{3,2,1,0:T(8,128)(2,1)S(1)}, bf16[3,3,128,128]{3,2,1,0:T(8,128)(2,1)}, u32[]{:S(2)}) copy-start(bf16[3,3,128,128]{3,2,1,0:T(8,128)(2,1)} %w2_ref.1) | copy-start | bytes 884740
  48.1 13.7 %copy-start.4 = (bf16[24,128]{1,0:T(8,128)(2,1)S(1)}, bf16[24,128]{1,0:T(8,128)(2,1)}, u32[]{:S(2)}) copy-start(bf16[24,128]{1,0:T(8,128)(2,1)} %embed_ref.3) | copy-start | bytes 18436
  53.9 1.6 %collective-permute-start = (bf16[20,16,128]{2,1,0:T(8,128)(2,1)S(1)}, bf16[20,16,128]{2,1,0:T(8,128)(2,1)S(1)}, u32[]{:S(2)}, u32[]{:S(2)}) collective-permute-start(bf16[20,16,128]{2,1,0:T(8,128)(2,1)S(1)} %get-tuple-element.18), channel_id=1, source_target_pairs={{0,1},{1,0},{2,3},{3,2},{4,5},{5,4},{6,7},{7,6},{8,9},{9,8},{10,11... | collective-permute-start | bytes 245768 | tf_op jit(solution)/shard_map/ppermute | solution.py:586
  54.6 3.9 %collective-permute-start.1 = (bf16[20,16,128]{2,1,0:T(8,128)(2,1)S(1)}, bf16[20,16,128]{2,1,0:T(8,128)(2,1)S(1)}, u32[]{:S(2)}, u32[]{:S(2)}) collective-permute-start(bf16[20,16,128]{2,1,0:T(8,128)(2,1)S(1)} %get-tuple-element.19), channel_id=1, source_target_pairs={{0,15},{1,2},{2,1},{3,4},{4,3},{5,6},{6,5},{7,8},{8,7},{9,10},{10,... | collective-permute-start | bytes 245768 | tf_op jit(solution)/shard_map/ppermute | solution.py:586
  59.0 6.8 %collective-permute-start.2 = (bf16[3,160,128]{2,1,0:T(8,128)(2,1)S(1)}, bf16[3,160,128]{2,1,0:T(8,128)(2,1)S(1)}, u32[]{:S(2)}, u32[]{:S(2)}) collective-permute-start(bf16[3,160,128]{2,1,0:T(8,128)(2,1)S(1)} %get-tuple-element.20), channel_id=1, source_target_pairs={{0,16},{1,17},{2,18},{3,19},{4,20},{5,21},{6,22},{7,23},{8,24},{9,... | collective-permute-start | bytes 368648 | tf_op jit(solution)/shard_map/ppermute | solution.py:586
  60.3 5.6 %copy-start.2 = (bf16[3,3,128,128]{3,2,1,0:T(8,128)(2,1)S(1)}, bf16[3,3,128,128]{3,2,1,0:T(8,128)(2,1)}, u32[]{:S(2)}) copy-start(bf16[3,3,128,128]{3,2,1,0:T(8,128)(2,1)} %w1_ref.1) | copy-start | bytes 884740
  60.3 5.6 %collective-permute-start.3 = (bf16[3,160,128]{2,1,0:T(8,128)(2,1)S(1)}, bf16[3,160,128]{2,1,0:T(8,128)(2,1)S(1)}, u32[]{:S(2)}, u32[]{:S(2)}) collective-permute-start(bf16[3,160,128]{2,1,0:T(8,128)(2,1)S(1)} %get-tuple-element.21), channel_id=1, source_target_pairs={{0,8},{1,9},{2,10},{3,11},{4,12},{5,13},{6,14},{7,15},{8,0},{9,1},... | collective-permute-start | bytes 368648 | tf_op jit(solution)/shard_map/ppermute | solution.py:586
  78.7 4.9 %collective-permute-start.4 = (bf16[2,1184,128]{2,1,0:T(8,128)(2,1)S(1)}, bf16[2,1184,128]{2,1,0:T(8,128)(2,1)S(1)}, u32[]{:S(2)}, u32[]{:S(2)}) collective-permute-start(bf16[2,1184,128]{2,1,0:T(8,128)(2,1)S(1)} %get-tuple-element.26), channel_id=1, source_target_pairs={{0,1},{1,0},{2,3},{3,2},{4,5},{5,4},{6,7},{7,6},{8,9},{9,8},{10,11... | collective-permute-start | bytes 1818632 | tf_op jit(solution)/shard_map/ppermute | solution.py:586
  114.7 4.6 %collective-permute-start.5 = (bf16[1536,128]{1,0:T(8,128)(2,1)S(1)}, bf16[1536,128]{1,0:T(8,128)(2,1)S(1)}, u32[]{:S(2)}, u32[]{:S(2)}) collective-permute-start(bf16[1536,128]{1,0:T(8,128)(2,1)S(1)} %bitcast.10), channel_id=1, source_target_pairs={{0,1},{1,0},{2,3},{3,2},{4,5},{5,4},{6,7},{7,6},{8,9},{9,8},{10,11... | collective-permute-start | bytes 1179656 | tf_op jit(solution)/shard_map/ppermute | solution.py:586

commit v4 on v3

--- a/solution.py
+++ b/solution.py
@@ -37,7 +37,7 @@
     return 16 + (i + 2) * PITCH
 
 
-def pack_kernel(where_ref, ids_hbm, rows_hbm, cols_hbm, vals_hbm, out_ref,
+def pack_kernel(ids_hbm, rows_hbm, cols_hbm, vals_hbm, out_ref,
                 ids_ref, rows_ref, cols_ref, vals_ref, q_ref, v_ref, pair_ref, acc_ref, sems):
     step = pl.program_id(0)
     count = ids_ref.shape[1]
@@ -62,6 +62,12 @@
         upto = jnp.concatenate(
             [jnp.where(upto, 1.0, 0.0).astype(BF16), jnp.ones((sub, 128), BF16)], axis=1
         )
+        slot = slot.astype(F32).astype(BF16)
+        one, none = jnp.ones((sub, sub), BF16), jnp.zeros((sub, sub), BF16)
+
+        def rows_of_16(row, rows):
+            return jnp.concatenate([jnp.broadcast_to(row, (16, sub)).astype(BF16)] * (rows // 16), axis=0)
+
         for move in moves:
             move.wait()
 
@@ -73,9 +79,9 @@
                 counted = dot(jnp.where(hot, 1.0, 0.0).astype(BF16), upto)
                 before = counted[:, :sub] + jnp.concatenate([carry, carry], axis=1)
                 rank = jnp.sum(jnp.where(hot, before, 0.0), axis=0, keepdims=True) - 1.0
-                key = rank.astype(jnp.int32) + (ids & 1) * 128
-                q_ref[:, at] = jnp.where(slot == key, 1.0, 0.0).astype(BF16)
-                pair_ref[:, at] = jnp.broadcast_to((ids >> 1).astype(F32), (FEAT, sub)).astype(BF16)
+                key = rank + ((ids & 1) * 128).astype(F32)
+                q_ref[:, at] = jnp.where(slot == rows_of_16(key, sub), one, none)
+                pair_ref[:, at] = rows_of_16((ids >> 1).astype(F32), FEAT)
                 rows, cols = rows_ref[:, at], cols_ref[:, at]
                 rows_hi, cols_hi = rows.astype(BF16).astype(F32), cols.astype(BF16).astype(F32)
                 tail = jnp.concatenate(
@@ -104,14 +110,14 @@
         out_ref[2 * p + 1] = acc_ref[p * FEAT : (p + 1) * FEAT, 128:].astype(BF16)
 
 
-def pack(where, ids, rows, cols, values):
+def pack(ids, rows, cols, values):
     count = ids.shape[1]
     owners = 128
     steps = 4
     return pl.pallas_call(
         pack_kernel,
         grid=(steps,),
-        in_specs=[pl.BlockSpec(memory_space=pltpu.SMEM)] + [pl.BlockSpec(memory_space=pl.ANY)] * 4,
+        in_specs=[pl.BlockSpec(memory_space=pl.ANY)] * 4,
         out_specs=pl.BlockSpec((owners // steps, FEAT, 128), lambda i: (i, 0, 0)),
         out_shape=jax.ShapeDtypeStruct((owners, FEAT, 128), BF16),
         scratch_shapes=[
@@ -128,7 +134,7 @@
         compiler_params=pltpu.CompilerParams(vmem_limit_bytes=58 << 20),
         cost_estimate=pl.CostEstimate(flops=2 * 2048 * 256 * 8192, bytes_accessed=3 << 20, transcendentals=0),
         name="pack",
-    )(where, ids, rows, cols, values)
+    )(ids, rows, cols, values)
 
 
 def setconv_kernel(where_ref, got_ref, cot_ref, s_ref, a_ref, b_ref, acc_ref):
@@ -173,7 +179,7 @@
 
 
 def setconv(where, got, cot):
-    steps = 8
+    steps = 4
     fixed = lambda *shape: pl.BlockSpec(shape, lambda i: (0,) * len(shape))
     lanes = TR * FEAT
     shapes = [(TC, lanes), (SG + TR, 16, C), (SG + TR, 16, C)]
@@ -271,8 +277,41 @@
             out_ref[r, :, s * C : (s + 1) * C] = w_ref[2 - r, 2 - s]
 
 
-def mid_kernel(where_ref, cot_ref, s_ref, a_ref, b_ref, w_ref, embed_ref,
-               hg_ref, cot_t_ref, x_ref, flat_ref, copies_ref, back_ref, own_ref, wide_ref):
+def prep_kernel(cot_ref, embed_ref, w1_ref, w2_ref, cot_t_ref, wide_ref, back1_ref, back2_ref, own_ref):
+    for i in range(TR):
+        own_ref[i * PITCH : i * PITCH + TC] = cot_ref[i]
+        own_ref[i * PITCH + TC : (i + 1) * PITCH] = jnp.zeros((PITCH - TC, C), BF16)
+    transpose_flat(own_ref, cot_t_ref)
+    values = embed_ref.shape[0]
+    padded = jnp.concatenate([embed_ref[...].astype(F32), jnp.zeros((FEAT - values, C), F32)], axis=0).astype(BF16)
+    wide_ref[...] = jnp.zeros_like(wide_ref)
+    for k in range(4):
+        wide_ref[k * FEAT : (k + 1) * FEAT, k * C : (k + 1) * C] = padded
+    arrange_back(w1_ref, back1_ref)
+    arrange_back(w2_ref, back2_ref)
+
+
+def prep(cot, w_embed, w_first, w_second):
+    vmem = pl.BlockSpec(memory_space=pltpu.VMEM)
+    return pl.pallas_call(
+        prep_kernel,
+        in_specs=[vmem] * 4,
+        out_specs=[vmem] * 4,
+        out_shape=[
+            jax.ShapeDtypeStruct((C, TR * PITCH), BF16),
+            jax.ShapeDtypeStruct((4 * FEAT, 4 * C), BF16),
+            jax.ShapeDtypeStruct((3, C, 3 * C), BF16),
+            jax.ShapeDtypeStruct((3, C, 3 * C), BF16),
+        ],
+        scratch_shapes=[pltpu.VMEM((TR * PITCH, C), BF16)],
+        compiler_params=pltpu.CompilerParams(vmem_limit_bytes=16 << 20),
+        cost_estimate=pl.CostEstimate(flops=1 << 20, bytes_accessed=4 << 20, transcendentals=0),
+        name="prep",
+    )(cot, w_embed, w_first, w_second)
+
+
+def mid_kernel(where_ref, cot_ref, s_ref, a_ref, b_ref, back_ref, wide_ref, w1_ref,
+               hg_ref, x_ref, pre_ref, flat_ref, copies_ref):
     even_lon, _ = evens(where_ref)
     left = jnp.where(even_lon, b_ref[SG:], a_ref[SG:])
     right = jnp.where(even_lon, a_ref[SG:], b_ref[SG:])
@@ -281,7 +320,6 @@
     clear_flat(flat_ref, 8 + place(TR), flat_ref.shape[0])
     fill_flat(flat_ref, 0, TR, row(cot_ref), row(left), row(right))
     shifted_copies(flat_ref, copies_ref, 0, LEN // PART)
-    arrange_back(w_ref, back_ref)
 
     def body(k, carry):
         at = pl.multiple_of(FIRST + k * 3 * PART, 16)
@@ -290,12 +328,7 @@
 
     lax.fori_loop(0, 3, body, 0)
 
-    for i in range(TR):
-        own_ref[i * PITCH : i * PITCH + TC] = cot_ref[i]
-        own_ref[i * PITCH + TC : (i + 1) * PITCH] = jnp.zeros((PITCH - TC, C), BF16)
-    transpose_flat(own_ref, cot_t_ref)
-
-    wide = spread_weights(embed_ref, wide_ref)
+    wide = wide_ref[...]
 
     def rows_of(groups):
         groups = [dot(group, wide) for group in groups]
@@ -307,47 +340,44 @@
     fill_flat(flat_ref, 0, TR, centre, left, right)
     shifted_copies(flat_ref, x_ref, 0, LEN // PART)
 
-
-def spread_weights(embed_ref, wide_ref):
-    values = embed_ref.shape[0]
-    wide_ref[...] = jnp.zeros_like(wide_ref)
-    for k in range(4):
-        wide_ref[k * FEAT : k * FEAT + values, k * C : (k + 1) * C] = embed_ref[...].astype(F32)
-    return wide_ref[...].astype(BF16)
+    def pre_body(k, carry):
+        at = pl.multiple_of(FIRST + k * 3 * PART, 16)
+        pre_ref[pl.ds(at, 3 * PART), :] = conv_rows(x_ref, at, 3 * PART, taps(w1_ref, (0, 1, 2)))
+        return carry
+
+    lax.fori_loop(0, 3, pre_body, 0)
+
+
+def taps(w_ref, order):
+    return [w_ref[r].reshape(3 * C, C) for r in order]
 
 
 def transpose_flat(own_ref, out_ref):
     out_ref[...] = own_ref[...].T
 
 
-def mid(where, cot, s, a, b, w_second, w_embed):
+def mid(where, cot, s, a, b, back, wide, w_first):
     vmem = pl.BlockSpec(memory_space=pltpu.VMEM)
     return pl.pallas_call(
         mid_kernel,
-        in_specs=[pl.BlockSpec(memory_space=pltpu.SMEM)] + [vmem] * 6,
+        in_specs=[pl.BlockSpec(memory_space=pltpu.SMEM)] + [vmem] * 7,
         out_specs=[vmem] * 3,
         out_shape=[
             jax.ShapeDtypeStruct((LEN, C), F32),
-            jax.ShapeDtypeStruct((C, TR * PITCH), BF16),
             jax.ShapeDtypeStruct((LEN, 3 * C), BF16),
+            jax.ShapeDtypeStruct((LEN, C), F32),
         ],
-        scratch_shapes=[
-            pltpu.VMEM((LEN + 16, C), F32),
-            pltpu.VMEM((LEN, 3 * C), BF16),
-            pltpu.VMEM((3, C, 3 * C), BF16),
-            pltpu.VMEM((TR * PITCH, C), BF16),
-            pltpu.VMEM((4 * FEAT, 4 * C), F32),
-        ],
+        scratch_shapes=[pltpu.VMEM((LEN + 16, C), F32), pltpu.VMEM((LEN, 3 * C), BF16)],
         compiler_params=pltpu.CompilerParams(vmem_limit_bytes=24 << 20),
         cost_estimate=pl.CostEstimate(flops=2 * 2736 * 1152 * 256, bytes_accessed=4 << 20, transcendentals=0),
         name="mid",
-    )(where, cot, s, a, b, w_second, w_embed)
+    )(where, cot, s, a, b, back, wide, w_first)
 
 
 def main_kernel(where_ref, cot_ref, s_ref, a_ref, b_ref, c_ref, d_ref,
-                embed_ref, w1_ref, w2_ref, cot_t_ref, hg_in, x_in,
-                field_ref, red_ref, hg_ref, x_ref,
-                flat_ref, pre_ref, h_ref, back_ref, own_ref, own_t_ref, eg_ref, wide_ref):
+                wide_ref, w1_ref, w2_ref, back1_ref, back2_ref, cot_t_ref, hg_in, x_in, pre_in,
+                field_ref, red_ref, hg_ref, x_ref, pre_ref,
+                flat_ref, h_ref, own_ref, own_t_ref, eg_ref):
     even_lon, even_lat = evens(where_ref)
     north = where_ref[0] == 0
     south = where_ref[0] == where_ref[2] - 1
@@ -379,15 +409,14 @@
     fill_flat(flat_ref, TR - 2, TR + 2, *rows)
     shifted_copies(flat_ref, h_ref, 0, 2)
     shifted_copies(flat_ref, h_ref, place(TR - 2) - 32, 2)
-    arrange_back(w2_ref, back_ref)
     at = place(-1) - 16
-    got = back_rows(h_ref, at, PART, [back_ref[north_row], back_ref[1], back_ref[2]])
+    got = back_rows(h_ref, at, PART, [back2_ref[north_row], back2_ref[1], back2_ref[2]])
     hg_ref[at + 8 : at + PART - 8] = got[8:-8]
     at = place(TR - 1) - 16
-    got = back_rows(h_ref, at, PART, [back_ref[0], back_ref[1], back_ref[south_row]])
+    got = back_rows(h_ref, at, PART, [back2_ref[0], back2_ref[1], back2_ref[south_row]])
     hg_ref[at + 8 : at + PART - 8] = got[8:-8]
 
-    wide = spread_weights(embed_ref, wide_ref)
+    wide = wide_ref[...]
     up, down, left, right = edge(0)
 
     def embed_rows(part, first, last):
@@ -414,18 +443,12 @@
     shifted_copies(flat_ref, x_ref, 0, 1)
     shifted_copies(flat_ref, x_ref, place(TR) - 16, 1)
 
-    def weights(w_ref, order):
-        return [w_ref[r].reshape(3 * C, C) for r in order]
-
-    def pre_body(k, carry):
-        at = pl.multiple_of(FIRST + k * 3 * PART, 16)
-        pre_ref[pl.ds(at, 3 * PART), :] = conv_rows(x_ref, at, 3 * PART, weights(w1_ref, (0, 1, 2)))
-        return carry
-
-    lax.fori_loop(0, 3, pre_body, 0)
+    for at in (place(-1) - 16, place(TR - 1) - 16):
+        got = conv_rows(x_ref, at, PART, taps(w1_ref, (0, 1, 2)))
+        pre_ref[at + 8 : at + PART - 8] = got[8:-8]
 
     def pole_pre(at):
-        got = conv_rows(x_ref, at, PITCH + 16, weights(w1_ref, (2, 1, 0)))
+        got = conv_rows(x_ref, at, PITCH + 16, taps(w1_ref, (2, 1, 0)))
         pre_ref[at + 8 : at + PITCH + 8] = got[8:-8]
 
     @pl.when(north)
@@ -450,7 +473,7 @@
 
     def field_body(k, carry):
         at = pl.multiple_of(OWN + k * WIDE * PITCH, 16)
-        got = conv_rows(h_ref, at, WIDE * PITCH, weights(w2_ref, (0, 1, 2))).astype(BF16)
+        got = conv_rows(h_ref, at, WIDE * PITCH, taps(w2_ref, (0, 1, 2))).astype(BF16)
         for u in range(WIDE):
             field_ref[WIDE * k + u] = got[u * PITCH : u * PITCH + TC]
         return carry
@@ -483,11 +506,10 @@
     transpose_flat(own_ref, own_t_ref)
     weight_grad(x_ref, own_t_ref, 1)
 
-    arrange_back(w1_ref, back_ref)
 
     def eg_body(k, carry):
         at = pl.multiple_of(OWN + k * WIDE * PITCH, 16)
-        got = back_rows(h_ref, at, WIDE * PITCH, [back_ref[0], back_ref[1], back_ref[2]])
+        got = back_rows(h_ref, at, WIDE * PITCH, [back1_ref[0], back1_ref[1], back1_ref[2]])
         eg_ref[pl.ds(pl.multiple_of(k * WIDE * PITCH, 16), WIDE * PITCH), :] = got.astype(BF16)
         return carry
 
@@ -495,12 +517,12 @@
 
     @pl.when(north)
     def _():
-        got = back_rows(h_ref, OWN, PITCH, [back_ref[2], back_ref[1], back_ref[2]])
+        got = back_rows(h_ref, OWN, PITCH, [back1_ref[2], back1_ref[1], back1_ref[2]])
         eg_ref[:PITCH] = got.astype(BF16)
 
     @pl.when(south)
     def _():
-        got = back_rows(h_ref, place(TR - 1), PITCH, [back_ref[0], back_ref[1], back_ref[0]])
+        got = back_rows(h_ref, place(TR - 1), PITCH, [back1_ref[0], back1_ref[1], back1_ref[0]])
         eg_ref[(TR - 1) * PITCH :] = got.astype(BF16)
 
     total = jnp.zeros((FEAT, C), F32)
@@ -513,33 +535,31 @@
     red_ref[1, 9 * C :] = total.astype(BF16)
 
 
-def main(where, cot, s, halo, w_embed, w_first, w_second, cot_t, hg, x):
+def main(where, cot, s, halo, wide, w_first, w_second, back1, back2, cot_t, hg, x, pre):
     vmem = pl.BlockSpec(memory_space=pltpu.VMEM)
     return pl.pallas_call(
         main_kernel,
-        in_specs=[pl.BlockSpec(memory_space=pltpu.SMEM)] + [vmem] * 12,
-        out_specs=[vmem] * 4,
+        in_specs=[pl.BlockSpec(memory_space=pltpu.SMEM)] + [vmem] * 15,
+        out_specs=[vmem] * 5,
         out_shape=[
             jax.ShapeDtypeStruct((TR, TC, C), BF16),
             jax.ShapeDtypeStruct((2, HALF, C), BF16),
             jax.ShapeDtypeStruct(hg.shape, hg.dtype),
             jax.ShapeDtypeStruct(x.shape, x.dtype),
+            jax.ShapeDtypeStruct(pre.shape, pre.dtype),
         ],
-        input_output_aliases={11: 2, 12: 3},
+        input_output_aliases={13: 2, 14: 3, 15: 4},
         scratch_shapes=[
             pltpu.VMEM((LEN + 16, C), F32),
-            pltpu.VMEM((LEN, C), F32),
             pltpu.VMEM((LEN, 3 * C), BF16),
-            pltpu.VMEM((3, C, 3 * C), BF16),
             pltpu.VMEM((TR * PITCH, C), BF16),
             pltpu.VMEM((C, TR * PITCH), BF16),
             pltpu.VMEM((TR * PITCH, C), BF16),
-            pltpu.VMEM((4 * FEAT, 4 * C), F32),
         ],
         compiler_params=pltpu.CompilerParams(vmem_limit_bytes=32 << 20),
         cost_estimate=pl.CostEstimate(flops=8 << 30, bytes_accessed=6 << 20, transcendentals=1 << 20),
         name="main",
-    )(where, cot, s, *halo, w_embed, w_first, w_second, cot_t, hg, x)
+    )(where, cot, s, *halo, wide, w_first, w_second, back1, back2, cot_t, hg, x, pre)
 
 
 def unpack_kernel(where_ref, own_ref, other_ref, embed_ref, first_ref, second_ref):
@@ -601,14 +621,15 @@
         [lax.axis_index("lat"), lax.axis_index("lon"), jnp.int32(bands), jnp.int32(sectors)]
     ).astype(jnp.int32)
     swap_a, swap_b, swap_c, swap_d = swaps(bands, sectors)
-    packed = pack(where, tile_ids.T, obs_rows.reshape(1, count), obs_cols.reshape(1, count), obs_values.T)
+    packed = pack(tile_ids.T, obs_rows.reshape(1, count), obs_cols.reshape(1, count), obs_values.T)
     got = lax.all_to_all(packed, ALL, 0, 0, tiled=True)
+    cot_t, wide, back1, back2 = prep(cotangent, w_embed, w_first, w_second)
     s, a, b = setconv(where, got, cotangent)
     a, b = swap_a(a), swap_b(b)
     c, d = join(where, a, b, s, cotangent)
-    hg, cot_t, x = mid(where, cotangent, s, a, b, w_second, w_embed)
+    hg, x, pre = mid(where, cotangent, s, a, b, back2, wide, w_first)
     halo = (a, b, swap_c(c), swap_d(d))
-    field, red, _, _ = main(where, cotangent, s, halo, w_embed, w_first, w_second, cot_t, hg, x)
+    field, red, _, _, _ = main(where, cotangent, s, halo, wide, w_first, w_second, back1, back2, cot_t, hg, x, pre)
 
     chips = owners // 2
     groups = [[2 * k + core for k in range(chips)] for core in range(2)]

time: 121 us -> 118 us (0.975)
  blocking collectives: 61.8 us -> 32.5 us
  waiting for transfers between devices: 6.57 us -> 25.6 us
  starting transfers between devices: 10.1 us -> 19.4 us
  Pallas kernels: 41 us -> 39 us
    all_to_all x1 -> x0, blocking collectives: 30.8 us -> none  [per_device(): got = lax.all_to_all(packed, ALL, 0, 0, tiled=True)]
    all_to_all x0 -> x1, waiting for transfers between devices: none -> 19.2 us  [per_device(): got = lax.all_to_all(packed, ALL, 0, 0, tiled=True)]
    all_to_all x0 -> x1, starting transfers between devices: none -> 11.5 us  [per_device(): got = lax.all_to_all(packed, ALL, 0, 0, tiled=True)]
    pallas_call x1, Pallas kernels: 4.1 us -> 6.42 us  [mid(): pl.pallas_call(mid_kernel, in_specs=[pl.BlockSpec(memory_space=pltpu.SMEM...]
    ppermute x6, starting transfers between devices: 10.1 us -> 7.87 us  [swap(): return lambda x: lax.ppermute(x, ALL, pairs)]
    pallas_call x1, Pallas kernels: 16 us -> 14.2 us  [pack(): pl.pallas_call(pack_kernel, grid=(steps,), in_specs=[pl.BlockSpec(memory_...]
    pallas_call x1, Pallas kernels: 12.8 us -> 11 us  [main(): pl.pallas_call(main_kernel, in_specs=[pl.BlockSpec(memory_space=pltpu.SME...]
    all_to_all x1, blocking collectives: 16.6 us -> 18.1 us  [per_device(): lax.all_to_all(half, ALL, 0, 0, axis_index_groups=groups, tiled=True)]
  transfers between devices with their start and end apart: 6 -> 7, of which waited for: 4 -> 5; matrix products, arithmetic and copies ran while one was open for 0% -> 0% of each run, Pallas kernels for 3% -> 6%
where the time goes in v4:
time: 118 us
  Pallas kernels  39 us (33%)
  blocking collectives  32.5 us (28%)
  waiting for transfers between devices  25.6 us (22%)
  starting transfers between devices  19.4 us (16%)
    all_to_all x1, waiting for transfers between devices, per_device(): got = lax.all_to_all(packed, ALL, 0, 0, tiled=True)  19.2 us
    all_to_all x1, blocking collectives, per_device(): lax.all_to_all(half, ALL, 0, 0, axis_index_groups=groups, tiled=True)  18.1 us
    all_to_all x1, blocking collectives, per_device(): lax.all_to_all(spread, ALL, 0, 0, axis_index_groups=groups, tiled=True)  14.4 us
    pallas_call x1, Pallas kernels, pack(): pl.pallas_call(pack_kernel, grid=(steps,), in_specs=[pl.BlockSpec(memory_...  14.2 us
    all_to_all x1, starting transfers between devices, per_device(): got = lax.all_to_all(packed, ALL, 0, 0, tiled=True)  11.5 us
    pallas_call x1, Pallas kernels, main(): pl.pallas_call(main_kernel, in_specs=[pl.BlockSpec(memory_space=pltpu.SME...  11 us
    ppermute x6, starting transfers between devices, swap(): return lambda x: lax.ppermute(x, ALL, pairs)  7.87 us
    pallas_call x1, Pallas kernels, mid(): pl.pallas_call(mid_kernel, in_specs=[pl.BlockSpec(memory_space=pltpu.SMEM...  6.42 us
  transfers between devices with their start and end apart: 7, of which 5 were waited for; matrix products, arithmetic and copies ran while one was open for 0% of the time, Pallas kernels for 6%

profile of v4, /device:TPU:1, one launch (start us, length us, event | category | flops | bytes accessed | tf_op | source)
XLA Modules:
  0.0 117.6 jit_solution(4113677810692918552)
XLA Ops:
  0.6 14.2 %pack.1 = bf16[128,32,128]{2,1,0:T(8,128)(2,1)} custom-call(s32[1,8192]{1,0:T(1,128)} %bitcast.14, f32[1,8192]{1,0:T(1,128)} %bitcast.15, f32[1,8192]{1,0:T(1,128)} %bitcast.16, bf16[24,8192]{1,0:T(8,128)(2,1)} %bitcast.13), custom_call_target="tpu_custom_call" | custom-call | flops 8589934592 | bytes 3145728 | tf_op jit(solution)/shard_map/pack/pallas_call | solution.py:117
  14.8 0.0 copy-start
  14.8 11.5 %all-to-all-start = ((bf16[128,32,128]{2,1,0:T(8,128)(2,1)}), bf16[128,32,128]{2,1,0:T(8,128)(2,1)S(1)}, u32[]{:S(2)}, u32[]{:S(2)}) async-start(bf16[128,32,128]{2,1,0:T(8,128)(2,1)} %pack.1), calls=%async_computation | async-start | bytes 2097152 | tf_op jit(solution)/shard_map/all_to_all | solution.py:625
  26.4 0.1 pad_add_fusion.where_ref
  26.4 0.0 copy-start.1
  26.4 0.0 copy-start.2
  26.4 0.0 copy-start.3
  26.4 19.2 %all-to-all-done.got_ref = bf16[128,32,128]{2,1,0:T(8,128)(2,1)S(1)} async-done(((bf16[128,32,128]{2,1,0:T(8,128)(2,1)}), bf16[128,32,128]{2,1,0:T(8,128)(2,1)S(1)}, u32[]{:S(2)}, u32[]{:S(2)}) %all-to-all-start) | async-done | bytes 1048608 | tf_op jit(solution)/shard_map/all_to_all | solution.py:625
  45.7 0.0 copy-done
  45.7 4.8 %setconv.1 = (bf16[128,512]{1,0:T(8,128)(2,1)S(1)}, bf16[20,16,128]{2,1,0:T(8,128)(2,1)S(1)}, bf16[20,16,128]{2,1,0:T(8,128)(2,1)S(1)}) custom-call(s32[4]{0:T(128)S(1)} %pad_add_fusion.where_ref, bf16[128,32,128]{2,1,0:T(8,128)(2,1)S(1)} %all-to-all-done.got_ref, bf16[16,128,128]{2,1,0:T(8,128)(2,1)S(1)} %copy-done), custom_call_target="tpu_custom_call" | custom-call | flops 3221225472 | bytes 2097152 | tf_op jit(solution)/shard_map/setconv/pallas_call | solution.py:186
  50.5 0.7 collective-permute-start
  51.2 0.3 collective-permute-start.1
  51.5 0.0 copy-done.1
  51.5 0.0 copy-done.2
  51.5 0.0 copy-done.3
  51.5 0.2 prep.1
  51.8 0.4 collective-permute-done.a_ref
  52.1 2.9 %collective-permute-done.1.b_ref = bf16[20,16,128]{2,1,0:T(8,128)(2,1)S(1)} collective-permute-done((bf16[20,16,128]{2,1,0:T(8,128)(2,1)S(1)}, bf16[20,16,128]{2,1,0:T(8,128)(2,1)S(1)}, u32[]{:S(2)}, u32[]{:S(2)}) %collective-permute-start.1) | collective-permute-done | bytes 81952 | tf_op jit(solution)/shard_map/ppermute | solution.py:606
  55.1 0.6 join.1
  55.7 1.2 %collective-permute-start.2 = (bf16[3,160,128]{2,1,0:T(8,128)(2,1)S(1)}, bf16[3,160,128]{2,1,0:T(8,128)(2,1)S(1)}, u32[]{:S(2)}, u32[]{:S(2)}) collective-permute-start(bf16[3,160,128]{2,1,0:T(8,128)(2,1)S(1)} %get-tuple-element.24), channel_id=1, source_target_pairs={{0,16},{1,17},{2,18},{3,19},{4,20},{5,21},{6,22},{7,23},{8,24},{9,... | collective-permute-start | bytes 368648 | tf_op jit(solution)/shard_map/ppermute | solution.py:606
  56.9 1.5 %collective-permute-start.3 = (bf16[3,160,128]{2,1,0:T(8,128)(2,1)S(1)}, bf16[3,160,128]{2,1,0:T(8,128)(2,1)S(1)}, u32[]{:S(2)}, u32[]{:S(2)}) collective-permute-start(bf16[3,160,128]{2,1,0:T(8,128)(2,1)S(1)} %get-tuple-element.25), channel_id=1, source_target_pairs={{0,8},{1,9},{2,10},{3,11},{4,12},{5,13},{6,14},{7,15},{8,0},{9,1},... | collective-permute-start | bytes 368648 | tf_op jit(solution)/shard_map/ppermute | solution.py:606
  58.4 6.4 %mid.1 = (f32[3040,128]{1,0:T(8,128)S(1)}, bf16[3040,384]{1,0:T(8,128)(2,1)S(1)}, f32[3040,128]{1,0:T(8,128)S(1)}) custom-call(s32[4]{0:T(128)S(1)} %pad_add_fusion.where_ref, bf16[16,128,128]{2,1,0:T(8,128)(2,1)S(1)} %copy-done, bf16[128,512]{1,0:T(8,128)(2,1)S(1)} %get-tuple-element.21.s_ref, bf16[20,16,128]{2,1,0:T(8,128)(2,1)S(1)} %collective-permute-done.a_ref, ...), custom_call_target="tpu_custom_call" | custom-call | flops 1613758464 | bytes 4194304 | tf_op jit(solution)/shard_map/mid/pallas_call | solution.py:361
  64.8 0.0 collective-permute-done.2.c_ref
  64.8 0.0 collective-permute-done.3.d_ref
  64.8 11.0 %main.1 = (bf16[16,128,128]{2,1,0:T(8,128)(2,1)}, bf16[2,1184,128]{2,1,0:T(8,128)(2,1)S(1)}, f32[3040,128]{1,0:T(8,128)S(1)}, bf16[3040,384]{1,0:T(8,128)(2,1)S(1)}, f32[3040,128]{1,0:T(8,128)S(1)}) custom-call(s32[4]{0:T(128)S(1)} %pad_add_fusion.where_ref, ...), custom_call_target="tpu_custom_call", output_to_operand_aliasing={{2}: (13, {}), {3}: (14, {}), {4}: (15, {})} | custom-call | flops 8589934592 | bytes 6291456 | tf_op jit(solution)/shard_map/main/pallas_call | solution.py:540
  75.8 1.0 collective-permute-start.4
  76.8 1.7 %collective-permute-done.4 = bf16[2,1184,128]{2,1,0:T(8,128)(2,1)S(1)} collective-permute-done((bf16[2,1184,128]{2,1,0:T(8,128)(2,1)S(1)}, bf16[2,1184,128]{2,1,0:T(8,128)(2,1)S(1)}, u32[]{:S(2)}, u32[]{:S(2)}) %collective-permute-start.4) | collective-permute-done | bytes 606240 | tf_op jit(solution)/shard_map/ppermute | solution.py:606
  78.5 0.1 fusion
  78.6 18.1 %all_to_all.15 = bf16[64,24,128]{2,1,0:T(8,128)(2,1)S(1)} all-to-all(bf16[64,24,128]{2,1,0:T(8,128)(2,1)S(1)} %bitcast.12), channel_id=1, replica_groups={{0,2,4,6,8,10,12,14,16,18,20,22,24,26,28,30,32,34,36,38,40,42,44,46,48,..., dimensions={0} | all-to-all | bytes 786432 | tf_op jit(solution)/shard_map/all_to_all | solution.py:640
  96.7 0.1 reduce_sum.12
  96.8 0.1 broadcast_in_dim.2
  96.9 14.4 %all_to_all.16 = bf16[64,24,128]{2,1,0:T(8,128)(2,1)S(1)} all-to-all(bf16[64,24,128]{2,1,0:T(8,128)(2,1)S(1)} %broadcast_in_dim.2), channel_id=1, replica_groups={{0,2,4,6,8,10,12,14,16,18,20,22,24,26,28,30,32,34,36,38,40,42,44,46,48,..., dimensions={0} | all-to-all | bytes 786432 | tf_op jit(solution)/shard_map/all_to_all | solution.py:643
  111.2 3.2 %collective-permute-start.5 = (bf16[1536,128]{1,0:T(8,128)(2,1)S(1)}, bf16[1536,128]{1,0:T(8,128)(2,1)S(1)}, u32[]{:S(2)}, u32[]{:S(2)}) collective-permute-start(bf16[1536,128]{1,0:T(8,128)(2,1)S(1)} %bitcast.10), channel_id=1, source_target_pairs={{0,1},{1,0},{2,3},{3,2},{4,5},{5,4},{6,7},{7,6},{8,9},{9,8},{10,11... | collective-permute-start | bytes 1179656 | tf_op jit(solution)/shard_map/ppermute | solution.py:606
  114.5 1.3 %collective-permute-done.5.other_ref = bf16[1536,128]{1,0:T(8,128)(2,1)S(1)} collective-permute-done((bf16[1536,128]{1,0:T(8,128)(2,1)S(1)}, bf16[1536,128]{1,0:T(8,128)(2,1)S(1)}, u32[]{:S(2)}, u32[]{:S(2)}) %collective-permute-start.5) | collective-permute-done | bytes 393248 | tf_op jit(solution)/shard_map/ppermute | solution.py:606
  115.8 1.7 %unpack.1 = (f32[24,128]{1,0:T(8,128)}, f32[3,3,128,128]{3,2,1,0:T(8,128)}, f32[3,3,128,128]{3,2,1,0:T(8,128)}) custom-call(s32[4]{0:T(128)S(1)} %pad_add_fusion.where_ref, bf16[1536,128]{1,0:T(8,128)(2,1)S(1)} %bitcast.11, bf16[1536,128]{1,0:T(8,128)(2,1)S(1)} %collective-permute-done.5.other_ref), custom_call_target="tpu_custom_call" | custom-call | tf_op jit(solution)/shard_map/unpack/pallas_call | solution.py:582
  (1 shorter events, 0.0 us)
Async XLA Ops:
  14.8 30.9 %copy-start = (bf16[16,128,128]{2,1,0:T(8,128)(2,1)S(1)}, bf16[16,128,128]{2,1,0:T(8,128)(2,1)}, u32[]{:S(2)}) copy-start(bf16[16,128,128]{2,1,0:T(8,128)(2,1)} %cot_ref.9) | copy-start | bytes 1572868
  14.8 30.9 %all-to-all-start = ((bf16[128,32,128]{2,1,0:T(8,128)(2,1)}), bf16[128,32,128]{2,1,0:T(8,128)(2,1)S(1)}, u32[]{:S(2)}, u32[]{:S(2)}) async-start(bf16[128,32,128]{2,1,0:T(8,128)(2,1)} %pack.1), calls=%async_computation | async-start | bytes 2097152 | tf_op jit(solution)/shard_map/all_to_all | solution.py:625
  26.4 25.1 %copy-start.1 = (bf16[3,3,128,128]{3,2,1,0:T(8,128)(2,1)S(1)}, bf16[3,3,128,128]{3,2,1,0:T(8,128)(2,1)}, u32[]{:S(2)}) copy-start(bf16[3,3,128,128]{3,2,1,0:T(8,128)(2,1)} %w1_ref.5) | copy-start | bytes 884740
  26.4 25.1 %copy-start.2 = (bf16[3,3,128,128]{3,2,1,0:T(8,128)(2,1)S(1)}, bf16[3,3,128,128]{3,2,1,0:T(8,128)(2,1)}, u32[]{:S(2)}) copy-start(bf16[3,3,128,128]{3,2,1,0:T(8,128)(2,1)} %w2_ref.3) | copy-start | bytes 884740
  26.4 25.1 %copy-start.3 = (bf16[24,128]{1,0:T(8,128)(2,1)S(1)}, bf16[24,128]{1,0:T(8,128)(2,1)}, u32[]{:S(2)}) copy-start(bf16[24,128]{1,0:T(8,128)(2,1)} %embed_ref.1) | copy-start | bytes 18436
  50.5 1.6 %collective-permute-start = (bf16[20,16,128]{2,1,0:T(8,128)(2,1)S(1)}, bf16[20,16,128]{2,1,0:T(8,128)(2,1)S(1)}, u32[]{:S(2)}, u32[]{:S(2)}) collective-permute-start(bf16[20,16,128]{2,1,0:T(8,128)(2,1)S(1)} %get-tuple-element.22), channel_id=1, source_target_pairs={{0,1},{1,0},{2,3},{3,2},{4,5},{5,4},{6,7},{7,6},{8,9},{9,8},{10,11... | collective-permute-start | bytes 245768 | tf_op jit(solution)/shard_map/ppermute | solution.py:606
  51.2 3.9 %collective-permute-start.1 = (bf16[20,16,128]{2,1,0:T(8,128)(2,1)S(1)}, bf16[20,16,128]{2,1,0:T(8,128)(2,1)S(1)}, u32[]{:S(2)}, u32[]{:S(2)}) collective-permute-start(bf16[20,16,128]{2,1,0:T(8,128)(2,1)S(1)} %get-tuple-element.23), channel_id=1, source_target_pairs={{0,15},{1,2},{2,1},{3,4},{4,3},{5,6},{6,5},{7,8},{8,7},{9,10},{10,... | collective-permute-start | bytes 245768 | tf_op jit(solution)/shard_map/ppermute | solution.py:606
  55.7 9.1 %collective-permute-start.2 = (bf16[3,160,128]{2,1,0:T(8,128)(2,1)S(1)}, bf16[3,160,128]{2,1,0:T(8,128)(2,1)S(1)}, u32[]{:S(2)}, u32[]{:S(2)}) collective-permute-start(bf16[3,160,128]{2,1,0:T(8,128)(2,1)S(1)} %get-tuple-element.24), channel_id=1, source_target_pairs={{0,16},{1,17},{2,18},{3,19},{4,20},{5,21},{6,22},{7,23},{8,24},{9,... | collective-permute-start | bytes 368648 | tf_op jit(solution)/shard_map/ppermute | solution.py:606
  56.9 7.9 %collective-permute-start.3 = (bf16[3,160,128]{2,1,0:T(8,128)(2,1)S(1)}, bf16[3,160,128]{2,1,0:T(8,128)(2,1)S(1)}, u32[]{:S(2)}, u32[]{:S(2)}) collective-permute-start(bf16[3,160,128]{2,1,0:T(8,128)(2,1)S(1)} %get-tuple-element.25), channel_id=1, source_target_pairs={{0,8},{1,9},{2,10},{3,11},{4,12},{5,13},{6,14},{7,15},{8,0},{9,1},... | collective-permute-start | bytes 368648 | tf_op jit(solution)/shard_map/ppermute | solution.py:606
  75.8 2.6 %collective-permute-start.4 = (bf16[2,1184,128]{2,1,0:T(8,128)(2,1)S(1)}, bf16[2,1184,128]{2,1,0:T(8,128)(2,1)S(1)}, u32[]{:S(2)}, u32[]{:S(2)}) collective-permute-start(bf16[2,1184,128]{2,1,0:T(8,128)(2,1)S(1)} %get-tuple-element.34), channel_id=1, source_target_pairs={{0,1},{1,0},{2,3},{3,2},{4,5},{5,4},{6,7},{7,6},{8,9},{9,8},{10,11... | collective-permute-start | bytes 1818632 | tf_op jit(solution)/shard_map/ppermute | solution.py:606
  111.2 4.6 %collective-permute-start.5 = (bf16[1536,128]{1,0:T(8,128)(2,1)S(1)}, bf16[1536,128]{1,0:T(8,128)(2,1)S(1)}, u32[]{:S(2)}, u32[]{:S(2)}) collective-permute-start(bf16[1536,128]{1,0:T(8,128)(2,1)S(1)} %bitcast.10), channel_id=1, source_target_pairs={{0,1},{1,0},{2,3},{3,2},{4,5},{5,4},{6,7},{7,6},{8,9},{9,8},{10,11... | collective-permute-start | bytes 1179656 | tf_op jit(solution)/shard_map/ppermute | solution.py:606

commit v5 on v4

--- a/solution.py
+++ b/solution.py
@@ -19,6 +19,7 @@
 FIRST = PITCH
 OWN = 16 + 2 * PITCH
 FEAT = 32
+SENT = 28
 RED = 24
 HALF = 9 * C + FEAT
 SG = TR * FEAT // 128
@@ -38,7 +39,7 @@
 
 
 def pack_kernel(ids_hbm, rows_hbm, cols_hbm, vals_hbm, out_ref,
-                ids_ref, rows_ref, cols_ref, vals_ref, q_ref, v_ref, pair_ref, acc_ref, sems):
+                ids_ref, rows_ref, cols_ref, vals_ref, q_ref, v_ref, pair_ref, even_ref, odd_ref, sems):
     step = pl.program_id(0)
     count = ids_ref.shape[1]
     owners = out_ref.shape[0] * pl.num_programs(0)
@@ -81,33 +82,43 @@
                 rank = jnp.sum(jnp.where(hot, before, 0.0), axis=0, keepdims=True) - 1.0
                 key = rank + ((ids & 1) * 128).astype(F32)
                 q_ref[:, at] = jnp.where(slot == rows_of_16(key, sub), one, none)
-                pair_ref[:, at] = rows_of_16((ids >> 1).astype(F32), FEAT)
+                pair_ref[:, at] = rows_of_16((ids >> 1).astype(F32), pairs)
                 rows, cols = rows_ref[:, at], cols_ref[:, at]
                 rows_hi, cols_hi = rows.astype(BF16).astype(F32), cols.astype(BF16).astype(F32)
                 tail = jnp.concatenate(
                     [rows_hi, rows - rows_hi, cols_hi, cols - cols_hi, jnp.zeros((4, sub), F32)], axis=0
                 )
-                v_ref[:, at] = jnp.concatenate([vals_ref[:, at].astype(F32), tail], axis=0).astype(BF16)
+                v_ref[:, at] = jnp.concatenate([vals_ref[:, at].astype(F32), tail], axis=0)
                 carry = carry + counted[:, sub:]
             return carry
 
         lax.fori_loop(0, count // sub // 4, body, jnp.zeros((owners, 128), F32))
 
-    base = jnp.full((FEAT, part), (step * pairs).astype(F32), F32).astype(BF16)
+    wanted = lax.broadcasted_iota(jnp.int32, (pairs, part), 0) + step * pairs
+    wanted = wanted.astype(F32).astype(BF16)
+    none = jnp.zeros((pairs, part), BF16)
     for k in range(count // part):
         at = pl.ds(k * part, part)
-        pair = pair_ref[:, at] - base
-        values = v_ref[:, at]
-        none = jnp.zeros_like(values)
-        left = jnp.concatenate([jnp.where(pair == p, values, none) for p in range(pairs)], axis=0)
+        mine = pair_ref[:, at] == wanted
+        left = jnp.concatenate(
+            [
+                jnp.where(mine, jnp.broadcast_to(v_ref[f : f + 1, at], (pairs, part)).astype(BF16), none)
+                for f in range(SENT)
+            ],
+            axis=0,
+        )
         term = dot_nt(left, q_ref[:, at])
-        if k == 0:
-            acc_ref[...] = term
-        else:
-            acc_ref[...] += term
+        for half, acc in enumerate((even_ref, odd_ref)):
+            piece = term[:, half * 128 : (half + 1) * 128]
+            if k == 0:
+                acc[...] = piece
+            else:
+                acc[...] += piece
+    rest = jnp.zeros((FEAT - SENT, 128), F32)
     for p in range(pairs):
-        out_ref[2 * p] = acc_ref[p * FEAT : (p + 1) * FEAT, :128].astype(BF16)
-        out_ref[2 * p + 1] = acc_ref[p * FEAT : (p + 1) * FEAT, 128:].astype(BF16)
+        for half, acc in enumerate((even_ref, odd_ref)):
+            got = jnp.concatenate([acc[pl.ds(p, SENT, stride=pairs), :], rest], axis=0)
+            out_ref[2 * p + half] = got.astype(BF16)
 
 
 def pack(ids, rows, cols, values):
@@ -126,9 +137,10 @@
             pltpu.VMEM(cols.shape, cols.dtype),
             pltpu.VMEM(values.shape, values.dtype),
             pltpu.VMEM((256, count), BF16),
-            pltpu.VMEM((FEAT, count), BF16),
-            pltpu.VMEM((FEAT, count), BF16),
-            pltpu.VMEM((owners // steps // 2 * FEAT, 256), F32),
+            pltpu.VMEM((FEAT, count), F32),
+            pltpu.VMEM((owners // steps // 2, count), BF16),
+            pltpu.VMEM((owners // steps // 2 * SENT, 128), F32),
+            pltpu.VMEM((owners // steps // 2 * SENT, 128), F32),
             pltpu.SemaphoreType.DMA((4,)),
         ],
         compiler_params=pltpu.CompilerParams(vmem_limit_bytes=58 << 20),
@@ -376,8 +388,8 @@
 
 def main_kernel(where_ref, cot_ref, s_ref, a_ref, b_ref, c_ref, d_ref,
                 wide_ref, w1_ref, w2_ref, back1_ref, back2_ref, cot_t_ref, hg_in, x_in, pre_in,
-                field_ref, red_ref, hg_ref, x_ref, pre_ref,
-                flat_ref, h_ref, own_ref, own_t_ref, eg_ref):
+                field_ref, keep_ref, send_ref, hg_ref, x_ref, pre_ref,
+                red_ref, flat_ref, h_ref, own_ref, own_t_ref, eg_ref):
     even_lon, even_lat = evens(where_ref)
     north = where_ref[0] == 0
     south = where_ref[0] == where_ref[2] - 1
@@ -533,6 +545,9 @@
             total += dot(s_t[k * FEAT : (k + 1) * FEAT], eg_ref[i * PITCH : i * PITCH + TC])
     red_ref[0, 9 * C :] = jnp.zeros((FEAT, C), BF16)
     red_ref[1, 9 * C :] = total.astype(BF16)
+    core = where_ref[1] % 2
+    keep_ref[...] = red_ref[core]
+    send_ref[...] = red_ref[1 - core]
 
 
 def main(where, cot, s, halo, wide, w_first, w_second, back1, back2, cot_t, hg, x, pre):
@@ -540,16 +555,18 @@
     return pl.pallas_call(
         main_kernel,
         in_specs=[pl.BlockSpec(memory_space=pltpu.SMEM)] + [vmem] * 15,
-        out_specs=[vmem] * 5,
+        out_specs=[vmem] * 6,
         out_shape=[
             jax.ShapeDtypeStruct((TR, TC, C), BF16),
-            jax.ShapeDtypeStruct((2, HALF, C), BF16),
+            jax.ShapeDtypeStruct((HALF, C), BF16),
+            jax.ShapeDtypeStruct((HALF, C), BF16),
             jax.ShapeDtypeStruct(hg.shape, hg.dtype),
             jax.ShapeDtypeStruct(x.shape, x.dtype),
             jax.ShapeDtypeStruct(pre.shape, pre.dtype),
         ],
-        input_output_aliases={13: 2, 14: 3, 15: 4},
+        input_output_aliases={13: 3, 14: 4, 15: 5},
         scratch_shapes=[
+            pltpu.VMEM((2, HALF, C), BF16),
             pltpu.VMEM((LEN + 16, C), F32),
             pltpu.VMEM((LEN, 3 * C), BF16),
             pltpu.VMEM((TR * PITCH, C), BF16),
@@ -629,13 +646,11 @@
     c, d = join(where, a, b, s, cotangent)
     hg, x, pre = mid(where, cotangent, s, a, b, back2, wide, w_first)
     halo = (a, b, swap_c(c), swap_d(d))
-    field, red, _, _, _ = main(where, cotangent, s, halo, wide, w_first, w_second, back1, back2, cot_t, hg, x, pre)
+    field, keep, send, _, _, _ = main(where, cotangent, s, halo, wide, w_first, w_second, back1, back2, cot_t, hg, x, pre)
 
     chips = owners // 2
     groups = [[2 * k + core for k in range(chips)] for core in range(2)]
-    mine = lax.axis_index("lon") % 2
-    theirs = swap_a(red)
-    half = red[mine].astype(F32) + theirs[mine].astype(F32)
+    half = keep.astype(F32) + swap_a(send).astype(F32)
     half = jnp.pad(half.astype(BF16), ((0, chips * RED - HALF), (0, 0))).reshape(chips, RED, C)
     parts = lax.all_to_all(half, ALL, 0, 0, axis_index_groups=groups, tiled=True)
     summed = jnp.sum(parts.astype(F32), axis=0).astype(BF16)

time: 118 us -> 117 us (level)
  no operation moved by 1% of the time
where the time goes in v5:
time: 117 us; the launch traced here: 116 us
  Pallas kernels  38.4 us (33%)
  blocking collectives  32.5 us (28%)
  waiting for transfers between devices  25.1 us (21%)
  starting transfers between devices  19.4 us (17%)
    all_to_all x1, waiting for transfers between devices, per_device(): got = lax.all_to_all(packed, ALL, 0, 0, tiled=True)  19.2 us
    all_to_all x1, blocking collectives, per_device(): lax.all_to_all(half, ALL, 0, 0, axis_index_groups=groups, tiled=True)  18.2 us
    all_to_all x1, blocking collectives, per_device(): lax.all_to_all(spread, ALL, 0, 0, axis_index_groups=groups, tiled=True)  14.4 us
    pallas_call x1, Pallas kernels, pack(): pl.pallas_call(pack_kernel, grid=(steps,), in_specs=[pl.BlockSpec(memory_...  13.5 us
    all_to_all x1, starting transfers between devices, per_device(): got = lax.all_to_all(packed, ALL, 0, 0, tiled=True)  11.5 us
    pallas_call x1, Pallas kernels, main(): pl.pallas_call(main_kernel, in_specs=[pl.BlockSpec(memory_space=pltpu.SME...  11 us
    ppermute x6, starting transfers between devices, swap(): return lambda x: lax.ppermute(x, ALL, pairs)  7.89 us
    pallas_call x1, Pallas kernels, mid(): pl.pallas_call(mid_kernel, in_specs=[pl.BlockSpec(memory_space=pltpu.SMEM...  6.41 us
  transfers between devices with their start and end apart: 7, of which 5 were waited for; matrix products, arithmetic and copies ran while one was open for 0% of the time, Pallas kernels for 6%

profile of v5, /device:TPU:1, one launch (start us, length us, event | category | flops | bytes accessed | tf_op | source)
XLA Modules:
  0.0 116.5 jit_solution(1276458712964101458)
XLA Ops:
  0.6 13.5 %pack.1 = bf16[128,32,128]{2,1,0:T(8,128)(2,1)} custom-call(s32[1,8192]{1,0:T(1,128)} %bitcast.12, f32[1,8192]{1,0:T(1,128)} %bitcast.13, f32[1,8192]{1,0:T(1,128)} %bitcast.14, bf16[24,8192]{1,0:T(8,128)(2,1)} %bitcast.11), custom_call_target="tpu_custom_call" | custom-call | flops 8589934592 | bytes 3145728 | tf_op jit(solution)/shard_map/pack/pallas_call | solution.py:128
  14.2 0.0 copy-start
  14.2 11.5 %all-to-all-start = ((bf16[128,32,128]{2,1,0:T(8,128)(2,1)}), bf16[128,32,128]{2,1,0:T(8,128)(2,1)S(1)}, u32[]{:S(2)}, u32[]{:S(2)}) async-start(bf16[128,32,128]{2,1,0:T(8,128)(2,1)} %pack.1), calls=%async_computation | async-start | bytes 2097152 | tf_op jit(solution)/shard_map/all_to_all | solution.py:642
  25.7 0.1 pad_add_fusion.where_ref
  25.8 0.0 copy-start.1
  25.8 0.0 copy-start.2
  25.8 0.0 copy-start.3
  25.8 19.2 %all-to-all-done.got_ref = bf16[128,32,128]{2,1,0:T(8,128)(2,1)S(1)} async-done(((bf16[128,32,128]{2,1,0:T(8,128)(2,1)}), bf16[128,32,128]{2,1,0:T(8,128)(2,1)S(1)}, u32[]{:S(2)}, u32[]{:S(2)}) %all-to-all-start) | async-done | bytes 1048608 | tf_op jit(solution)/shard_map/all_to_all | solution.py:642
  45.0 0.0 copy-done
  45.0 4.8 %setconv.1 = (bf16[128,512]{1,0:T(8,128)(2,1)S(1)}, bf16[20,16,128]{2,1,0:T(8,128)(2,1)S(1)}, bf16[20,16,128]{2,1,0:T(8,128)(2,1)S(1)}) custom-call(s32[4]{0:T(128)S(1)} %pad_add_fusion.where_ref, bf16[128,32,128]{2,1,0:T(8,128)(2,1)S(1)} %all-to-all-done.got_ref, bf16[16,128,128]{2,1,0:T(8,128)(2,1)S(1)} %copy-done), custom_call_target="tpu_custom_call" | custom-call | flops 3221225472 | bytes 2097152 | tf_op jit(solution)/shard_map/setconv/pallas_call | solution.py:198
  49.9 0.7 collective-permute-start
  50.5 0.3 collective-permute-start.1
  50.9 0.0 copy-done.1
  50.9 0.0 copy-done.2
  50.9 0.0 copy-done.3
  50.9 0.2 prep.1
  51.1 0.4 collective-permute-done.a_ref
  51.5 2.9 %collective-permute-done.1.b_ref = bf16[20,16,128]{2,1,0:T(8,128)(2,1)S(1)} collective-permute-done((bf16[20,16,128]{2,1,0:T(8,128)(2,1)S(1)}, bf16[20,16,128]{2,1,0:T(8,128)(2,1)S(1)}, u32[]{:S(2)}, u32[]{:S(2)}) %collective-permute-start.1) | collective-permute-done | bytes 81952 | tf_op jit(solution)/shard_map/ppermute | solution.py:623
  54.4 0.6 join.1
  55.0 1.2 %collective-permute-start.2 = (bf16[3,160,128]{2,1,0:T(8,128)(2,1)S(1)}, bf16[3,160,128]{2,1,0:T(8,128)(2,1)S(1)}, u32[]{:S(2)}, u32[]{:S(2)}) collective-permute-start(bf16[3,160,128]{2,1,0:T(8,128)(2,1)S(1)} %get-tuple-element.25), channel_id=1, source_target_pairs={{0,16},{1,17},{2,18},{3,19},{4,20},{5,21},{6,22},{7,23},{8,24},{9,... | collective-permute-start | bytes 368648 | tf_op jit(solution)/shard_map/ppermute | solution.py:623
  56.2 1.5 %collective-permute-start.3 = (bf16[3,160,128]{2,1,0:T(8,128)(2,1)S(1)}, bf16[3,160,128]{2,1,0:T(8,128)(2,1)S(1)}, u32[]{:S(2)}, u32[]{:S(2)}) collective-permute-start(bf16[3,160,128]{2,1,0:T(8,128)(2,1)S(1)} %get-tuple-element.26), channel_id=1, source_target_pairs={{0,8},{1,9},{2,10},{3,11},{4,12},{5,13},{6,14},{7,15},{8,0},{9,1},... | collective-permute-start | bytes 368648 | tf_op jit(solution)/shard_map/ppermute | solution.py:623
  57.7 6.4 %mid.1 = (f32[3040,128]{1,0:T(8,128)S(1)}, bf16[3040,384]{1,0:T(8,128)(2,1)S(1)}, f32[3040,128]{1,0:T(8,128)S(1)}) custom-call(s32[4]{0:T(128)S(1)} %pad_add_fusion.where_ref, bf16[16,128,128]{2,1,0:T(8,128)(2,1)S(1)} %copy-done, bf16[128,512]{1,0:T(8,128)(2,1)S(1)} %get-tuple-element.22.s_ref, bf16[20,16,128]{2,1,0:T(8,128)(2,1)S(1)} %collective-permute-done.a_ref, ...), custom_call_target="tpu_custom_call" | custom-call | flops 1613758464 | bytes 4194304 | tf_op jit(solution)/shard_map/mid/pallas_call | solution.py:373
  64.1 0.0 collective-permute-done.2.c_ref
  64.1 0.0 collective-permute-done.3.d_ref
  64.1 11.0 %main.1 = (bf16[16,128,128]{2,1,0:T(8,128)(2,1)}, bf16[1184,128]{1,0:T(8,128)(2,1)S(1)}, bf16[1184,128]{1,0:T(8,128)(2,1)S(1)}, f32[3040,128]{1,0:T(8,128)S(1)},...) custom-call(s32[4]{0:T(128)S(1)} %pad_add_fusion.where_ref, ...), custom_call_target="tpu_custom_call", output_to_operand_aliasing={{3}: (13, {}), {4}: (14, {}), {5}: (15, {})} | custom-call | flops 8589934592 | bytes 6291456 | tf_op jit(solution)/shard_map/main/pallas_call | solution.py:555
  75.2 1.0 collective-permute-start.4
  76.2 1.2 %collective-permute-done.4 = bf16[1184,128]{1,0:T(8,128)(2,1)S(1)} collective-permute-done((bf16[1184,128]{1,0:T(8,128)(2,1)S(1)}, bf16[1184,128]{1,0:T(8,128)(2,1)S(1)}, u32[]{:S(2)}, u32[]{:S(2)}) %collective-permute-start.4) | collective-permute-done | bytes 303136 | tf_op jit(solution)/shard_map/ppermute | solution.py:623
  77.4 0.1 add_convert_fusion
  77.5 18.2 %all_to_all.15 = bf16[64,24,128]{2,1,0:T(8,128)(2,1)S(1)} all-to-all(bf16[64,24,128]{2,1,0:T(8,128)(2,1)S(1)} %bitcast.10), channel_id=1, replica_groups={{0,2,4,6,8,10,12,14,16,18,20,22,24,26,28,30,32,34,36,38,40,42,44,46,48,..., dimensions={0} | all-to-all | bytes 786432 | tf_op jit(solution)/shard_map/all_to_all | solution.py:655
  95.7 0.1 reduce_sum.12
  95.8 0.1 broadcast_in_dim.2
  95.8 14.4 %all_to_all.16 = bf16[64,24,128]{2,1,0:T(8,128)(2,1)S(1)} all-to-all(bf16[64,24,128]{2,1,0:T(8,128)(2,1)S(1)} %broadcast_in_dim.2), channel_id=1, replica_groups={{0,2,4,6,8,10,12,14,16,18,20,22,24,26,28,30,32,34,36,38,40,42,44,46,48,..., dimensions={0} | all-to-all | bytes 786432 | tf_op jit(solution)/shard_map/all_to_all | solution.py:658
  110.2 3.2 %collective-permute-start.5 = (bf16[1536,128]{1,0:T(8,128)(2,1)S(1)}, bf16[1536,128]{1,0:T(8,128)(2,1)S(1)}, u32[]{:S(2)}, u32[]{:S(2)}) collective-permute-start(bf16[1536,128]{1,0:T(8,128)(2,1)S(1)} %bitcast.8), channel_id=1, source_target_pairs={{0,1},{1,0},{2,3},{3,2},{4,5},{5,4},{6,7},{7,6},{8,9},{9,8},{10,11... | collective-permute-start | bytes 1179656 | tf_op jit(solution)/shard_map/ppermute | solution.py:623
  113.4 1.3 %collective-permute-done.5.other_ref = bf16[1536,128]{1,0:T(8,128)(2,1)S(1)} collective-permute-done((bf16[1536,128]{1,0:T(8,128)(2,1)S(1)}, bf16[1536,128]{1,0:T(8,128)(2,1)S(1)}, u32[]{:S(2)}, u32[]{:S(2)}) %collective-permute-start.5) | collective-permute-done | bytes 393248 | tf_op jit(solution)/shard_map/ppermute | solution.py:623
  114.7 1.7 %unpack.1 = (f32[24,128]{1,0:T(8,128)}, f32[3,3,128,128]{3,2,1,0:T(8,128)}, f32[3,3,128,128]{3,2,1,0:T(8,128)}) custom-call(s32[4]{0:T(128)S(1)} %pad_add_fusion.where_ref, bf16[1536,128]{1,0:T(8,128)(2,1)S(1)} %bitcast.9, bf16[1536,128]{1,0:T(8,128)(2,1)S(1)} %collective-permute-done.5.other_ref), custom_call_target="tpu_custom_call" | custom-call | tf_op jit(solution)/shard_map/unpack/pallas_call | solution.py:599
  (1 shorter events, 0.0 us)
Async XLA Ops:
  14.2 30.9 %copy-start = (bf16[16,128,128]{2,1,0:T(8,128)(2,1)S(1)}, bf16[16,128,128]{2,1,0:T(8,128)(2,1)}, u32[]{:S(2)}) copy-start(bf16[16,128,128]{2,1,0:T(8,128)(2,1)} %cot_ref.9) | copy-start | bytes 1572868
  14.2 30.8 %all-to-all-start = ((bf16[128,32,128]{2,1,0:T(8,128)(2,1)}), bf16[128,32,128]{2,1,0:T(8,128)(2,1)S(1)}, u32[]{:S(2)}, u32[]{:S(2)}) async-start(bf16[128,32,128]{2,1,0:T(8,128)(2,1)} %pack.1), calls=%async_computation | async-start | bytes 2097152 | tf_op jit(solution)/shard_map/all_to_all | solution.py:642
  25.8 25.1 %copy-start.1 = (bf16[3,3,128,128]{3,2,1,0:T(8,128)(2,1)S(1)}, bf16[3,3,128,128]{3,2,1,0:T(8,128)(2,1)}, u32[]{:S(2)}) copy-start(bf16[3,3,128,128]{3,2,1,0:T(8,128)(2,1)} %w1_ref.5) | copy-start | bytes 884740
  25.8 25.1 %copy-start.2 = (bf16[3,3,128,128]{3,2,1,0:T(8,128)(2,1)S(1)}, bf16[3,3,128,128]{3,2,1,0:T(8,128)(2,1)}, u32[]{:S(2)}) copy-start(bf16[3,3,128,128]{3,2,1,0:T(8,128)(2,1)} %w2_ref.3) | copy-start | bytes 884740
  25.8 25.1 %copy-start.3 = (bf16[24,128]{1,0:T(8,128)(2,1)S(1)}, bf16[24,128]{1,0:T(8,128)(2,1)}, u32[]{:S(2)}) copy-start(bf16[24,128]{1,0:T(8,128)(2,1)} %embed_ref.1) | copy-start | bytes 18436
  49.9 1.6 %collective-permute-start = (bf16[20,16,128]{2,1,0:T(8,128)(2,1)S(1)}, bf16[20,16,128]{2,1,0:T(8,128)(2,1)S(1)}, u32[]{:S(2)}, u32[]{:S(2)}) collective-permute-start(bf16[20,16,128]{2,1,0:T(8,128)(2,1)S(1)} %get-tuple-element.23), channel_id=1, source_target_pairs={{0,1},{1,0},{2,3},{3,2},{4,5},{5,4},{6,7},{7,6},{8,9},{9,8},{10,11... | collective-permute-start | bytes 245768 | tf_op jit(solution)/shard_map/ppermute | solution.py:623
  50.5 3.9 %collective-permute-start.1 = (bf16[20,16,128]{2,1,0:T(8,128)(2,1)S(1)}, bf16[20,16,128]{2,1,0:T(8,128)(2,1)S(1)}, u32[]{:S(2)}, u32[]{:S(2)}) collective-permute-start(bf16[20,16,128]{2,1,0:T(8,128)(2,1)S(1)} %get-tuple-element.24), channel_id=1, source_target_pairs={{0,15},{1,2},{2,1},{3,4},{4,3},{5,6},{6,5},{7,8},{8,7},{9,10},{10,... | collective-permute-start | bytes 245768 | tf_op jit(solution)/shard_map/ppermute | solution.py:623
  55.0 9.1 %collective-permute-start.2 = (bf16[3,160,128]{2,1,0:T(8,128)(2,1)S(1)}, bf16[3,160,128]{2,1,0:T(8,128)(2,1)S(1)}, u32[]{:S(2)}, u32[]{:S(2)}) collective-permute-start(bf16[3,160,128]{2,1,0:T(8,128)(2,1)S(1)} %get-tuple-element.25), channel_id=1, source_target_pairs={{0,16},{1,17},{2,18},{3,19},{4,20},{5,21},{6,22},{7,23},{8,24},{9,... | collective-permute-start | bytes 368648 | tf_op jit(solution)/shard_map/ppermute | solution.py:623
  56.2 7.9 %collective-permute-start.3 = (bf16[3,160,128]{2,1,0:T(8,128)(2,1)S(1)}, bf16[3,160,128]{2,1,0:T(8,128)(2,1)S(1)}, u32[]{:S(2)}, u32[]{:S(2)}) collective-permute-start(bf16[3,160,128]{2,1,0:T(8,128)(2,1)S(1)} %get-tuple-element.26), channel_id=1, source_target_pairs={{0,8},{1,9},{2,10},{3,11},{4,12},{5,13},{6,14},{7,15},{8,0},{9,1},... | collective-permute-start | bytes 368648 | tf_op jit(solution)/shard_map/ppermute | solution.py:623
  75.2 2.2 %collective-permute-start.4 = (bf16[1184,128]{1,0:T(8,128)(2,1)S(1)}, bf16[1184,128]{1,0:T(8,128)(2,1)S(1)}, u32[]{:S(2)}, u32[]{:S(2)}) collective-permute-start(bf16[1184,128]{1,0:T(8,128)(2,1)S(1)} %get-tuple-element.36), channel_id=1, source_target_pairs={{0,1},{1,0},{2,3},{3,2},{4,5},{5,4},{6,7},{7,6},{8,9},{9,8},{10,11... | collective-permute-start | bytes 909320 | tf_op jit(solution)/shard_map/ppermute | solution.py:623
  110.2 4.6 %collective-permute-start.5 = (bf16[1536,128]{1,0:T(8,128)(2,1)S(1)}, bf16[1536,128]{1,0:T(8,128)(2,1)S(1)}, u32[]{:S(2)}, u32[]{:S(2)}) collective-permute-start(bf16[1536,128]{1,0:T(8,128)(2,1)S(1)} %bitcast.8), channel_id=1, source_target_pairs={{0,1},{1,0},{2,3},{3,2},{4,5},{5,4},{6,7},{7,6},{8,9},{9,8},{10,11... | collective-permute-start | bytes 1179656 | tf_op jit(solution)/shard_map/ppermute | solution.py:623

commit v6 on v5

--- a/solution.py
+++ b/solution.py
@@ -73,8 +73,8 @@
             move.wait()
 
         def body(k, carry):
-            for u in range(4):
-                at = pl.ds(pl.multiple_of(k * 4 * sub + u * sub, sub), sub)
+            for u in range(8):
+                at = pl.ds(pl.multiple_of(k * 8 * sub + u * sub, sub), sub)
                 ids = ids_ref[:, at]
                 hot = owner == ids
                 counted = dot(jnp.where(hot, 1.0, 0.0).astype(BF16), upto)
@@ -92,7 +92,7 @@
                 carry = carry + counted[:, sub:]
             return carry
 
-        lax.fori_loop(0, count // sub // 4, body, jnp.zeros((owners, 128), F32))
+        lax.fori_loop(0, count // sub // 8, body, jnp.zeros((owners, 128), F32))
 
     wanted = lax.broadcasted_iota(jnp.int32, (pairs, part), 0) + step * pairs
     wanted = wanted.astype(F32).astype(BF16)
@@ -191,7 +191,7 @@
 
 
 def setconv(where, got, cot):
-    steps = 4
+    steps = 2
     fixed = lambda *shape: pl.BlockSpec(shape, lambda i: (0,) * len(shape))
     lanes = TR * FEAT
     shapes = [(TC, lanes), (SG + TR, 16, C), (SG + TR, 16, C)]
@@ -579,26 +579,41 @@
     )(where, cot, s, *halo, wide, w_first, w_second, back1, back2, cot_t, hg, x, pre)
 
 
-def unpack_kernel(where_ref, own_ref, other_ref, embed_ref, first_ref, second_ref):
-    first_core = where_ref[1] % 2 == 0
-
-    def half(k, at, rows):
-        own, other = own_ref[at : at + rows], other_ref[at : at + rows]
-        return jnp.where(first_core, own, other) if k == 0 else jnp.where(first_core, other, own)
-
+def turn_kernel(own_ref, out_ref):
+    for k in range(9):
+        out_ref[k] = own_ref[k * C : (k + 1) * C].T
+
+
+def turn(own):
+    vmem = pl.BlockSpec(memory_space=pltpu.VMEM)
+    return pl.pallas_call(
+        turn_kernel,
+        in_specs=[vmem],
+        out_specs=vmem,
+        out_shape=jax.ShapeDtypeStruct((9, C, C), BF16),
+        compiler_params=pltpu.CompilerParams(vmem_limit_bytes=8 << 20),
+        cost_estimate=pl.CostEstimate(flops=1 << 20, bytes_accessed=1 << 20, transcendentals=0),
+        name="turn",
+    )(own)
+
+
+def unpack_kernel(where_ref, own_ref, turned_ref, other_ref, embed_ref, first_ref, second_ref):
+    even = where_ref[1] % 2 == 0
     for r in range(3):
         for s in range(3):
-            at = (3 * r + s) * C
-            first_ref[r, s] = half(1, at, C).T.astype(F32)
-            second_ref[r, s] = half(0, at, C).T.astype(F32)
-    embed_ref[...] = half(1, 9 * C, FEAT)[: embed_ref.shape[0]].astype(F32)
-
-
-def unpack(where, own, other, values):
+            k = 3 * r + s
+            mine, other = turned_ref[k], other_ref[k * C : (k + 1) * C].T
+            first_ref[r, s] = jnp.where(even, other, mine).astype(F32)
+            second_ref[r, s] = jnp.where(even, mine, other).astype(F32)
+    embed = jnp.where(even, other_ref[9 * C : 9 * C + FEAT], own_ref[9 * C : 9 * C + FEAT])
+    embed_ref[...] = embed[: embed_ref.shape[0]].astype(F32)
+
+
+def unpack(where, own, turned, other, values):
     vmem = pl.BlockSpec(memory_space=pltpu.VMEM)
     return pl.pallas_call(
         unpack_kernel,
-        in_specs=[pl.BlockSpec(memory_space=pltpu.SMEM), vmem, vmem],
+        in_specs=[pl.BlockSpec(memory_space=pltpu.SMEM), vmem, vmem, vmem],
         out_specs=[vmem] * 3,
         out_shape=[
             jax.ShapeDtypeStruct((values, C), F32),
@@ -607,7 +622,7 @@
         ],
         compiler_params=pltpu.CompilerParams(vmem_limit_bytes=16 << 20),
         name="unpack",
-    )(where, own, other)
+    )(where, own, turned, other)
 
 
 def swaps(bands, sectors):
@@ -657,7 +672,7 @@
     spread = jnp.broadcast_to(summed[None], (chips, RED, C))
     own = lax.all_to_all(spread, ALL, 0, 0, axis_index_groups=groups, tiled=True).reshape(chips * RED, C)
     other = swap_a(own)
-    grad_embed, grad_first, grad_second = unpack(where, own, other, values)
+    grad_embed, grad_first, grad_second = unpack(where, own, turn(own), other, values)
     return (field, grad_embed, grad_first, grad_second)
 
 

time: 117 us -> 116 us (level)
  no operation moved by 1% of the time
where the time goes in v6:
time: 116 us
  Pallas kernels  37.8 us (33%)
  blocking collectives  32.5 us (28%)
  waiting for transfers between devices  25 us (22%)
  starting transfers between devices  19.4 us (17%)
    all_to_all x1, waiting for transfers between devices, per_device(): got = lax.all_to_all(packed, ALL, 0, 0, tiled=True)  19.2 us
    all_to_all x1, blocking collectives, per_device(): lax.all_to_all(half, ALL, 0, 0, axis_index_groups=groups, tiled=True)  18.1 us
    all_to_all x1, blocking collectives, per_device(): lax.all_to_all(spread, ALL, 0, 0, axis_index_groups=groups, tiled=True)  14.4 us
    pallas_call x1, Pallas kernels, pack(): pl.pallas_call(pack_kernel, grid=(steps,), in_specs=[pl.BlockSpec(memory_...  13.3 us
    all_to_all x1, starting transfers between devices, per_device(): got = lax.all_to_all(packed, ALL, 0, 0, tiled=True)  11.5 us
    pallas_call x1, Pallas kernels, main(): pl.pallas_call(main_kernel, in_specs=[pl.BlockSpec(memory_space=pltpu.SME...  11 us
    ppermute x6, starting transfers between devices, swap(): return lambda x: lax.ppermute(x, ALL, pairs)  7.91 us
    pallas_call x1, Pallas kernels, mid(): pl.pallas_call(mid_kernel, in_specs=[pl.BlockSpec(memory_space=pltpu.SMEM...  6.41 us
  transfers between devices with their start and end apart: 7, of which 5 were waited for; matrix products, arithmetic and copies ran while one was open for 0% of the time, Pallas kernels for 6%

profile of v6, /device:TPU:1, one launch (start us, length us, event | category | flops | bytes accessed | tf_op | source)
XLA Modules:
  0.0 115.8 jit_solution(13984733100077698997)
XLA Ops:
  0.6 13.3 %pack.1 = bf16[128,32,128]{2,1,0:T(8,128)(2,1)} custom-call(s32[1,8192]{1,0:T(1,128)} %bitcast.13, f32[1,8192]{1,0:T(1,128)} %bitcast.14, f32[1,8192]{1,0:T(1,128)} %bitcast.15, bf16[24,8192]{1,0:T(8,128)(2,1)} %bitcast.12), custom_call_target="tpu_custom_call" | custom-call | flops 8589934592 | bytes 3145728 | tf_op jit(solution)/shard_map/pack/pallas_call | solution.py:128
  14.0 0.0 copy-start
  14.0 11.5 %all-to-all-start = ((bf16[128,32,128]{2,1,0:T(8,128)(2,1)}), bf16[128,32,128]{2,1,0:T(8,128)(2,1)S(1)}, u32[]{:S(2)}, u32[]{:S(2)}) async-start(bf16[128,32,128]{2,1,0:T(8,128)(2,1)} %pack.1), calls=%async_computation | async-start | bytes 2097152 | tf_op jit(solution)/shard_map/all_to_all | solution.py:657
  25.5 0.1 pad_add_fusion.where_ref
  25.6 0.0 copy-start.1
  25.6 0.0 copy-start.2
  25.6 0.0 copy-start.3
  25.6 19.2 %all-to-all-done.got_ref = bf16[128,32,128]{2,1,0:T(8,128)(2,1)S(1)} async-done(((bf16[128,32,128]{2,1,0:T(8,128)(2,1)}), bf16[128,32,128]{2,1,0:T(8,128)(2,1)S(1)}, u32[]{:S(2)}, u32[]{:S(2)}) %all-to-all-start) | async-done | bytes 1048608 | tf_op jit(solution)/shard_map/all_to_all | solution.py:657
  44.8 0.0 copy-done
  44.8 4.4 %setconv.1 = (bf16[128,512]{1,0:T(8,128)(2,1)S(1)}, bf16[20,16,128]{2,1,0:T(8,128)(2,1)S(1)}, bf16[20,16,128]{2,1,0:T(8,128)(2,1)S(1)}) custom-call(s32[4]{0:T(128)S(1)} %pad_add_fusion.where_ref, bf16[128,32,128]{2,1,0:T(8,128)(2,1)S(1)} %all-to-all-done.got_ref, bf16[16,128,128]{2,1,0:T(8,128)(2,1)S(1)} %copy-done), custom_call_target="tpu_custom_call" | custom-call | flops 3221225472 | bytes 2097152 | tf_op jit(solution)/shard_map/setconv/pallas_call | solution.py:198
  49.2 0.7 collective-permute-start
  49.9 0.3 collective-permute-start.1
  50.2 0.0 copy-done.1
  50.2 0.0 copy-done.2
  50.2 0.0 copy-done.3
  50.2 0.2 prep.1
  50.5 0.3 collective-permute-done.a_ref
  50.8 2.9 %collective-permute-done.1.b_ref = bf16[20,16,128]{2,1,0:T(8,128)(2,1)S(1)} collective-permute-done((bf16[20,16,128]{2,1,0:T(8,128)(2,1)S(1)}, bf16[20,16,128]{2,1,0:T(8,128)(2,1)S(1)}, u32[]{:S(2)}, u32[]{:S(2)}) %collective-permute-start.1) | collective-permute-done | bytes 81952 | tf_op jit(solution)/shard_map/ppermute | solution.py:638
  53.8 0.6 join.1
  54.4 1.2 %collective-permute-start.2 = (bf16[3,160,128]{2,1,0:T(8,128)(2,1)S(1)}, bf16[3,160,128]{2,1,0:T(8,128)(2,1)S(1)}, u32[]{:S(2)}, u32[]{:S(2)}) collective-permute-start(bf16[3,160,128]{2,1,0:T(8,128)(2,1)S(1)} %get-tuple-element.25), channel_id=1, source_target_pairs={{0,16},{1,17},{2,18},{3,19},{4,20},{5,21},{6,22},{7,23},{8,24},{9,... | collective-permute-start | bytes 368648 | tf_op jit(solution)/shard_map/ppermute | solution.py:638
  55.6 1.5 %collective-permute-start.3 = (bf16[3,160,128]{2,1,0:T(8,128)(2,1)S(1)}, bf16[3,160,128]{2,1,0:T(8,128)(2,1)S(1)}, u32[]{:S(2)}, u32[]{:S(2)}) collective-permute-start(bf16[3,160,128]{2,1,0:T(8,128)(2,1)S(1)} %get-tuple-element.26), channel_id=1, source_target_pairs={{0,8},{1,9},{2,10},{3,11},{4,12},{5,13},{6,14},{7,15},{8,0},{9,1},... | collective-permute-start | bytes 368648 | tf_op jit(solution)/shard_map/ppermute | solution.py:638
  57.1 6.4 %mid.1 = (f32[3040,128]{1,0:T(8,128)S(1)}, bf16[3040,384]{1,0:T(8,128)(2,1)S(1)}, f32[3040,128]{1,0:T(8,128)S(1)}) custom-call(s32[4]{0:T(128)S(1)} %pad_add_fusion.where_ref, bf16[16,128,128]{2,1,0:T(8,128)(2,1)S(1)} %copy-done, bf16[128,512]{1,0:T(8,128)(2,1)S(1)} %get-tuple-element.22.s_ref, bf16[20,16,128]{2,1,0:T(8,128)(2,1)S(1)} %collective-permute-done.a_ref, ...), custom_call_target="tpu_custom_call" | custom-call | flops 1613758464 | bytes 4194304 | tf_op jit(solution)/shard_map/mid/pallas_call | solution.py:373
  63.5 0.0 collective-permute-done.2.c_ref
  63.5 0.0 collective-permute-done.3.d_ref
  63.5 11.0 %main.1 = (bf16[16,128,128]{2,1,0:T(8,128)(2,1)}, bf16[1184,128]{1,0:T(8,128)(2,1)S(1)}, bf16[1184,128]{1,0:T(8,128)(2,1)S(1)}, f32[3040,128]{1,0:T(8,128)S(1)},...) custom-call(s32[4]{0:T(128)S(1)} %pad_add_fusion.where_ref, ...), custom_call_target="tpu_custom_call", output_to_operand_aliasing={{3}: (13, {}), {4}: (14, {}), {5}: (15, {})} | custom-call | flops 8589934592 | bytes 6291456 | tf_op jit(solution)/shard_map/main/pallas_call | solution.py:555
  74.5 1.0 collective-permute-start.4
  75.5 1.2 %collective-permute-done.4 = bf16[1184,128]{1,0:T(8,128)(2,1)S(1)} collective-permute-done((bf16[1184,128]{1,0:T(8,128)(2,1)S(1)}, bf16[1184,128]{1,0:T(8,128)(2,1)S(1)}, u32[]{:S(2)}, u32[]{:S(2)}) %collective-permute-start.4) | collective-permute-done | bytes 303136 | tf_op jit(solution)/shard_map/ppermute | solution.py:638
  76.8 0.1 add_convert_fusion
  76.9 18.1 %all_to_all.15 = bf16[64,24,128]{2,1,0:T(8,128)(2,1)S(1)} all-to-all(bf16[64,24,128]{2,1,0:T(8,128)(2,1)S(1)} %bitcast.11), channel_id=1, replica_groups={{0,2,4,6,8,10,12,14,16,18,20,22,24,26,28,30,32,34,36,38,40,42,44,46,48,..., dimensions={0} | all-to-all | bytes 786432 | tf_op jit(solution)/shard_map/all_to_all | solution.py:670
  95.0 0.1 reduce_sum.12
  95.1 0.1 broadcast_in_dim.2
  95.2 14.4 %all_to_all.16 = bf16[64,24,128]{2,1,0:T(8,128)(2,1)S(1)} all-to-all(bf16[64,24,128]{2,1,0:T(8,128)(2,1)S(1)} %broadcast_in_dim.2), channel_id=1, replica_groups={{0,2,4,6,8,10,12,14,16,18,20,22,24,26,28,30,32,34,36,38,40,42,44,46,48,..., dimensions={0} | all-to-all | bytes 786432 | tf_op jit(solution)/shard_map/all_to_all | solution.py:673
  109.5 3.2 %collective-permute-start.5 = (bf16[1536,128]{1,0:T(8,128)(2,1)S(1)}, bf16[1536,128]{1,0:T(8,128)(2,1)S(1)}, u32[]{:S(2)}, u32[]{:S(2)}) collective-permute-start(bf16[1536,128]{1,0:T(8,128)(2,1)S(1)} %bitcast.8), channel_id=1, source_target_pairs={{0,1},{1,0},{2,3},{3,2},{4,5},{5,4},{6,7},{7,6},{8,9},{9,8},{10,11... | collective-permute-start | bytes 1179656 | tf_op jit(solution)/shard_map/ppermute | solution.py:638
  112.7 0.1 turn.1.turned_ref
  112.9 1.2 %collective-permute-done.5.other_ref = bf16[1536,128]{1,0:T(8,128)(2,1)S(1)} collective-permute-done((bf16[1536,128]{1,0:T(8,128)(2,1)S(1)}, bf16[1536,128]{1,0:T(8,128)(2,1)S(1)}, u32[]{:S(2)}, u32[]{:S(2)}) %collective-permute-start.5) | collective-permute-done | bytes 393248 | tf_op jit(solution)/shard_map/ppermute | solution.py:638
  114.1 1.7 %unpack.1 = (f32[24,128]{1,0:T(8,128)}, f32[3,3,128,128]{3,2,1,0:T(8,128)}, f32[3,3,128,128]{3,2,1,0:T(8,128)}) custom-call(s32[4]{0:T(128)S(1)} %pad_add_fusion.where_ref, bf16[1536,128]{1,0:T(8,128)(2,1)S(1)} %bitcast.10, bf16[9,128,128]{2,1,0:T(8,128)(2,1)S(1)} %turn.1.turned_ref, bf16[1536,128]{1,0:T(8,128)(2,1)S(1)} %collective-permute-done.5.other_ref), custom_call_target="tpu_custom_call" | custom-call | tf_op jit(solution)/shard_map/unpack/pallas_call | solution.py:614
  (1 shorter events, 0.0 us)
Async XLA Ops:
  14.0 30.9 %copy-start = (bf16[16,128,128]{2,1,0:T(8,128)(2,1)S(1)}, bf16[16,128,128]{2,1,0:T(8,128)(2,1)}, u32[]{:S(2)}) copy-start(bf16[16,128,128]{2,1,0:T(8,128)(2,1)} %cot_ref.9) | copy-start | bytes 1572868
  14.0 30.8 %all-to-all-start = ((bf16[128,32,128]{2,1,0:T(8,128)(2,1)}), bf16[128,32,128]{2,1,0:T(8,128)(2,1)S(1)}, u32[]{:S(2)}, u32[]{:S(2)}) async-start(bf16[128,32,128]{2,1,0:T(8,128)(2,1)} %pack.1), calls=%async_computation | async-start | bytes 2097152 | tf_op jit(solution)/shard_map/all_to_all | solution.py:657
  25.6 24.6 %copy-start.1 = (bf16[3,3,128,128]{3,2,1,0:T(8,128)(2,1)S(1)}, bf16[3,3,128,128]{3,2,1,0:T(8,128)(2,1)}, u32[]{:S(2)}) copy-start(bf16[3,3,128,128]{3,2,1,0:T(8,128)(2,1)} %w1_ref.5) | copy-start | bytes 884740
  25.6 24.6 %copy-start.2 = (bf16[3,3,128,128]{3,2,1,0:T(8,128)(2,1)S(1)}, bf16[3,3,128,128]{3,2,1,0:T(8,128)(2,1)}, u32[]{:S(2)}) copy-start(bf16[3,3,128,128]{3,2,1,0:T(8,128)(2,1)} %w2_ref.3) | copy-start | bytes 884740
  25.6 24.6 %copy-start.3 = (bf16[24,128]{1,0:T(8,128)(2,1)S(1)}, bf16[24,128]{1,0:T(8,128)(2,1)}, u32[]{:S(2)}) copy-start(bf16[24,128]{1,0:T(8,128)(2,1)} %embed_ref.1) | copy-start | bytes 18436
  49.2 1.6 %collective-permute-start = (bf16[20,16,128]{2,1,0:T(8,128)(2,1)S(1)}, bf16[20,16,128]{2,1,0:T(8,128)(2,1)S(1)}, u32[]{:S(2)}, u32[]{:S(2)}) collective-permute-start(bf16[20,16,128]{2,1,0:T(8,128)(2,1)S(1)} %get-tuple-element.23), channel_id=1, source_target_pairs={{0,1},{1,0},{2,3},{3,2},{4,5},{5,4},{6,7},{7,6},{8,9},{9,8},{10,11... | collective-permute-start | bytes 245768 | tf_op jit(solution)/shard_map/ppermute | solution.py:638
  49.9 3.9 %collective-permute-start.1 = (bf16[20,16,128]{2,1,0:T(8,128)(2,1)S(1)}, bf16[20,16,128]{2,1,0:T(8,128)(2,1)S(1)}, u32[]{:S(2)}, u32[]{:S(2)}) collective-permute-start(bf16[20,16,128]{2,1,0:T(8,128)(2,1)S(1)} %get-tuple-element.24), channel_id=1, source_target_pairs={{0,15},{1,2},{2,1},{3,4},{4,3},{5,6},{6,5},{7,8},{8,7},{9,10},{10,... | collective-permute-start | bytes 245768 | tf_op jit(solution)/shard_map/ppermute | solution.py:638
  54.4 9.1 %collective-permute-start.2 = (bf16[3,160,128]{2,1,0:T(8,128)(2,1)S(1)}, bf16[3,160,128]{2,1,0:T(8,128)(2,1)S(1)}, u32[]{:S(2)}, u32[]{:S(2)}) collective-permute-start(bf16[3,160,128]{2,1,0:T(8,128)(2,1)S(1)} %get-tuple-element.25), channel_id=1, source_target_pairs={{0,16},{1,17},{2,18},{3,19},{4,20},{5,21},{6,22},{7,23},{8,24},{9,... | collective-permute-start | bytes 368648 | tf_op jit(solution)/shard_map/ppermute | solution.py:638
  55.6 7.9 %collective-permute-start.3 = (bf16[3,160,128]{2,1,0:T(8,128)(2,1)S(1)}, bf16[3,160,128]{2,1,0:T(8,128)(2,1)S(1)}, u32[]{:S(2)}, u32[]{:S(2)}) collective-permute-start(bf16[3,160,128]{2,1,0:T(8,128)(2,1)S(1)} %get-tuple-element.26), channel_id=1, source_target_pairs={{0,8},{1,9},{2,10},{3,11},{4,12},{5,13},{6,14},{7,15},{8,0},{9,1},... | collective-permute-start | bytes 368648 | tf_op jit(solution)/shard_map/ppermute | solution.py:638
  74.5 2.2 %collective-permute-start.4 = (bf16[1184,128]{1,0:T(8,128)(2,1)S(1)}, bf16[1184,128]{1,0:T(8,128)(2,1)S(1)}, u32[]{:S(2)}, u32[]{:S(2)}) collective-permute-start(bf16[1184,128]{1,0:T(8,128)(2,1)S(1)} %get-tuple-element.36), channel_id=1, source_target_pairs={{0,1},{1,0},{2,3},{3,2},{4,5},{5,4},{6,7},{7,6},{8,9},{9,8},{10,11... | collective-permute-start | bytes 909320 | tf_op jit(solution)/shard_map/ppermute | solution.py:638
  109.5 4.6 %collective-permute-start.5 = (bf16[1536,128]{1,0:T(8,128)(2,1)S(1)}, bf16[1536,128]{1,0:T(8,128)(2,1)S(1)}, u32[]{:S(2)}, u32[]{:S(2)}) collective-permute-start(bf16[1536,128]{1,0:T(8,128)(2,1)S(1)} %bitcast.8), channel_id=1, source_target_pairs={{0,1},{1,0},{2,3},{3,2},{4,5},{5,4},{6,7},{7,6},{8,9},{9,8},{10,11... | collective-permute-start | bytes 1179656 | tf_op jit(solution)/shard_map/ppermute | solution.py:638

commit v7 on v6

--- a/solution.py
+++ b/solution.py
@@ -191,7 +191,7 @@
 
 
 def setconv(where, got, cot):
-    steps = 2
+    steps = 1
     fixed = lambda *shape: pl.BlockSpec(shape, lambda i: (0,) * len(shape))
     lanes = TR * FEAT
     shapes = [(TC, lanes), (SG + TR, 16, C), (SG + TR, 16, C)]

time: 116 us -> 116 us (level)
  no operation moved by 1% of the time
where the time goes in v7:
time: 116 us
  Pallas kernels  37.6 us (32%)
  blocking collectives  32.5 us (28%)
  waiting for transfers between devices  25 us (22%)
  starting transfers between devices  19.4 us (17%)
    all_to_all x1, waiting for transfers between devices, per_device(): got = lax.all_to_all(packed, ALL, 0, 0, tiled=True)  19.2 us
    all_to_all x1, blocking collectives, per_device(): lax.all_to_all(half, ALL, 0, 0, axis_index_groups=groups, tiled=True)  18.2 us
    all_to_all x1, blocking collectives, per_device(): lax.all_to_all(spread, ALL, 0, 0, axis_index_groups=groups, tiled=True)  14.4 us
    pallas_call x1, Pallas kernels, pack(): pl.pallas_call(pack_kernel, grid=(steps,), in_specs=[pl.BlockSpec(memory_...  13.3 us
    all_to_all x1, starting transfers between devices, per_device(): got = lax.all_to_all(packed, ALL, 0, 0, tiled=True)  11.5 us
    pallas_call x1, Pallas kernels, main(): pl.pallas_call(main_kernel, in_specs=[pl.BlockSpec(memory_space=pltpu.SME...  11 us
    ppermute x6, starting transfers between devices, swap(): return lambda x: lax.ppermute(x, ALL, pairs)  7.9 us
    pallas_call x1, Pallas kernels, mid(): pl.pallas_call(mid_kernel, in_specs=[pl.BlockSpec(memory_space=pltpu.SMEM...  6.41 us
  transfers between devices with their start and end apart: 7, of which 5 were waited for; matrix products, arithmetic and copies ran while one was open for 0% of the time, Pallas kernels for 6%

profile of v7, /device:TPU:1, one launch (start us, length us, event | category | flops | bytes accessed | tf_op | source)
XLA Modules:
  0.0 115.6 jit_solution(10725365943110069477)
XLA Ops:
  0.6 13.3 %pack.1 = bf16[128,32,128]{2,1,0:T(8,128)(2,1)} custom-call(s32[1,8192]{1,0:T(1,128)} %bitcast.13, f32[1,8192]{1,0:T(1,128)} %bitcast.14, f32[1,8192]{1,0:T(1,128)} %bitcast.15, bf16[24,8192]{1,0:T(8,128)(2,1)} %bitcast.12), custom_call_target="tpu_custom_call" | custom-call | flops 8589934592 | bytes 3145728 | tf_op jit(solution)/shard_map/pack/pallas_call | solution.py:128
  14.0 0.0 copy-start
  14.0 11.5 %all-to-all-start = ((bf16[128,32,128]{2,1,0:T(8,128)(2,1)}), bf16[128,32,128]{2,1,0:T(8,128)(2,1)S(1)}, u32[]{:S(2)}, u32[]{:S(2)}) async-start(bf16[128,32,128]{2,1,0:T(8,128)(2,1)} %pack.1), calls=%async_computation | async-start | bytes 2097152 | tf_op jit(solution)/shard_map/all_to_all | solution.py:657
  25.5 0.1 pad_add_fusion.where_ref
  25.6 0.0 copy-start.1
  25.6 0.0 copy-start.2
  25.6 0.0 copy-start.3
  25.6 19.2 %all-to-all-done.got_ref = bf16[128,32,128]{2,1,0:T(8,128)(2,1)S(1)} async-done(((bf16[128,32,128]{2,1,0:T(8,128)(2,1)}), bf16[128,32,128]{2,1,0:T(8,128)(2,1)S(1)}, u32[]{:S(2)}, u32[]{:S(2)}) %all-to-all-start) | async-done | bytes 1048608 | tf_op jit(solution)/shard_map/all_to_all | solution.py:657
  44.8 0.0 copy-done
  44.8 4.1 %setconv.1 = (bf16[128,512]{1,0:T(8,128)(2,1)S(1)}, bf16[20,16,128]{2,1,0:T(8,128)(2,1)S(1)}, bf16[20,16,128]{2,1,0:T(8,128)(2,1)S(1)}) custom-call(s32[4]{0:T(128)S(1)} %pad_add_fusion.where_ref, bf16[128,32,128]{2,1,0:T(8,128)(2,1)S(1)} %all-to-all-done.got_ref, bf16[16,128,128]{2,1,0:T(8,128)(2,1)S(1)} %copy-done), custom_call_target="tpu_custom_call" | custom-call | flops 3221225472 | bytes 2097152 | tf_op jit(solution)/shard_map/setconv/pallas_call | solution.py:198
  49.0 0.7 collective-permute-start
  49.7 0.3 collective-permute-start.1
  50.0 0.0 copy-done.1
  50.0 0.0 copy-done.2
  50.0 0.0 copy-done.3
  50.0 0.2 prep.1
  50.2 0.4 collective-permute-done.a_ref
  50.6 2.9 %collective-permute-done.1.b_ref = bf16[20,16,128]{2,1,0:T(8,128)(2,1)S(1)} collective-permute-done((bf16[20,16,128]{2,1,0:T(8,128)(2,1)S(1)}, bf16[20,16,128]{2,1,0:T(8,128)(2,1)S(1)}, u32[]{:S(2)}, u32[]{:S(2)}) %collective-permute-start.1) | collective-permute-done | bytes 81952 | tf_op jit(solution)/shard_map/ppermute | solution.py:638
  53.5 0.6 join.1
  54.1 1.2 %collective-permute-start.2 = (bf16[3,160,128]{2,1,0:T(8,128)(2,1)S(1)}, bf16[3,160,128]{2,1,0:T(8,128)(2,1)S(1)}, u32[]{:S(2)}, u32[]{:S(2)}) collective-permute-start(bf16[3,160,128]{2,1,0:T(8,128)(2,1)S(1)} %get-tuple-element.25), channel_id=1, source_target_pairs={{0,16},{1,17},{2,18},{3,19},{4,20},{5,21},{6,22},{7,23},{8,24},{9,... | collective-permute-start | bytes 368648 | tf_op jit(solution)/shard_map/ppermute | solution.py:638
  55.3 1.5 %collective-permute-start.3 = (bf16[3,160,128]{2,1,0:T(8,128)(2,1)S(1)}, bf16[3,160,128]{2,1,0:T(8,128)(2,1)S(1)}, u32[]{:S(2)}, u32[]{:S(2)}) collective-permute-start(bf16[3,160,128]{2,1,0:T(8,128)(2,1)S(1)} %get-tuple-element.26), channel_id=1, source_target_pairs={{0,8},{1,9},{2,10},{3,11},{4,12},{5,13},{6,14},{7,15},{8,0},{9,1},... | collective-permute-start | bytes 368648 | tf_op jit(solution)/shard_map/ppermute | solution.py:638
  56.8 6.4 %mid.1 = (f32[3040,128]{1,0:T(8,128)S(1)}, bf16[3040,384]{1,0:T(8,128)(2,1)S(1)}, f32[3040,128]{1,0:T(8,128)S(1)}) custom-call(s32[4]{0:T(128)S(1)} %pad_add_fusion.where_ref, bf16[16,128,128]{2,1,0:T(8,128)(2,1)S(1)} %copy-done, bf16[128,512]{1,0:T(8,128)(2,1)S(1)} %get-tuple-element.22.s_ref, bf16[20,16,128]{2,1,0:T(8,128)(2,1)S(1)} %collective-permute-done.a_ref, ...), custom_call_target="tpu_custom_call" | custom-call | flops 1613758464 | bytes 4194304 | tf_op jit(solution)/shard_map/mid/pallas_call | solution.py:373
  63.2 0.0 collective-permute-done.2.c_ref
  63.2 0.0 collective-permute-done.3.d_ref
  63.2 11.0 %main.1 = (bf16[16,128,128]{2,1,0:T(8,128)(2,1)}, bf16[1184,128]{1,0:T(8,128)(2,1)S(1)}, bf16[1184,128]{1,0:T(8,128)(2,1)S(1)}, f32[3040,128]{1,0:T(8,128)S(1)},...) custom-call(s32[4]{0:T(128)S(1)} %pad_add_fusion.where_ref, ...), custom_call_target="tpu_custom_call", output_to_operand_aliasing={{3}: (13, {}), {4}: (14, {}), {5}: (15, {})} | custom-call | flops 8589934592 | bytes 6291456 | tf_op jit(solution)/shard_map/main/pallas_call | solution.py:555
  74.3 1.0 collective-permute-start.4
  75.3 1.2 %collective-permute-done.4 = bf16[1184,128]{1,0:T(8,128)(2,1)S(1)} collective-permute-done((bf16[1184,128]{1,0:T(8,128)(2,1)S(1)}, bf16[1184,128]{1,0:T(8,128)(2,1)S(1)}, u32[]{:S(2)}, u32[]{:S(2)}) %collective-permute-start.4) | collective-permute-done | bytes 303136 | tf_op jit(solution)/shard_map/ppermute | solution.py:638
  76.5 0.1 add_convert_fusion
  76.6 18.2 %all_to_all.15 = bf16[64,24,128]{2,1,0:T(8,128)(2,1)S(1)} all-to-all(bf16[64,24,128]{2,1,0:T(8,128)(2,1)S(1)} %bitcast.11), channel_id=1, replica_groups={{0,2,4,6,8,10,12,14,16,18,20,22,24,26,28,30,32,34,36,38,40,42,44,46,48,..., dimensions={0} | all-to-all | bytes 786432 | tf_op jit(solution)/shard_map/all_to_all | solution.py:670
  94.8 0.1 reduce_sum.12
  94.9 0.1 broadcast_in_dim.2
  94.9 14.4 %all_to_all.16 = bf16[64,24,128]{2,1,0:T(8,128)(2,1)S(1)} all-to-all(bf16[64,24,128]{2,1,0:T(8,128)(2,1)S(1)} %broadcast_in_dim.2), channel_id=1, replica_groups={{0,2,4,6,8,10,12,14,16,18,20,22,24,26,28,30,32,34,36,38,40,42,44,46,48,..., dimensions={0} | all-to-all | bytes 786432 | tf_op jit(solution)/shard_map/all_to_all | solution.py:673
  109.3 3.2 %collective-permute-start.5 = (bf16[1536,128]{1,0:T(8,128)(2,1)S(1)}, bf16[1536,128]{1,0:T(8,128)(2,1)S(1)}, u32[]{:S(2)}, u32[]{:S(2)}) collective-permute-start(bf16[1536,128]{1,0:T(8,128)(2,1)S(1)} %bitcast.8), channel_id=1, source_target_pairs={{0,1},{1,0},{2,3},{3,2},{4,5},{5,4},{6,7},{7,6},{8,9},{9,8},{10,11... | collective-permute-start | bytes 1179656 | tf_op jit(solution)/shard_map/ppermute | solution.py:638
  112.5 0.1 turn.1.turned_ref
  112.6 1.2 %collective-permute-done.5.other_ref = bf16[1536,128]{1,0:T(8,128)(2,1)S(1)} collective-permute-done((bf16[1536,128]{1,0:T(8,128)(2,1)S(1)}, bf16[1536,128]{1,0:T(8,128)(2,1)S(1)}, u32[]{:S(2)}, u32[]{:S(2)}) %collective-permute-start.5) | collective-permute-done | bytes 393248 | tf_op jit(solution)/shard_map/ppermute | solution.py:638
  113.9 1.7 %unpack.1 = (f32[24,128]{1,0:T(8,128)}, f32[3,3,128,128]{3,2,1,0:T(8,128)}, f32[3,3,128,128]{3,2,1,0:T(8,128)}) custom-call(s32[4]{0:T(128)S(1)} %pad_add_fusion.where_ref, bf16[1536,128]{1,0:T(8,128)(2,1)S(1)} %bitcast.10, bf16[9,128,128]{2,1,0:T(8,128)(2,1)S(1)} %turn.1.turned_ref, bf16[1536,128]{1,0:T(8,128)(2,1)S(1)} %collective-permute-done.5.other_ref), custom_call_target="tpu_custom_call" | custom-call | tf_op jit(solution)/shard_map/unpack/pallas_call | solution.py:614
  (1 shorter events, 0.0 us)
Async XLA Ops:
  14.0 30.9 %copy-start = (bf16[16,128,128]{2,1,0:T(8,128)(2,1)S(1)}, bf16[16,128,128]{2,1,0:T(8,128)(2,1)}, u32[]{:S(2)}) copy-start(bf16[16,128,128]{2,1,0:T(8,128)(2,1)} %cot_ref.9) | copy-start | bytes 1572868
  14.0 30.8 %all-to-all-start = ((bf16[128,32,128]{2,1,0:T(8,128)(2,1)}), bf16[128,32,128]{2,1,0:T(8,128)(2,1)S(1)}, u32[]{:S(2)}, u32[]{:S(2)}) async-start(bf16[128,32,128]{2,1,0:T(8,128)(2,1)} %pack.1), calls=%async_computation | async-start | bytes 2097152 | tf_op jit(solution)/shard_map/all_to_all | solution.py:657
  25.6 24.4 %copy-start.1 = (bf16[3,3,128,128]{3,2,1,0:T(8,128)(2,1)S(1)}, bf16[3,3,128,128]{3,2,1,0:T(8,128)(2,1)}, u32[]{:S(2)}) copy-start(bf16[3,3,128,128]{3,2,1,0:T(8,128)(2,1)} %w1_ref.5) | copy-start | bytes 884740
  25.6 24.4 %copy-start.2 = (bf16[3,3,128,128]{3,2,1,0:T(8,128)(2,1)S(1)}, bf16[3,3,128,128]{3,2,1,0:T(8,128)(2,1)}, u32[]{:S(2)}) copy-start(bf16[3,3,128,128]{3,2,1,0:T(8,128)(2,1)} %w2_ref.3) | copy-start | bytes 884740
  25.6 24.4 %copy-start.3 = (bf16[24,128]{1,0:T(8,128)(2,1)S(1)}, bf16[24,128]{1,0:T(8,128)(2,1)}, u32[]{:S(2)}) copy-start(bf16[24,128]{1,0:T(8,128)(2,1)} %embed_ref.1) | copy-start | bytes 18436
  49.0 1.6 %collective-permute-start = (bf16[20,16,128]{2,1,0:T(8,128)(2,1)S(1)}, bf16[20,16,128]{2,1,0:T(8,128)(2,1)S(1)}, u32[]{:S(2)}, u32[]{:S(2)}) collective-permute-start(bf16[20,16,128]{2,1,0:T(8,128)(2,1)S(1)} %get-tuple-element.23), channel_id=1, source_target_pairs={{0,1},{1,0},{2,3},{3,2},{4,5},{5,4},{6,7},{7,6},{8,9},{9,8},{10,11... | collective-permute-start | bytes 245768 | tf_op jit(solution)/shard_map/ppermute | solution.py:638
  49.7 3.9 %collective-permute-start.1 = (bf16[20,16,128]{2,1,0:T(8,128)(2,1)S(1)}, bf16[20,16,128]{2,1,0:T(8,128)(2,1)S(1)}, u32[]{:S(2)}, u32[]{:S(2)}) collective-permute-start(bf16[20,16,128]{2,1,0:T(8,128)(2,1)S(1)} %get-tuple-element.24), channel_id=1, source_target_pairs={{0,15},{1,2},{2,1},{3,4},{4,3},{5,6},{6,5},{7,8},{8,7},{9,10},{10,... | collective-permute-start | bytes 245768 | tf_op jit(solution)/shard_map/ppermute | solution.py:638
  54.1 9.1 %collective-permute-start.2 = (bf16[3,160,128]{2,1,0:T(8,128)(2,1)S(1)}, bf16[3,160,128]{2,1,0:T(8,128)(2,1)S(1)}, u32[]{:S(2)}, u32[]{:S(2)}) collective-permute-start(bf16[3,160,128]{2,1,0:T(8,128)(2,1)S(1)} %get-tuple-element.25), channel_id=1, source_target_pairs={{0,16},{1,17},{2,18},{3,19},{4,20},{5,21},{6,22},{7,23},{8,24},{9,... | collective-permute-start | bytes 368648 | tf_op jit(solution)/shard_map/ppermute | solution.py:638
  55.3 7.9 %collective-permute-start.3 = (bf16[3,160,128]{2,1,0:T(8,128)(2,1)S(1)}, bf16[3,160,128]{2,1,0:T(8,128)(2,1)S(1)}, u32[]{:S(2)}, u32[]{:S(2)}) collective-permute-start(bf16[3,160,128]{2,1,0:T(8,128)(2,1)S(1)} %get-tuple-element.26), channel_id=1, source_target_pairs={{0,8},{1,9},{2,10},{3,11},{4,12},{5,13},{6,14},{7,15},{8,0},{9,1},... | collective-permute-start | bytes 368648 | tf_op jit(solution)/shard_map/ppermute | solution.py:638
  74.3 2.2 %collective-permute-start.4 = (bf16[1184,128]{1,0:T(8,128)(2,1)S(1)}, bf16[1184,128]{1,0:T(8,128)(2,1)S(1)}, u32[]{:S(2)}, u32[]{:S(2)}) collective-permute-start(bf16[1184,128]{1,0:T(8,128)(2,1)S(1)} %get-tuple-element.36), channel_id=1, source_target_pairs={{0,1},{1,0},{2,3},{3,2},{4,5},{5,4},{6,7},{7,6},{8,9},{9,8},{10,11... | collective-permute-start | bytes 909320 | tf_op jit(solution)/shard_map/ppermute | solution.py:638
  109.3 4.6 %collective-permute-start.5 = (bf16[1536,128]{1,0:T(8,128)(2,1)S(1)}, bf16[1536,128]{1,0:T(8,128)(2,1)S(1)}, u32[]{:S(2)}, u32[]{:S(2)}) collective-permute-start(bf16[1536,128]{1,0:T(8,128)(2,1)S(1)} %bitcast.8), channel_id=1, source_target_pairs={{0,1},{1,0},{2,3},{3,2},{4,5},{5,4},{6,7},{7,6},{8,9},{9,8},{10,11... | collective-permute-start | bytes 1179656 | tf_op jit(solution)/shard_map/ppermute | solution.py:638
